TPU v7x, 32 devices: a whole 2x2x4 slice. The times are simulated.
32 devices in a mesh: groups: 2 (over x), blk: 16 (over z, y, core).
Axes of the slice: x: 2, y: 2, z: 4, core: 2. Of those that a mesh axis runs over, the one named last changes fastest.
Arguments:
- attn: bfloat16 [8192, 3072], P(('groups', 'blk')), parts along dimension 0, may hold values from -6 to 6
- resid: bfloat16 [8192, 3072], P(('groups', 'blk')), parts along dimension 0, may hold values from -6 to 6
- frozen: bfloat16 [3072, 3072], P('blk'), may hold values from -0.109375 to 0.109375
- adapter_down_weight: float32 [3072, 64], replicated, may hold values from -0.109375 to 0.109375
- adapter_up_weight: float32 [64, 3072], replicated, may hold values from -0.109375 to 0.109375
- timestep_gate: float32 [50, 3072], replicated, may hold values from 0.25 to 1.5
- guidance_gate: float32 [16, 3072], replicated, may hold values from -0.5 to 0.5
- timestep_index: int32 [2], P('groups'), parts along dimension 0, may hold values from 0 to 49
- guidance_index: int32 [2], P('groups'), parts along dimension 0, may hold values from 0 to 15
- cotangent: bfloat16 [8192, 3072], P(('groups', 'blk')), parts along dimension 0, may hold values from -6 to 6
Outputs:
- updated: bfloat16 [8192, 3072], P(('groups', 'blk')), parts along dimension 0
- grad_attn: bfloat16 [8192, 3072], P(('groups', 'blk')), parts along dimension 0
- grad_down: float32 [6144, 64], P(('groups', 'blk')), parts along dimension 0
- grad_up_t: float32 [6144, 64], P(('groups', 'blk')), parts along dimension 0
There are 2 independent parts, one for each index of `groups`. A program takes and returns all parts, laid end to end along the dimension named above; an argument that names none is the same for every part. Nothing has to cross between parts.
All inputs are finite; a program needn't handle non-finite values.
Results may differ from a plain program's by a relative error of at most 0.0059.
Values may be sent and summed in bfloat16 or wider, within the bound.
No kernel may reach another device: no remote copies, remote signals or barrier semaphores. Data moves between devices by JAX's collectives and lax.ppermute only.
A program may use at most 128 MiB of HBM per device.

v0:
```python
import jax
import jax.numpy as jnp
from jax import lax
from jax.sharding import PartitionSpec as P

IMAGE_TOKENS = 4096


def contract_rows(left, right):
    return lax.dot_general(
        left, right, (((0,), (0,)), ((), ())), preferred_element_type=jnp.float32
    )


def contract_cols(left, right):
    return lax.dot_general(
        left, right, (((1,), (1,)), ((), ())), preferred_element_type=jnp.float32
    )


def body(
    attn,
    resid,
    frozen,
    adapter_down_weight,
    adapter_up_weight,
    timestep_gate,
    guidance_gate,
    timestep_index,
    guidance_index,
    cotangent,
):
    row_count = attn.shape[0]
    features = attn.shape[1]
    axis_size = lax.axis_size("blk")
    highest = lax.Precision.HIGHEST
    row_ids = lax.axis_index("blk") * row_count + jnp.arange(row_count, dtype=jnp.int32)
    owner_sample = row_ids // IMAGE_TOKENS
    sample_pick = (
        owner_sample[:, None] == jnp.arange(timestep_index.shape[0], dtype=jnp.int32)[None, :]
    ).astype(jnp.float32)
    time_pick = (
        timestep_index[:, None] == jnp.arange(timestep_gate.shape[0], dtype=jnp.int32)[None, :]
    ).astype(jnp.float32)
    guide_pick = (
        guidance_index[:, None] == jnp.arange(guidance_gate.shape[0], dtype=jnp.int32)[None, :]
    ).astype(jnp.float32)
    gate_sample = jnp.dot(time_pick, timestep_gate, precision=highest) + jnp.dot(
        guide_pick, guidance_gate, precision=highest
    )
    gate_per_row = jnp.dot(sample_pick, gate_sample, precision=highest)
    down_portion = adapter_down_weight.astype(jnp.bfloat16)
    up_portion = adapter_up_weight.astype(jnp.bfloat16)
    reduced_rank_rows = jnp.dot(attn, down_portion, preferred_element_type=jnp.float32).astype(
        jnp.bfloat16
    )
    adapter_lifted = jnp.dot(reduced_rank_rows, up_portion, preferred_element_type=jnp.float32)
    grad_out = (gate_per_row * cotangent.astype(jnp.float32)).astype(jnp.bfloat16)
    grad_low = contract_cols(grad_out, up_portion).astype(jnp.bfloat16)
    slab_rows = lax.all_gather(frozen, "blk", axis=0, tiled=True)
    forward = jnp.dot(attn, slab_rows, preferred_element_type=jnp.float32)
    back_part = contract_cols(grad_out, slab_rows)
    updated = (resid.astype(jnp.float32) + gate_per_row * (forward + adapter_lifted)).astype(
        jnp.bfloat16
    )
    grad_attn = (back_part + contract_cols(grad_low, down_portion)).astype(jnp.bfloat16)
    term_down = contract_rows(attn, grad_low)
    term_up = contract_rows(grad_out, reduced_rank_rows)
    grad_scale = float(row_count * axis_size) ** (-0.5)
    total_down, total_up = lax.psum((term_down, term_up), "blk")
    share_rows = features // axis_size
    first_row = lax.axis_index("blk") * share_rows
    own_down = lax.dynamic_slice_in_dim(total_down, first_row, share_rows, 0)
    own_up = lax.dynamic_slice_in_dim(total_up, first_row, share_rows, 0)
    return (updated, grad_attn, grad_scale * own_down, grad_scale * own_up)


def solution(mesh):
    return jax.shard_map(
        body,
        mesh=mesh,
        in_specs=(
            P(("groups", "blk"), None),
            P(("groups", "blk"), None),
            P("blk", None),
            P(),
            P(),
            P(),
            P(),
            P("groups"),
            P("groups"),
            P(("groups", "blk"), None),
        ),
        out_specs=(
            P(("groups", "blk"), None),
            P(("groups", "blk"), None),
            P(("groups", "blk"), None),
            P(("groups", "blk"), None),
        ),
        check_vma=False,
    )
```

profile of v0, /device:TPU:0, one launch (start us, length us, event | category | flops | bytes accessed | tf_op | source)
XLA Modules:
  0.0 243.0 jit_solution(14946744857238231432)
XLA Ops:
  7.2 0.0 copy-start
  7.2 0.0 copy-start.4
  7.2 0.0 copy-start.3
  7.2 0.0 all-reduce.3.cloned.1.call-start
  8.7 0.0 copy-start.5
  8.7 0.0 copy-done
  8.7 1.8 convolution_convert_fusion.1
  10.6 1.4 fusion.10
  12.0 0.0 copy-done.4
  12.0 0.2 fusion.8
  12.2 0.0 copy-done.3
  12.2 0.0 copy-done.5
  12.3 0.7 convolution_convert_fusion
  12.9 1.3 convolution_bitcast_fusion
  14.2 1.5 fusion.18
  15.7 0.0 all-reduce.3.cloned.1.call-update
  15.7 0.0 all-gather.2.cloned.1.call-start
  15.8 0.7 all-gather.2.cloned.1.call-update
  16.5 97.8 %all-reduce.3.cloned.1.call-done = (f32[3072,64]{0,1:T(8,128)}, f32[3072,64]{0,1:T(8,128)}) async-done(((f32[3072,64]{0,1:T(8,128)}, f32[3072,64]{0,1:T(8,128)}), (f32[3072,64]{0,1:T(8,128)}, f32[3072,64]{0,1:T(8,128)})) %all-reduce.3.cloned.1.call-update) | async-done | bytes 1572880 | tf_op jit(solution)/shard_map/psum | solution.py:70
  114.3 1.7 dynamic-slice_multiply_fusion
  115.9 0.0 copy-start.1
  116.0 97.8 %all-gather.2.cloned.1.call-done = bf16[3072,3072]{1,0:T(8,128)(2,1)} async-done(((bf16[192,3072]{1,0:T(8,128)(2,1)}), bf16[3072,3072]{1,0:T(8,128)(2,1)}) %all-gather.2.cloned.1.call-update) | async-done | bytes 18874384 | tf_op jit(solution)/shard_map/all_gather | solution.py:60
  213.7 9.5 %fusion.21 = f32[256,3072]{1,0:T(8,128)S(1)} fusion(bf16[3072,3072]{1,0:T(8,128)(2,1)} %all-gather.2.cloned.1.call-done, bf16[256,3072]{1,0:T(8,128)(2,1)} %param.19, f32[3072]{0:T(1024)S(1)} %add.34, f32[256]{0:T(256)S(1)} %compare_convert_fusion), kind=kOutput, calls=%fused_computation.33 | convolution fusion | flops 4834983936 | bytes 23606272 | tf_op jit(solution)/shard_map/dot_general | solution.py:16
  223.2 0.0 copy-done.1
  223.2 1.7 fusion.2
  225.0 0.0 copy-start.2
  225.0 9.1 %fusion.23 = f32[256,3072]{1,0:T(8,128)S(1)} fusion(bf16[256,3072]{1,0:T(8,128)(2,1)S(1)} %copy-done, bf16[3072,3072]{1,0:T(8,128)(2,1)} %all-gather.2.cloned.1.call-done), kind=kOutput, calls=%fused_computation.34 | convolution fusion | flops 4831838208 | bytes 23592960 | tf_op jit(solution)/shard_map/dot_general | solution.py:61
  234.1 0.0 copy-done.2
  234.1 2.0 fusion.1
  (2 shorter events, 0.0 us)
Async XLA Ops:
  7.2 1.6 copy-start
  7.2 4.8 %copy-start.4 = (f32[16,3072]{1,0:T(8,128)S(1)}, f32[16,3072]{1,0:T(8,128)}, u32[]{:S(2)}) copy-start(f32[16,3072]{1,0:T(8,128)} %param.16) | copy-start | bytes 589828
  7.2 5.0 %copy-start.3 = (f32[64,3072]{1,0:T(8,128)S(1)}, f32[64,3072]{1,0:T(8,128)}, u32[]{:S(2)}) copy-start(f32[64,3072]{1,0:T(8,128)} %param.14) | copy-start | bytes 2359300
  7.2 107.0 %all-reduce.3.cloned.1.call-start = ((), (), s32[]{:S(2)}) async-start(), calls=%async_computation.1 | async-start | bytes 3145728 | tf_op jit(solution)/shard_map/psum | solution.py:70
  8.7 3.6 %copy-start.5 = (bf16[256,3072]{1,0:T(8,128)(2,1)S(1)}, bf16[256,3072]{1,0:T(8,128)(2,1)}, u32[]{:S(2)}) copy-start(bf16[256,3072]{1,0:T(8,128)(2,1)} %param.19) | copy-start | bytes 4718596
  15.7 198.0 %all-gather.2.cloned.1.call-start = ((), (), s32[]{:S(2)}) async-start(), calls=%async_computation | async-start | bytes 20054016 | tf_op jit(solution)/shard_map/all_gather | solution.py:60
  115.9 107.3 %copy-start.1 = (f32[3072,64]{0,1:T(8,128)S(1)}, f32[3072,64]{0,1:T(8,128)}, u32[]{:S(2)}) copy-start(f32[3072,64]{0,1:T(8,128)} %param.13) | copy-start | bytes 2359300
  225.0 9.1 %copy-start.2 = (bf16[256,3072]{1,0:T(8,128)(2,1)S(1)}, bf16[256,3072]{1,0:T(8,128)(2,1)}, u32[]{:S(2)}) copy-start(bf16[256,3072]{1,0:T(8,128)(2,1)} %param.11) | copy-start | bytes 4718596
Sparse Core Ops, SparseCore 0:
  15.9 98.3 all-reduce.2
  115.8 97.8 all-gather.1
where the time goes:
time: 243 us
  waiting for transfers between devices  196 us (81%)
  matrix products  29.3 us (12%)
  between operations  15.6 us (6%)
    all_gather x1, waiting for transfers between devices, body(): slab_rows = lax.all_gather(frozen, 'blk', axis=0, tiled=True)  97.8 us
    psum x1, waiting for transfers between devices, body(): total_down, total_up = lax.psum((term_down, term_up), 'blk')  97.8 us
    dot_general x3, matrix products, contract_cols(): lax.dot_general(left, right, (((1,), (1,)), ((), ())), preferred_element_...  11.9 us
    dot_general x1, matrix products, body(): forward = jnp.dot(attn, slab_rows, preferred_element_type=jnp.float32)  9.09 us
  transfers between devices with their start and end apart: 2, of which 2 were waited for; matrix products, arithmetic and copies ran while one was open for 1% of the time, Pallas kernels for 0%

commit v1 on v0

v1 whole, which is shorter than its diff:
```python
import functools

import jax
import jax.numpy as jnp
from jax import lax
from jax.experimental import pallas as pl
from jax.experimental.pallas import tpu as pltpu
from jax.sharding import PartitionSpec as P

IMAGE_TOKENS = 4096
F32 = jnp.float32
BF16 = jnp.bfloat16


def contract_rows(left, right):
    return lax.dot_general(left, right, (((0,), (0,)), ((), ())), preferred_element_type=F32)


def contract_cols(left, right):
    return lax.dot_general(left, right, (((1,), (1,)), ((), ())), preferred_element_type=F32)


def matmul(left, right):
    return jnp.dot(left, right, preferred_element_type=F32)


def ring_order(chips):
    return [0] + list(range(1, chips, 2)) + list(range(chips - 2, 0, -2))


def ring_pairs(chips):
    order = ring_order(chips)
    pairs = []
    for place, chip in enumerate(order):
        after, before = order[(place + 1) % chips], order[(place - 1) % chips]
        pairs += [(2 * chip, 2 * after), (2 * chip + 1, 2 * before + 1)]
    return pairs


def step_kernel(spec, *refs):
    refs = list(refs)
    place = refs.pop(0)
    attn, gout, low, up, glow, down = refs[:6]
    refs = refs[6:]
    piece_refs = [refs.pop(0) for _ in spec["pieces"]]
    total_in = refs.pop(0) if spec["total_in"] else None
    part_in = refs.pop(0) if spec["part_in"] else None
    resid, gate = (refs.pop(0), refs.pop(0)) if spec["final"] else (None, None)
    for _ in range(spec["aliased"]):
        refs.pop(0)
    main_out = refs.pop(0)
    back_out = refs.pop(0)
    attn_v, gout_v, pieces_v, total_v, resid_v, result_v, back_v, load, store = refs
    rows = gout_v.shape[0]
    chips, span = spec["chips"], spec["span"]

    def cols(start, width):
        return pl.ds(pl.multiple_of(start, 128), width)

    def chip_cols(c):
        return cols(place[c], span)

    def block_cols(b):
        return cols(place[chips + b], spec["blocks"][b])

    loads = []

    def fetch(src, dst):
        copy = pltpu.make_async_copy(src, dst, load.at[len(loads)])
        copy.start()
        loads.append(copy)
        return copy

    get_attn = [fetch(attn.at[:, chip_cols(c)], attn_v.at[c]) for c in range(chips)]
    get_piece, get_total, get_gout, get_resid = [], [], [], []
    by_block = {}
    for i, (c, b) in enumerate(spec["pieces"]):
        by_block.setdefault(b, []).append((i, c))
    offset = []
    at = 0
    for b, width in enumerate(spec["blocks"]):
        offset.append(at)
        at += width
    get_piece = {}
    for b in by_block:
        width = spec["blocks"][b]
        for i, c in by_block[b]:
            get_piece[i] = fetch(piece_refs[i], pieces_v.at[i, :, pl.ds(0, width)])
        here = pl.ds(offset[b], width)
        get_gout.append(fetch(gout.at[:, block_cols(b)], gout_v.at[:, here]))
        if spec["total_in"]:
            get_total.append(fetch(total_in.at[:, block_cols(b)], total_v.at[:, here]))
        if spec["final"]:
            get_resid.append(fetch(resid.at[:, block_cols(b)], resid_v.at[:, here]))
    for copy in get_attn:
        copy.wait()
    stores = []
    back = [None] * chips
    for n, b in enumerate(by_block):
        width = spec["blocks"][b]
        here = pl.ds(offset[b], width)
        value = None
        for i, c in by_block[b]:
            get_piece[i].wait()
            term = matmul(attn_v[c], pieces_v[i, :, pl.ds(0, width)])
            value = term if value is None else value + term
        if spec["total_in"]:
            get_total[n].wait()
            value = value + total_v[:, here]
        else:
            value = value + matmul(low[...], up[:, block_cols(b)])
        if spec["final"]:
            get_resid[n].wait()
            value = resid_v[:, here].astype(F32) + gate[:, block_cols(b)] * value
        result_v[:, here] = value.astype(result_v.dtype)
        copy = pltpu.make_async_copy(result_v.at[:, here], main_out.at[:, block_cols(b)], store.at[len(stores)])
        copy.start()
        stores.append(copy)
        get_gout[n].wait()
        for i, c in by_block[b]:
            term = contract_cols(gout_v[:, here], pieces_v[i, :, pl.ds(0, width)])
            back[c] = term if back[c] is None else back[c] + term
    for c in range(chips):
        if spec["part_in"]:
            value = back[c] + part_in[...]
        else:
            value = back[c] + matmul(glow[...], down[:, chip_cols(c)])
        if spec["part_out"]:
            back_out[...] = value
        else:
            back_v[c] = value.astype(BF16)
            copy = pltpu.make_async_copy(back_v.at[c], back_out.at[:, chip_cols(c)], store.at[len(stores)])
            copy.start()
            stores.append(copy)
    for copy in stores:
        copy.wait()


def step(place, common, pieces, blocks, chips, span, total=None, part=None, part_out=False, final=None, main=None, back=None):
    rows, features = common[0].shape
    spec = dict(
        pieces=[(c, b) for _, c, b in pieces],
        blocks=blocks,
        chips=chips,
        span=span,
        total_in=total is not None,
        part_in=part is not None,
        part_out=part_out,
        final=final is not None,
    )
    vmem = pl.BlockSpec(memory_space=pltpu.VMEM)
    anywhere = pl.BlockSpec(memory_space=pl.ANY)
    args = [place, *common, *[p for p, _, _ in pieces]]
    specs = [pl.BlockSpec(memory_space=pltpu.SMEM), anywhere, anywhere, vmem, vmem, vmem, vmem]
    specs += [anywhere] * len(pieces)
    aliases = {}
    if total is not None:
        if final is None:
            aliases[len(args)] = 0
        args.append(total)
        specs.append(anywhere)
    if part is not None:
        args.append(part)
        specs.append(vmem)
    if final is not None:
        args += list(final)
        specs += [anywhere, vmem]
    aliased = 0
    if main is not None:
        aliases[len(args)] = 0
        args.append(main)
        specs.append(anywhere)
        aliased += 1
    if back is not None:
        aliases[len(args)] = 1
        args.append(back)
        specs.append(anywhere)
        aliased += 1
    spec["aliased"] = aliased
    main_type = BF16 if final is not None else F32
    width = sum(blocks)
    back_shape = jax.ShapeDtypeStruct((rows, span), F32) if part_out else jax.ShapeDtypeStruct((rows, features), BF16)
    n_load = chips + len(pieces) + 3 * len(blocks)
    n_store = len(blocks) + chips
    return pl.pallas_call(
        functools.partial(step_kernel, spec),
        out_shape=(jax.ShapeDtypeStruct((rows, features), main_type), back_shape),
        in_specs=specs,
        out_specs=(anywhere, vmem if part_out else anywhere),
        scratch_shapes=[
            pltpu.VMEM((chips, rows, span), BF16),
            pltpu.VMEM((rows, width), BF16),
            pltpu.VMEM((len(pieces), span, max(blocks)), BF16),
            pltpu.VMEM((rows, width) if total is not None else (8, 128), F32),
            pltpu.VMEM((rows, width) if final is not None else (16, 128), BF16),
            pltpu.VMEM((rows, width), main_type),
            pltpu.VMEM((chips, rows, span), BF16),
            pltpu.SemaphoreType.DMA((n_load,)),
            pltpu.SemaphoreType.DMA((n_store,)),
        ],
        input_output_aliases=aliases,
        compiler_params=pltpu.CompilerParams(vmem_limit_bytes=28 * 1024 * 1024),
        cost_estimate=pl.CostEstimate(
            flops=4 * rows * span * sum(blocks[b] for _, _, b in pieces),
            bytes_accessed=12 * 1024 * 1024,
            transcendentals=0,
        ),
    )(*args)


def scatter_sum(terms, axis_size):
    me = lax.axis_index("blk")
    bit = 1
    while bit < axis_size:
        pairs = [(i, i ^ bit) for i in range(axis_size)]
        mine = lax.rem(lax.div(me, bit), 2)
        slots = terms.reshape((terms.shape[0] // 2, 2) + terms.shape[1:])
        keep = jnp.where(mine == 0, slots[:, 0], slots[:, 1])
        give = jnp.where(mine == 0, slots[:, 1], slots[:, 0]).astype(BF16)
        terms = keep + lax.ppermute(give, "blk", pairs).astype(F32)
        bit *= 2
    return terms[0]


def ring_body(
    attn,
    resid,
    frozen,
    adapter_down_weight,
    adapter_up_weight,
    timestep_gate,
    guidance_gate,
    timestep_index,
    guidance_index,
    cotangent,
):
    rows, features = attn.shape
    axis_size = lax.axis_size("blk")
    chips = axis_size // 2
    shard = frozen.shape[0]
    span = 2 * shard
    third = features // 3
    half = third // 2
    me = lax.axis_index("blk")
    g = lax.axis_index("groups")
    chip, k = me // 2, me % 2
    core_pairs = [(i, i ^ 1) for i in range(axis_size)]
    ring = functools.partial(lax.ppermute, axis_name="blk", perm=ring_pairs(chips))
    swap = functools.partial(lax.ppermute, axis_name="blk", perm=core_pairs)
    cross = functools.partial(lax.ppermute, axis_name="groups", perm=[(0, 1), (1, 0)])
    order = jnp.asarray(ring_order(chips), jnp.int32)
    at = jnp.argmax(order == chip).astype(jnp.int32)

    def first_col(distance):
        return order[(at + distance + chips) % chips] * span

    own, common_third, others = g * 2 * third, third, (1 - g) * 2 * third

    def both_cores(start):
        mine = lax.dynamic_slice_in_dim(frozen, start, third, 1)
        other = swap(mine)
        low_rows, high_rows = jnp.where(k == 0, mine, other), jnp.where(k == 0, other, mine)
        return jnp.concatenate([low_rows, high_rows], 0)

    own_r, own_q = both_cores(own), both_cores(common_third)

    steps = chips // 2 - 1
    r, q = own_r, own_q
    r_all, q_all, x_all = [], [], []
    for _ in range(steps):
        r, q = ring(r), ring(q)
        x = cross(r)
        r_all.append(r)
        q_all.append(q)
        x_all.append(x)
    r_last = ring(lax.dynamic_slice_in_dim(r, k * half, half, 1))
    q_last = ring(lax.dynamic_slice_in_dim(q, k * half, half, 1))
    x_last = cross(r_last)

    own_x = both_cores(others)

    sample = me * rows // IMAGE_TOKENS
    t_row = lax.dynamic_index_in_dim(timestep_index, sample, 0, False)
    g_row = lax.dynamic_index_in_dim(guidance_index, sample, 0, False)
    gate = lax.dynamic_slice_in_dim(timestep_gate, t_row, 1, 0) + lax.dynamic_slice_in_dim(guidance_gate, g_row, 1, 0)
    down_half = adapter_down_weight.astype(BF16)
    up_half = adapter_up_weight.astype(BF16)
    low = matmul(attn, down_half).astype(BF16)
    gout = (gate * cotangent.astype(F32)).astype(BF16)
    glow = contract_cols(gout, up_half).astype(BF16)
    terms = jnp.concatenate([contract_rows(attn, glow), contract_rows(gout, low)], 1)
    summed = scatter_sum(terms.reshape(axis_size, shard, terms.shape[1]), axis_size)
    grad_scale = float(rows * axis_size) ** (-0.5)
    rank = glow.shape[1]
    grad_down, grad_up_t = grad_scale * summed[:, :rank], grad_scale * summed[:, rank:]

    common = (attn, gout, low, up_half, glow, down_half.T)
    blocks = [third] * 3

    def where(*values):
        return jnp.stack([jnp.asarray(v, jnp.int32) for v in values])

    total, grad_attn = step(
        where(first_col(0), own, common_third, others),
        common,
        [(own_r, 0, 0), (own_q, 0, 1), (own_x, 0, 2)],
        blocks, 1, span,
    )
    toward = 2 * k - 1
    for n in range(steps):
        pieces = [(r_all[n], 0, 0), (swap(r_all[n]), 1, 0)]
        pieces += [(q_all[n], 0, 1), (swap(q_all[n]), 1, 1)]
        pieces += [(x_all[n], 0, 2), (swap(x_all[n]), 1, 2)]
        total, grad_attn = step(
            where(first_col(toward * (n + 1)), first_col(-toward * (n + 1)), own, common_third, others),
            common, pieces, blocks, 2, span, total=total, back=grad_attn,
        )
    far = first_col(chips // 2)
    mine, theirs = k * half, (1 - k) * half
    updated, part = step(
        where(far, own + mine, own + theirs, common_third + mine, common_third + theirs),
        common,
        [(r_last, 0, 0), (swap(r_last), 0, 1), (q_last, 0, 2), (swap(q_last), 0, 3)],
        [half] * 4, 1, span, total=total, part_out=True, final=(resid, gate),
    )
    updated, grad_attn = step(
        where(far, others + mine, others + theirs),
        common,
        [(x_last, 0, 0), (swap(x_last), 0, 1)],
        [half] * 2, 1, span, total=total, part=part, final=(resid, gate), main=updated, back=grad_attn,
    )
    return updated, grad_attn, grad_down, grad_up_t


def gather_body(
    attn,
    resid,
    frozen,
    adapter_down_weight,
    adapter_up_weight,
    timestep_gate,
    guidance_gate,
    timestep_index,
    guidance_index,
    cotangent,
):
    rows, features = attn.shape
    axis_size = lax.axis_size("blk")
    whole = lax.all_gather(frozen, "blk", axis=0, tiled=True)
    sample = (lax.axis_index("blk") * rows + jnp.arange(rows, dtype=jnp.int32)) // IMAGE_TOKENS
    gate = timestep_gate[timestep_index[sample]] + guidance_gate[guidance_index[sample]]
    down_half = adapter_down_weight.astype(BF16)
    up_half = adapter_up_weight.astype(BF16)
    low = matmul(attn, down_half).astype(BF16)
    gout = (gate * cotangent.astype(F32)).astype(BF16)
    glow = contract_cols(gout, up_half).astype(BF16)
    terms = jnp.concatenate([contract_rows(attn, glow), contract_rows(gout, low)], 1)
    summed = lax.psum_scatter(terms, "blk", scatter_dimension=0, tiled=True)
    grad_scale = float(rows * axis_size) ** (-0.5)
    rank = glow.shape[1]
    base = matmul(attn, whole) + matmul(low, up_half)
    updated = (resid.astype(F32) + gate * base).astype(BF16)
    grad_attn = (contract_cols(gout, whole) + contract_cols(glow, down_half)).astype(BF16)
    return updated, grad_attn, grad_scale * summed[:, :rank], grad_scale * summed[:, rank:]


def solution(mesh):
    def run(attn, resid, frozen, *rest):
        axis_size, groups = mesh.shape["blk"], mesh.shape["groups"]
        rows, span = attn.shape[0] // (axis_size * groups), 2 * frozen.shape[0] // axis_size
        by_ring = groups == 2 and axis_size % 4 == 0 and axis_size >= 8 and axis_size & (axis_size - 1) == 0
        by_ring = by_ring and span % 128 == 0 and frozen.shape[1] % 768 == 0 and IMAGE_TOKENS % rows == 0
        spec = P(("groups", "blk"), None)
        return jax.shard_map(
            ring_body if by_ring else gather_body,
            mesh=mesh,
            in_specs=(spec, spec, P("blk", None), P(), P(), P(), P(), P("groups"), P("groups"), spec),
            out_specs=(spec, spec, spec, spec),
            check_vma=False,
        )(attn, resid, frozen, *rest)

    return run
```

time: 243 us -> 178 us (0.73); the launches traced: 243 us -> 175 us
  waiting for transfers between devices: 196 us -> 53.1 us
  Pallas kernels: 0 us -> 37.8 us
  starting transfers between devices: 0.08 us -> 26.1 us
  matrix products: 29.3 us -> 4.42 us
  other arithmetic: 1.71 us -> 23.6 us
  local copies, waits for them, and re-layouts: 0.03 us -> 18 us
  between operations: 15.6 us -> 12.3 us
    all_gather x1 -> x0, waiting for transfers between devices: 97.8 us -> none  [body(): slab_rows = lax.all_gather(frozen, 'blk', axis=0, tiled=True)]
    psum x1 -> x0, waiting for transfers between devices: 97.8 us -> none  [body(): total_down, total_up = lax.psum((term_down, term_up), 'blk')]
    ppermute x0 -> x31, waiting for transfers between devices: none -> 53.1 us  [the longest x4 34 us: scatter_sum(): terms = keep + lax.ppermute(give, 'blk', pairs).astype(F32)]
    pallas_call x0 -> x6, Pallas kernels: none -> 37.8 us  [step(): pl.pallas_call(functools.partial(step_kernel, spec), out_shape=(jax.Shape...]
    ppermute x0 -> x31, starting transfers between devices: none -> 26.1 us  [the longest x6 8.62 us: ring_body(): r, q = (ring(r), ring(q))]
    dot_general x5 -> x1, matrix products: 14.6 us -> 1.21 us  [matmul(): return jnp.dot(left, right, preferred_element_type=F32)]
    dot_general x3 -> x1, matrix products: 11.9 us -> 0.55 us  [contract_cols(): lax.dot_general(left, right, (((1,), (1,)), ((), ())), preferred_element_...]
    unnamed x12 -> x44, local copies, waits for them, and re-layouts: 0.03 us -> 6.35 us
  transfers between devices with their start and end apart: 2 -> 31, of which waited for: 2 -> 5; matrix products, arithmetic and copies ran while one was open for 1% -> 22% of each run, Pallas kernels for 0% -> 20%
where the time goes in v1:
time: 178 us; the launch traced here: 175 us
  waiting for transfers between devices  53.1 us (30%)
  Pallas kernels  37.8 us (21%)
  starting transfers between devices  26.1 us (15%)
  other arithmetic  23.6 us (13%)
  local copies, waits for them, and re-layouts  18 us (10%)
  between operations  12.3 us (7%)
  matrix products  4.42 us (2%)
    pallas_call x6, Pallas kernels, step(): pl.pallas_call(functools.partial(step_kernel, spec), out_shape=(jax.Shape...  37.8 us
    ppermute x4, waiting for transfers between devices, scatter_sum(): terms = keep + lax.ppermute(give, 'blk', pairs).astype(F32)  34 us
    ppermute x3, waiting for transfers between devices, ring_body(): x = cross(r)  19 us
    ppermute x6, starting transfers between devices, ring_body(): r, q = (ring(r), ring(q))  8.62 us
    ppermute x4, starting transfers between devices, scatter_sum(): terms = keep + lax.ppermute(give, 'blk', pairs).astype(F32)  7.13 us
    unnamed x44, local copies, waits for them, and re-layouts  6.35 us
    select_n x3, other arithmetic, both_cores(): jnp.where(k == 0, mine, other)  4.81 us
    ppermute x3, starting transfers between devices, ring_body(): x = cross(r)  3.58 us
  transfers between devices with their start and end apart: 31, of which 5 were waited for; matrix products, arithmetic and copies ran while one was open for 22% of the time, Pallas kernels for 20%

profile of v1, /device:TPU:0, one launch (start us, length us, event | category | flops | bytes accessed | tf_op | source)
XLA Modules:
  0.0 175.3 jit_solution(4148460426640540590)
XLA Ops:
  0.6 1.9 %dynamic_slice.55 = bf16[192,1024]{1,0:T(8,128)(2,1)} slice(bf16[192,3072]{1,0:T(8,128)(2,1)} %param.13), slice={[0:192], [1024:2048]} | slice | bytes 786432 | tf_op jit(solution)/shard_map/dynamic_slice | solution.py:260
  10.8 1.4 fusion.19
  12.2 2.5 %broadcast_select_fusion.3 = (bf16[192,1024]{1,0:T(8,128)(2,1)}, bf16[192,1024]{1,0:T(8,128)(2,1)}, bf16[192,1024]{1,0:T(8,128)(2,1)}, bf16[192,1024]{1,0:T(8,128)(2,1)}) fusion(bf16[192,1024]{1,0:T(8,128)(2,1)} %collective-permute-done.8, pred[]{:T(512)S(6)} %eq.44, bf16[192,3072]{1,0:T(8,128)(2,1)S(1)} %copy-done.16, s32[]{:T(128)S(6)} %select_n.226, ...), kind=kLoop, calls=%fused_computation.18 | loop fusion | flops 393216 | bytes 3145737 | tf_op jit(solution)/shard_map/jit(_where)/select_n | solution.py:262
  16.0 3.0 %copy.35 = f32[3072,128]{1,0:T(8,128)} copy(f32[3072,128]{0,1:T(8,128)} %pad_maximum_fusion) | data formatting | bytes 3145728 | tf_op jit(solution)/shard_map/concatenate | solution.py:291
  19.0 2.2 %fusion.7 = bf16[8,192,128]{2,1,0:T(8,128)(2,1)} fusion(f32[8,2,192,128]{3,2,1,0:T(8,128)} %bitcast.74, pred[]{:T(512)S(6)} %eq.48), kind=kLoop, calls=%fused_computation.12 | loop fusion | flops 196608 | bytes 1179649 | tf_op jit(solution)/shard_map/convert_element_type | solution.py:219
  21.7 2.1 %pad_maximum_fusion.2.refs_8_ = bf16[384,1024]{1,0:T(8,128)(2,1)} fusion(bf16[192,1024]{1,0:T(8,128)(2,1)} %get-tuple-element.35, bf16[192,1024]{1,0:T(8,128)(2,1)} %get-tuple-element.34), kind=kLoop, calls=%fused_computation.8 | loop fusion | flops 1572864 | bytes 1572864 | tf_op jit(solution)/shard_map/concatenate | solution.py:263
  23.7 2.5 %collective-permute-start.9 = (bf16[384,1024]{1,0:T(8,128)(2,1)}, bf16[384,1024]{1,0:T(8,128)(2,1)}, u32[]{:S(2)}, u32[]{:S(2)}) collective-permute-start(bf16[384,1024]{1,0:T(8,128)(2,1)} %pad_maximum_fusion.2.refs_8_), channel_id=1, source_target_pairs={{0,2},{1,5},{2,6},{3,1},{6,10},{7,3},{10,14},{11,7},{14,12},{15,11... | collective-permute-start | bytes 2359304 | tf_op jit(solution)/shard_map/ppermute | solution.py:271
  28.4 1.6 collective-permute-start.1
  32.7 1.6 collective-permute-start.28
  34.2 14.5 %collective-permute-done.28 = bf16[4,192,128]{2,1,0:T(8,128)(2,1)} collective-permute-done((bf16[4,192,128]{2,1,0:T(8,128)(2,1)}, bf16[4,192,128]{2,1,0:T(8,128)(2,1)}, u32[]{:S(2)}, u32[]{:S(2)}) %collective-permute-start.28) | collective-permute-done | bytes 196640 | tf_op jit(solution)/shard_map/ppermute | solution.py:220
  50.2 2.5 %collective-permute-start.10 = (bf16[384,1024]{1,0:T(8,128)(2,1)}, bf16[384,1024]{1,0:T(8,128)(2,1)}, u32[]{:S(2)}, u32[]{:S(2)}) collective-permute-start(bf16[384,1024]{1,0:T(8,128)(2,1)} %collective-permute-done.9.refs_9_), channel_id=1, source_target_pairs={{0,2},{1,5},{2,6},{3,1},{6,10},{7,3},{10,14},{11,7},{14,12},{15,11... | collective-permute-start | bytes 2359304 | tf_op jit(solution)/shard_map/ppermute | solution.py:271
  53.4 2.0 %collective-permute-start.29 = (bf16[2,192,128]{2,1,0:T(8,128)(2,1)}, bf16[2,192,128]{2,1,0:T(8,128)(2,1)}, u32[]{:S(2)}, u32[]{:S(2)}) collective-permute-start(bf16[2,192,128]{2,1,0:T(8,128)(2,1)} %fusion.14), channel_id=1, source_target_pairs={{0,4},{1,5},{2,6},{3,7},{4,0},{5,1},{6,2},{7,3},{8,12},{9,13},{10,... | collective-permute-start | bytes 294920 | tf_op jit(solution)/shard_map/ppermute | solution.py:220
  56.1 16.9 %collective-permute-done.29 = bf16[2,192,128]{2,1,0:T(8,128)(2,1)} collective-permute-done((bf16[2,192,128]{2,1,0:T(8,128)(2,1)}, bf16[2,192,128]{2,1,0:T(8,128)(2,1)}, u32[]{:S(2)}, u32[]{:S(2)}) %collective-permute-start.29) | collective-permute-done | bytes 98336 | tf_op jit(solution)/shard_map/ppermute | solution.py:220
  74.8 3.1 %collective-permute-start.30 = (bf16[1,192,128]{2,1,0:T(8,128)(2,1)S(1)}, bf16[1,192,128]{2,1,0:T(8,128)(2,1)S(1)}, u32[]{:S(2)}, u32[]{:S(2)}) collective-permute-start(bf16[1,192,128]{2,1,0:T(8,128)(2,1)S(1)} %fusion.16), channel_id=1, source_target_pairs={{0,8},{1,9},{2,10},{3,11},{4,12},{5,13},{6,14},{7,15},{8,0},{9,1},... | collective-permute-start | bytes 147464 | tf_op jit(solution)/shard_map/ppermute | solution.py:220
  78.0 2.6 %collective-permute-done.30 = bf16[1,192,128]{2,1,0:T(8,128)(2,1)S(1)} collective-permute-done((bf16[1,192,128]{2,1,0:T(8,128)(2,1)S(1)}, bf16[1,192,128]{2,1,0:T(8,128)(2,1)S(1)}, u32[]{:S(2)}, u32[]{:S(2)}) %collective-permute-start.30) | collective-permute-done | bytes 49184 | tf_op jit(solution)/shard_map/ppermute | solution.py:220
  81.2 1.5 collective-permute-start.21
  83.3 1.8 %collective-permute-start.3 = (bf16[384,1024]{1,0:T(8,128)(2,1)}, bf16[384,1024]{1,0:T(8,128)(2,1)}, u32[]{:S(2)}, u32[]{:S(2)}) collective-permute-start(bf16[384,1024]{1,0:T(8,128)(2,1)} %collective-permute-done.2.refs_7_), channel_id=1, source_target_pairs={{0,2},{1,5},{2,6},{3,1},{6,10},{7,3},{10,14},{11,7},{14,12},{15,11... | collective-permute-start | bytes 2359304 | tf_op jit(solution)/shard_map/ppermute | solution.py:271
  85.1 1.9 %convert_bitcast_fusion.refs_6_ = bf16[64,3072]{1,0:T(8,128)(2,1)} fusion(f32[3072,64]{0,1:T(8,128)} %param.14), kind=kLoop, calls=%fused_computation.27 | loop fusion | flops 196608 | bytes 1179648 | tf_op jit(solution)/shard_map/transpose | solution.py:297
  87.0 11.9 %collective-permute-done.21.refs_11_ = bf16[384,1024]{1,0:T(8,128)(2,1)} collective-permute-done((bf16[384,1024]{1,0:T(8,128)(2,1)}, bf16[384,1024]{1,0:T(8,128)(2,1)}, u32[]{:S(2)}, u32[]{:S(2)}) %collective-permute-start.21) | collective-permute-done | bytes 786464 | tf_op jit(solution)/shard_map/ppermute | solution.py:272
  98.9 1.6 collective-permute-start.17
  115.7 1.8 %constant_dynamic-slice_fusion = bf16[384,512]{1,0:T(8,128)(2,1)} fusion(bf16[384,1024]{1,0:T(8,128)(2,1)} %collective-permute-done.11.refs_9_, s32[]{:T(128)S(6)} %select_n.209), kind=kLoop, calls=%fused_computation.39 | loop fusion | bytes 786436 | tf_op jit(solution)/shard_map/dynamic_slice | solution.py:277
  117.5 2.4 %collective-permute-start.25 = (bf16[384,512]{1,0:T(8,128)(2,1)}, bf16[384,512]{1,0:T(8,128)(2,1)}, u32[]{:S(2)}, u32[]{:S(2)}) collective-permute-start(bf16[384,512]{1,0:T(8,128)(2,1)} %constant_dynamic-slice_fusion), channel_id=1, source_target_pairs={{0,2},{1,5},{2,6},{3,1},{6,10},{7,3},{10,14},{11,7},{14,12},{15,11... | collective-permute-start | bytes 1179656 | tf_op jit(solution)/shard_map/ppermute | solution.py:277
  120.9 1.8 %constant_dynamic-slice_fusion.2 = bf16[384,512]{1,0:T(8,128)(2,1)} fusion(bf16[384,1024]{1,0:T(8,128)(2,1)} %collective-permute-done.3.refs_7_, s32[]{:T(128)S(6)} %select_n.209), kind=kLoop, calls=%fused_computation.41 | loop fusion | bytes 786436 | tf_op jit(solution)/shard_map/dynamic_slice | solution.py:276
  124.0 1.6 copy.40
  125.6 1.6 copy.41
  127.4 7.1 %collective-permute-done.13.refs_11_ = bf16[384,1024]{1,0:T(8,128)(2,1)} collective-permute-done((bf16[384,1024]{1,0:T(8,128)(2,1)}, bf16[384,1024]{1,0:T(8,128)(2,1)}, u32[]{:S(2)}, u32[]{:S(2)}) %collective-permute-start.13) | collective-permute-done | bytes 786464 | tf_op jit(solution)/shard_map/ppermute | solution.py:272
  136.3 5.9 %shard_map.138 = (f32[256,3072]{1,0:T(8,128)S(1)}, bf16[256,3072]{1,0:T(8,128)(2,1)}) custom-call(s32[4]{0:T(128)S(1)} %pad_add_fusion.1.refs_0_, bf16[256,3072]{1,0:T(8,128)(2,1)S(1)} %copy-done, bf16[256,3072]{1,0:T(8,128)(2,1)S(1)} %multiply_convert_fusion.refs_2_, bf16[256,64]{1,0:T(8,128)(2,1)S(1)} %copy-done.3, ...), custom_call_target="tpu_custom_call" | custom-call | flops 1207959552 | bytes 12582912 | tf_op jit(solution)/shard_map/pallas_call | solution.py:185
  142.3 8.0 %shard_map.139 = (f32[256,3072]{1,0:T(8,128)S(1)}, bf16[256,3072]{1,0:T(8,128)(2,1)}) custom-call(s32[5]{0:T(128)S(1)} %copy-done.10, bf16[256,3072]{1,0:T(8,128)(2,1)S(1)} %copy-done, bf16[256,3072]{1,0:T(8,128)(2,1)S(1)} %multiply_convert_fusion.refs_2_, bf16[256,64]{1,0:T(8,128)(2,1)S(1)} %copy-done.3, ...), custom_call_target="tpu_custom_call", output_to_operand_aliasing={{0}: (13, {}), {1}: (14, {})} | custom-call | flops 2415919104 | bytes 12582912 | tf_op jit(solution)/shard_map/pallas_call | solution.py:185
  151.1 7.9 %shard_map.140 = (f32[256,3072]{1,0:T(8,128)S(1)}, bf16[256,3072]{1,0:T(8,128)(2,1)}) custom-call(s32[5]{0:T(128)S(1)} %copy-done.9, bf16[256,3072]{1,0:T(8,128)(2,1)S(1)} %copy-done, bf16[256,3072]{1,0:T(8,128)(2,1)S(1)} %multiply_convert_fusion.refs_2_, bf16[256,64]{1,0:T(8,128)(2,1)S(1)} %copy-done.3, ...), custom_call_target="tpu_custom_call", output_to_operand_aliasing={{0}: (13, {}), {1}: (14, {})} | custom-call | flops 2415919104 | bytes 12582912 | tf_op jit(solution)/shard_map/pallas_call | solution.py:185
  159.1 8.0 %shard_map.141 = (f32[256,3072]{1,0:T(8,128)S(1)}, bf16[256,3072]{1,0:T(8,128)(2,1)}) custom-call(s32[5]{0:T(128)S(1)} %copy-done.8, bf16[256,3072]{1,0:T(8,128)(2,1)S(1)} %copy-done, bf16[256,3072]{1,0:T(8,128)(2,1)S(1)} %multiply_convert_fusion.refs_2_, bf16[256,64]{1,0:T(8,128)(2,1)S(1)} %copy-done.3, ...), custom_call_target="tpu_custom_call", output_to_operand_aliasing={{0}: (13, {}), {1}: (14, {})} | custom-call | flops 2415919104 | bytes 12582912 | tf_op jit(solution)/shard_map/pallas_call | solution.py:185
  167.1 4.7 %shard_map.142 = (bf16[256,3072]{1,0:T(8,128)(2,1)}, f32[256,384]{1,0:T(8,128)S(1)}) custom-call(s32[5]{0:T(128)S(1)} %copy-done.7, bf16[256,3072]{1,0:T(8,128)(2,1)S(1)} %copy-done, bf16[256,3072]{1,0:T(8,128)(2,1)S(1)} %multiply_convert_fusion.refs_2_, bf16[256,64]{1,0:T(8,128)(2,1)S(1)} %copy-done.3, bf16[64,3072]{1,0:T(8,128)(2,1)S(1)} %convert_element_type.66.refs_4_, ...), custom_call_target="tpu_custom_call" | custom-call | flops 805306368 | bytes 12582912 | tf_op jit(solution)/shard_map/pallas_call | solution.py:185
  171.9 3.2 %shard_map.143 = (bf16[256,3072]{1,0:T(8,128)(2,1)}, bf16[256,3072]{1,0:T(8,128)(2,1)}) custom-call(s32[3]{0:T(128)S(1)} %copy-done.6, bf16[256,3072]{1,0:T(8,128)(2,1)S(1)} %copy-done, bf16[256,3072]{1,0:T(8,128)(2,1)S(1)} %multiply_convert_fusion.refs_2_, bf16[256,64]{1,0:T(8,128)(2,1)S(1)} %copy-done.3, ...), custom_call_target="tpu_custom_call", output_to_operand_aliasing={{0}: (13, {}), {1}: (14, {})} | custom-call | flops 402653184 | bytes 12582912 | tf_op jit(solution)/shard_map/pallas_call | solution.py:185
  (116 shorter events, 30.1 us)
Async XLA Ops:
  2.5 9.7 %collective-permute-start.8 = (bf16[192,1024]{1,0:T(8,128)(2,1)}, bf16[192,1024]{1,0:T(8,128)(2,1)}, u32[]{:S(2)}, u32[]{:S(2)}) collective-permute-start(bf16[192,1024]{1,0:T(8,128)(2,1)} %dynamic_slice.55), channel_id=1, source_target_pairs={{0,1},{1,0},{2,3},{3,2},{4,5},{5,4},{6,7},{7,6},{8,9},{9,8},{10,11... | collective-permute-start | bytes 1179656 | tf_op jit(solution)/shard_map/ppermute | solution.py:261
  14.7 11.6 %collective-permute-start = (bf16[192,1024]{1,0:T(8,128)(2,1)}, bf16[192,1024]{1,0:T(8,128)(2,1)}, u32[]{:S(2)}, u32[]{:S(2)}) collective-permute-start(bf16[192,1024]{1,0:T(8,128)(2,1)} %get-tuple-element.37), channel_id=1, source_target_pairs={{0,1},{1,0},{2,3},{3,2},{4,5},{5,4},{6,7},{7,6},{8,9},{9,8},{10,11... | collective-permute-start | bytes 1179656 | tf_op jit(solution)/shard_map/ppermute | solution.py:261
  21.2 8.7 %collective-permute-start.27 = (bf16[8,192,128]{2,1,0:T(8,128)(2,1)}, bf16[8,192,128]{2,1,0:T(8,128)(2,1)}, u32[]{:S(2)}, u32[]{:S(2)}) collective-permute-start(bf16[8,192,128]{2,1,0:T(8,128)(2,1)} %fusion.7), channel_id=1, source_target_pairs={{0,1},{1,0},{2,3},{3,2},{4,5},{5,4},{6,7},{7,6},{8,9},{9,8},{10,11... | collective-permute-start | bytes 1179656 | tf_op jit(solution)/shard_map/ppermute | solution.py:220
  23.7 26.3 %collective-permute-start.9 = (bf16[384,1024]{1,0:T(8,128)(2,1)}, bf16[384,1024]{1,0:T(8,128)(2,1)}, u32[]{:S(2)}, u32[]{:S(2)}) collective-permute-start(bf16[384,1024]{1,0:T(8,128)(2,1)} %pad_maximum_fusion.2.refs_8_), channel_id=1, source_target_pairs={{0,2},{1,5},{2,6},{3,1},{6,10},{7,3},{10,14},{11,7},{14,12},{15,11... | collective-permute-start | bytes 2359304 | tf_op jit(solution)/shard_map/ppermute | solution.py:271
  28.4 24.3 %collective-permute-start.1 = (bf16[384,1024]{1,0:T(8,128)(2,1)}, bf16[384,1024]{1,0:T(8,128)(2,1)}, u32[]{:S(2)}, u32[]{:S(2)}) collective-permute-start(bf16[384,1024]{1,0:T(8,128)(2,1)} %pad_maximum_fusion.1.refs_7_), channel_id=1, source_target_pairs={{0,2},{1,5},{2,6},{3,1},{6,10},{7,3},{10,14},{11,7},{14,12},{15,11... | collective-permute-start | bytes 2359304 | tf_op jit(solution)/shard_map/ppermute | solution.py:271
  32.7 16.1 %collective-permute-start.28 = (bf16[4,192,128]{2,1,0:T(8,128)(2,1)}, bf16[4,192,128]{2,1,0:T(8,128)(2,1)}, u32[]{:S(2)}, u32[]{:S(2)}) collective-permute-start(bf16[4,192,128]{2,1,0:T(8,128)(2,1)} %fusion.8), channel_id=1, source_target_pairs={{0,2},{1,3},{2,0},{3,1},{4,6},{5,7},{6,4},{7,5},{8,10},{9,11},{10,... | collective-permute-start | bytes 589832 | tf_op jit(solution)/shard_map/ppermute | solution.py:220
  34.2 66.7 %copy-start.20 = (s32[8]{0:T(128)S(1)}, s32[8]{0:T(128)}, u32[]{:S(2)}) copy-start(s32[8]{0:T(128)} %constant.139.clone) | copy-start | bytes 100
  50.0 32.9 %collective-permute-start.20 = (bf16[384,1024]{1,0:T(8,128)(2,1)}, bf16[384,1024]{1,0:T(8,128)(2,1)}, u32[]{:S(2)}, u32[]{:S(2)}) collective-permute-start(bf16[384,1024]{1,0:T(8,128)(2,1)} %collective-permute-done.9.refs_9_), channel_id=1, source_target_pairs={{0,1},{1,0},{2,3},{3,2},{4,5},{5,4},{6,7},{7,6},{8,9},{9,8},{10,11... | collective-permute-start | bytes 2359304 | tf_op jit(solution)/shard_map/ppermute | solution.py:312
  50.2 32.6 %collective-permute-start.10 = (bf16[384,1024]{1,0:T(8,128)(2,1)}, bf16[384,1024]{1,0:T(8,128)(2,1)}, u32[]{:S(2)}, u32[]{:S(2)}) collective-permute-start(bf16[384,1024]{1,0:T(8,128)(2,1)} %collective-permute-done.9.refs_9_), channel_id=1, source_target_pairs={{0,2},{1,5},{2,6},{3,1},{6,10},{7,3},{10,14},{11,7},{14,12},{15,11... | collective-permute-start | bytes 2359304 | tf_op jit(solution)/shard_map/ppermute | solution.py:271
  52.6 30.7 %collective-permute-start.2 = (bf16[384,1024]{1,0:T(8,128)(2,1)}, bf16[384,1024]{1,0:T(8,128)(2,1)}, u32[]{:S(2)}, u32[]{:S(2)}) collective-permute-start(bf16[384,1024]{1,0:T(8,128)(2,1)} %collective-permute-done.1.refs_7_), channel_id=1, source_target_pairs={{0,2},{1,5},{2,6},{3,1},{6,10},{7,3},{10,14},{11,7},{14,12},{15,11... | collective-permute-start | bytes 2359304 | tf_op jit(solution)/shard_map/ppermute | solution.py:271
  53.4 19.6 %collective-permute-start.29 = (bf16[2,192,128]{2,1,0:T(8,128)(2,1)}, bf16[2,192,128]{2,1,0:T(8,128)(2,1)}, u32[]{:S(2)}, u32[]{:S(2)}) collective-permute-start(bf16[2,192,128]{2,1,0:T(8,128)(2,1)} %fusion.14), channel_id=1, source_target_pairs={{0,4},{1,5},{2,6},{3,7},{4,0},{5,1},{6,2},{7,3},{8,12},{9,13},{10,... | collective-permute-start | bytes 294920 | tf_op jit(solution)/shard_map/ppermute | solution.py:220
  55.3 27.4 %collective-permute-start.23 = (bf16[192,1024]{1,0:T(8,128)(2,1)}, bf16[192,1024]{1,0:T(8,128)(2,1)}, u32[]{:S(2)}, u32[]{:S(2)}) collective-permute-start(bf16[192,1024]{1,0:T(8,128)(2,1)} %get-tuple-element.36), channel_id=1, source_target_pairs={{0,1},{1,0},{2,3},{3,2},{4,5},{5,4},{6,7},{7,6},{8,9},{9,8},{10,11... | collective-permute-start | bytes 1179656 | tf_op jit(solution)/shard_map/ppermute | solution.py:261
  74.8 5.7 %collective-permute-start.30 = (bf16[1,192,128]{2,1,0:T(8,128)(2,1)S(1)}, bf16[1,192,128]{2,1,0:T(8,128)(2,1)S(1)}, u32[]{:S(2)}, u32[]{:S(2)}) collective-permute-start(bf16[1,192,128]{2,1,0:T(8,128)(2,1)S(1)} %fusion.16), channel_id=1, source_target_pairs={{0,8},{1,9},{2,10},{3,11},{4,12},{5,13},{6,14},{7,15},{8,0},{9,1},... | collective-permute-start | bytes 147464 | tf_op jit(solution)/shard_map/ppermute | solution.py:220
  81.2 17.7 %collective-permute-start.21 = (bf16[384,1024]{1,0:T(8,128)(2,1)}, bf16[384,1024]{1,0:T(8,128)(2,1)}, u32[]{:S(2)}, u32[]{:S(2)}) collective-permute-start(bf16[384,1024]{1,0:T(8,128)(2,1)} %collective-permute-done.1.refs_7_), channel_id=1, source_target_pairs={{0,16},{16,0},{1,17},{17,1},{2,18},{18,2},{3,19},{19,3},{4,20},{20... | collective-permute-start | bytes 2359304 | tf_op jit(solution)/shard_map/ppermute | solution.py:272
  82.7 17.7 %collective-permute-start.19 = (bf16[384,1024]{1,0:T(8,128)(2,1)}, bf16[384,1024]{1,0:T(8,128)(2,1)}, u32[]{:S(2)}, u32[]{:S(2)}) collective-permute-start(bf16[384,1024]{1,0:T(8,128)(2,1)} %collective-permute-done.1.refs_7_), channel_id=1, source_target_pairs={{0,1},{1,0},{2,3},{3,2},{4,5},{5,4},{6,7},{7,6},{8,9},{9,8},{10,11... | collective-permute-start | bytes 2359304 | tf_op jit(solution)/shard_map/ppermute | solution.py:311
  82.7 17.7 %collective-permute-start.11 = (bf16[384,1024]{1,0:T(8,128)(2,1)}, bf16[384,1024]{1,0:T(8,128)(2,1)}, u32[]{:S(2)}, u32[]{:S(2)}) collective-permute-start(bf16[384,1024]{1,0:T(8,128)(2,1)} %collective-permute-done.10.refs_9_), channel_id=1, source_target_pairs={{0,2},{1,5},{2,6},{3,1},{6,10},{7,3},{10,14},{11,7},{14,12},{15,11... | collective-permute-start | bytes 2359304 | tf_op jit(solution)/shard_map/ppermute | solution.py:271
  83.0 34.6 %collective-permute-start.16 = (bf16[384,1024]{1,0:T(8,128)(2,1)}, bf16[384,1024]{1,0:T(8,128)(2,1)}, u32[]{:S(2)}, u32[]{:S(2)}) collective-permute-start(bf16[384,1024]{1,0:T(8,128)(2,1)} %collective-permute-done.10.refs_9_), channel_id=1, source_target_pairs={{0,1},{1,0},{2,3},{3,2},{4,5},{5,4},{6,7},{7,6},{8,9},{9,8},{10,11... | collective-permute-start | bytes 2359304 | tf_op jit(solution)/shard_map/ppermute | solution.py:312
  83.3 31.3 %collective-permute-start.3 = (bf16[384,1024]{1,0:T(8,128)(2,1)}, bf16[384,1024]{1,0:T(8,128)(2,1)}, u32[]{:S(2)}, u32[]{:S(2)}) collective-permute-start(bf16[384,1024]{1,0:T(8,128)(2,1)} %collective-permute-done.2.refs_7_), channel_id=1, source_target_pairs={{0,2},{1,5},{2,6},{3,1},{6,10},{7,3},{10,14},{11,7},{14,12},{15,11... | collective-permute-start | bytes 2359304 | tf_op jit(solution)/shard_map/ppermute | solution.py:271
  98.9 23.8 %collective-permute-start.17 = (bf16[384,1024]{1,0:T(8,128)(2,1)}, bf16[384,1024]{1,0:T(8,128)(2,1)}, u32[]{:S(2)}, u32[]{:S(2)}) collective-permute-start(bf16[384,1024]{1,0:T(8,128)(2,1)} %collective-permute-done.2.refs_7_), channel_id=1, source_target_pairs={{0,16},{16,0},{1,17},{17,1},{2,18},{18,2},{3,19},{19,3},{4,20},{20... | collective-permute-start | bytes 2359304 | tf_op jit(solution)/shard_map/ppermute | solution.py:272
  100.4 22.3 %collective-permute-start.15 = (bf16[384,1024]{1,0:T(8,128)(2,1)}, bf16[384,1024]{1,0:T(8,128)(2,1)}, u32[]{:S(2)}, u32[]{:S(2)}) collective-permute-start(bf16[384,1024]{1,0:T(8,128)(2,1)} %collective-permute-done.2.refs_7_), channel_id=1, source_target_pairs={{0,1},{1,0},{2,3},{3,2},{4,5},{5,4},{6,7},{7,6},{8,9},{9,8},{10,11... | collective-permute-start | bytes 2359304 | tf_op jit(solution)/shard_map/ppermute | solution.py:311
  100.5 22.2 %collective-permute-start.22 = (bf16[384,1024]{1,0:T(8,128)(2,1)}, bf16[384,1024]{1,0:T(8,128)(2,1)}, u32[]{:S(2)}, u32[]{:S(2)}) collective-permute-start(bf16[384,1024]{1,0:T(8,128)(2,1)} %collective-permute-done.21.refs_11_), channel_id=1, source_target_pairs={{0,1},{1,0},{2,3},{3,2},{4,5},{5,4},{6,7},{7,6},{8,9},{9,8},{10,11... | collective-permute-start | bytes 2359304 | tf_op jit(solution)/shard_map/ppermute | solution.py:313
  114.7 19.8 %collective-permute-start.13 = (bf16[384,1024]{1,0:T(8,128)(2,1)}, bf16[384,1024]{1,0:T(8,128)(2,1)}, u32[]{:S(2)}, u32[]{:S(2)}) collective-permute-start(bf16[384,1024]{1,0:T(8,128)(2,1)} %collective-permute-done.3.refs_7_), channel_id=1, source_target_pairs={{0,16},{16,0},{1,17},{17,1},{2,18},{18,2},{3,19},{19,3},{4,20},{20... | collective-permute-start | bytes 2359304 | tf_op jit(solution)/shard_map/ppermute | solution.py:272
  117.5 9.7 %collective-permute-start.25 = (bf16[384,512]{1,0:T(8,128)(2,1)}, bf16[384,512]{1,0:T(8,128)(2,1)}, u32[]{:S(2)}, u32[]{:S(2)}) collective-permute-start(bf16[384,512]{1,0:T(8,128)(2,1)} %constant_dynamic-slice_fusion), channel_id=1, source_target_pairs={{0,2},{1,5},{2,6},{3,1},{6,10},{7,3},{10,14},{11,7},{14,12},{15,11... | collective-permute-start | bytes 1179656 | tf_op jit(solution)/shard_map/ppermute | solution.py:277
  122.7 27.6 %collective-permute-start.12 = (bf16[384,1024]{1,0:T(8,128)(2,1)}, bf16[384,1024]{1,0:T(8,128)(2,1)}, u32[]{:S(2)}, u32[]{:S(2)}) collective-permute-start(bf16[384,1024]{1,0:T(8,128)(2,1)} %collective-permute-done.11.refs_9_), channel_id=1, source_target_pairs={{0,1},{1,0},{2,3},{3,2},{4,5},{5,4},{6,7},{7,6},{8,9},{9,8},{10,11... | collective-permute-start | bytes 2359304 | tf_op jit(solution)/shard_map/ppermute | solution.py:312
  122.7 13.0 %collective-permute-start.4 = (bf16[384,512]{1,0:T(8,128)(2,1)}, bf16[384,512]{1,0:T(8,128)(2,1)}, u32[]{:S(2)}, u32[]{:S(2)}) collective-permute-start(bf16[384,512]{1,0:T(8,128)(2,1)} %constant_dynamic-slice_fusion.2), channel_id=1, source_target_pairs={{0,2},{1,5},{2,6},{3,1},{6,10},{7,3},{10,14},{11,7},{14,12},{15,11... | collective-permute-start | bytes 1179656 | tf_op jit(solution)/shard_map/ppermute | solution.py:276
  122.8 27.8 %collective-permute-start.18 = (bf16[384,1024]{1,0:T(8,128)(2,1)}, bf16[384,1024]{1,0:T(8,128)(2,1)}, u32[]{:S(2)}, u32[]{:S(2)}) collective-permute-start(bf16[384,1024]{1,0:T(8,128)(2,1)} %collective-permute-done.17.refs_11_), channel_id=1, source_target_pairs={{0,1},{1,0},{2,3},{3,2},{4,5},{5,4},{6,7},{7,6},{8,9},{9,8},{10,11... | collective-permute-start | bytes 2359304 | tf_op jit(solution)/shard_map/ppermute | solution.py:313
  127.2 31.8 %collective-permute-start.7 = (bf16[384,1024]{1,0:T(8,128)(2,1)}, bf16[384,1024]{1,0:T(8,128)(2,1)S(1)}, u32[]{:S(2)}, u32[]{:S(2)}) collective-permute-start(bf16[384,1024]{1,0:T(8,128)(2,1)} %collective-permute-done.3.refs_7_), channel_id=1, source_target_pairs={{0,1},{1,0},{2,3},{3,2},{4,5},{5,4},{6,7},{7,6},{8,9},{9,8},{10,11... | collective-permute-start | bytes 2359304 | tf_op jit(solution)/shard_map/ppermute | solution.py:311
  134.5 24.5 %collective-permute-start.14 = (bf16[384,1024]{1,0:T(8,128)(2,1)}, bf16[384,1024]{1,0:T(8,128)(2,1)S(1)}, u32[]{:S(2)}, u32[]{:S(2)}) collective-permute-start(bf16[384,1024]{1,0:T(8,128)(2,1)} %collective-permute-done.13.refs_11_), channel_id=1, source_target_pairs={{0,1},{1,0},{2,3},{3,2},{4,5},{5,4},{6,7},{7,6},{8,9},{9,8},{10,11... | collective-permute-start | bytes 2359304 | tf_op jit(solution)/shard_map/ppermute | solution.py:313
  135.7 15.1 %collective-permute-start.5 = (bf16[384,512]{1,0:T(8,128)(2,1)}, bf16[384,512]{1,0:T(8,128)(2,1)S(1)}, u32[]{:S(2)}, u32[]{:S(2)}) collective-permute-start(bf16[384,512]{1,0:T(8,128)(2,1)} %collective-permute-done.4.refs_7_), channel_id=1, source_target_pairs={{0,16},{16,0},{1,17},{17,1},{2,18},{18,2},{3,19},{19,3},{4,20},{20... | collective-permute-start | bytes 1179656 | tf_op jit(solution)/shard_map/ppermute | solution.py:278
  150.3 16.8 %collective-permute-start.26 = (bf16[384,512]{1,0:T(8,128)(2,1)}, bf16[384,512]{1,0:T(8,128)(2,1)S(1)}, u32[]{:S(2)}, u32[]{:S(2)}) collective-permute-start(bf16[384,512]{1,0:T(8,128)(2,1)} %collective-permute-done.25.refs_9_), channel_id=1, source_target_pairs={{0,1},{1,0},{2,3},{3,2},{4,5},{5,4},{6,7},{7,6},{8,9},{9,8},{10,11... | collective-permute-start | bytes 1179656 | tf_op jit(solution)/shard_map/ppermute | solution.py:323
  150.6 16.5 %collective-permute-start.24 = (bf16[384,512]{1,0:T(8,128)(2,1)}, bf16[384,512]{1,0:T(8,128)(2,1)S(1)}, u32[]{:S(2)}, u32[]{:S(2)}) collective-permute-start(bf16[384,512]{1,0:T(8,128)(2,1)} %collective-permute-done.4.refs_7_), channel_id=1, source_target_pairs={{0,1},{1,0},{2,3},{3,2},{4,5},{5,4},{6,7},{7,6},{8,9},{9,8},{10,11... | collective-permute-start | bytes 1179656 | tf_op jit(solution)/shard_map/ppermute | solution.py:323
  150.8 21.0 %collective-permute-start.6 = (bf16[384,512]{1,0:T(8,128)(2,1)S(1)}, bf16[384,512]{1,0:T(8,128)(2,1)S(1)}, u32[]{:S(2)}, u32[]{:S(2)}) collective-permute-start(bf16[384,512]{1,0:T(8,128)(2,1)S(1)} %collective-permute-done.5.refs_7_), channel_id=1, source_target_pairs={{0,1},{1,0},{2,3},{3,2},{4,5},{5,4},{6,7},{7,6},{8,9},{9,8},{10,11... | collective-permute-start | bytes 1179656 | tf_op jit(solution)/shard_map/ppermute | solution.py:329
  (20 other events, 96.8 us)

commit v2 on v0

v2 whole, which is shorter than its diff:
```python
import functools

import jax
import jax.numpy as jnp
import numpy as np
from jax import lax
from jax.experimental import pallas as pl
from jax.experimental.pallas import tpu as pltpu
from jax.sharding import PartitionSpec as P

IMAGE_TOKENS = 4096
F32 = jnp.float32
BF16 = jnp.bfloat16


def contract_rows(left, right):
    return lax.dot_general(left, right, (((0,), (0,)), ((), ())), preferred_element_type=F32)


def contract_cols(left, right):
    return lax.dot_general(left, right, (((1,), (1,)), ((), ())), preferred_element_type=F32)


def matmul(left, right):
    return jnp.dot(left, right, preferred_element_type=F32)


def ring_order(chips):
    return [0] + list(range(1, chips, 2)) + list(range(chips - 2, 0, -2))


def ring_pairs(chips):
    order = ring_order(chips)
    pairs = []
    for place, chip in enumerate(order):
        after, before = order[(place + 1) % chips], order[(place - 1) % chips]
        pairs += [(2 * chip, 2 * after), (2 * chip + 1, 2 * before + 1)]
    return pairs


WIDTHS = (7, 4, 6, 7)
OWN = 6


def near(distance):
    return 5 + 2 * distance


def across(distance):
    return 6 + 2 * distance


def blocks_of(features):
    lane = features // 24
    return tuple(width * lane for width in WIDTHS)


def place_table(groups, axis_size, rows, span, features):
    chips = axis_size // 2
    order = ring_order(chips)
    wide, middle, third, _ = blocks_of(features)
    table = []
    for g in range(groups):
        for b in range(axis_size):
            chip, core = divmod(b, 2)
            at, toward = order.index(chip), 2 * core - 1
            far_side = wide + middle + third
            own, others = (0, far_side) if g == 0 else (far_side, 0)
            line = [core, b * rows // IMAGE_TOKENS, own, wide, wide + middle, others, chip * span]
            for n in range(1, chips // 2):
                line += [order[(at + toward * n) % chips] * span, order[(at - toward * n) % chips] * span]
            table.append(line + [order[(at + chips // 2) % chips] * span])
    return np.asarray(table, np.int32)


STEP_LIMIT = 16
VMEM_SPEC = pl.BlockSpec(memory_space=pltpu.VMEM)
SMEM_SPEC = pl.BlockSpec(memory_space=pltpu.SMEM)
HBM_SPEC = pl.BlockSpec(memory_space=pltpu.HBM)


def cols(start, width):
    return pl.ds(pl.multiple_of(start, 128), width)


def half_rows(core, shard):
    return pl.ds(pl.multiple_of(core * shard, 16), shard)


def call(kernel, args, specs, out_shape, out_specs, scratch=(), aliases=None, weight=1, limit=16):
    return pl.pallas_call(
        kernel,
        in_specs=specs,
        out_shape=out_shape,
        out_specs=out_specs,
        scratch_shapes=scratch,
        input_output_aliases=aliases or {},
        compiler_params=pltpu.CompilerParams(vmem_limit_bytes=limit * 1024 * 1024),
        cost_estimate=pl.CostEstimate(flops=0, bytes_accessed=weight, transcendentals=0),
    )(*args)


def cut(place, frozen, blocks):
    shard = frozen.shape[0]

    def kernel(place, frozen, *refs):
        outs, sems = refs[:-1], refs[-1]
        copies = []
        for n, width in enumerate(blocks):
            copies.append(pltpu.make_async_copy(frozen.at[:, cols(place[2 + n], width)], outs[n], sems.at[n]))
            copies[n].start()
        for copy in copies:
            copy.wait()

    return call(
        kernel, (place, frozen), [SMEM_SPEC, HBM_SPEC], [jax.ShapeDtypeStruct((shard, w), BF16) for w in blocks],
        [VMEM_SPEC] * len(blocks), [pltpu.SemaphoreType.DMA((len(blocks),))], limit=4,
    )


def pair(place, mine, theirs, blocks, which):
    shard = theirs.shape[0]

    def kernel(place, *refs):
        theirs, refs = refs[len(which)], refs[: len(which)] + refs[len(which) + 1 :]
        for n, block in enumerate(which):
            out = refs[len(which) + n]
            out[half_rows(place[0], shard), :] = refs[n][...]
            out[half_rows(1 - place[0], shard), :] = theirs[:, cols(place[2 + block], blocks[block])]

    return call(
        kernel, (place, *[mine[block] for block in which], theirs), [SMEM_SPEC] + [VMEM_SPEC] * (len(which) + 1),
        [jax.ShapeDtypeStruct((2 * shard, blocks[block]), BF16) for block in which], [VMEM_SPEC] * len(which), limit=4,
    )


def own_half(place, whole):
    shard, width = whole.shape[0] // 2, whole.shape[1]

    def kernel(place, whole, out):
        out[...] = whole[half_rows(place[0], shard), :]

    return call(
        kernel, (place, whole), [SMEM_SPEC, VMEM_SPEC], jax.ShapeDtypeStruct((shard, width), BF16), VMEM_SPEC, limit=4,
    )


def adapter(place, t_index, g_index, attn, cotangent, down_t, up, t_gate, g_gate, blocks, chips):
    rows, features = attn.shape
    rank = up.shape[0]
    span = features // chips

    def kernel(place, t_index, g_index, attn, cotangent, down_t, up, t_gate, g_gate,
               gate_out, gout_out, low_out, up_out, down_out, terms_out, give_out, gout_v):
        sample = place[1]
        gate = t_gate[pl.ds(t_index[sample], 1), :] + g_gate[pl.ds(g_index[sample], 1), :]
        gout = (gate * cotangent[...].astype(F32)).astype(BF16)
        gout_v[...] = gout
        up_half = up[...].astype(BF16)
        down_half = down_t[...].astype(BF16)
        down_out[...] = down_half
        low = contract_cols(attn[...], down_half).astype(BF16)
        glow = contract_cols(gout, up_half).astype(BF16)
        low_out[...] = low
        at = 0
        for n, width in enumerate(blocks):
            here, there = pl.ds(at, width), cols(place[2 + n], width)
            gout_out[:, here] = gout_v[:, there]
            up_out[:, here] = up[:, there].astype(BF16)
            gate_out[:, here] = t_gate[pl.ds(t_index[sample], 1), there] + g_gate[pl.ds(g_index[sample], 1), there]
            at += width
        gout_out[:, pl.ds(features, 128)] = jnp.concatenate([glow, jnp.zeros((rows, 128 - rank), BF16)], 1)
        both = jnp.concatenate([contract_rows(glow, attn[...]), contract_rows(low, gout)], 0)
        terms = both.T.reshape(chips, span, 2 * rank)
        terms_out[...] = terms
        give_out[...] = terms.astype(BF16)

    shape = jax.ShapeDtypeStruct
    return call(
        kernel,
        (place, t_index, g_index, attn, cotangent, down_t, up, t_gate, g_gate),
        [SMEM_SPEC] * 3 + [VMEM_SPEC] * 6,
        [
            shape((1, features), F32),
            shape((rows, features + 128), BF16),
            shape((rows, rank), BF16),
            shape((rank, features), BF16),
            shape((rank, features), BF16),
            shape((chips, span, 2 * rank), F32),
            shape((chips, span, 2 * rank), BF16),
        ],
        [VMEM_SPEC] * 7,
        [pltpu.VMEM((rows, features), BF16)],
    )


def chunk(place, slot, block, width, terms, theirs, which):
    _, span, lanes = terms.shape
    shard = span // 2

    def kernel(place, block, terms, theirs, out):
        chip, rest = lax.div(place[slot], span), pl.ds(width, lanes)
        mine, other = half_rows(place[0], shard), half_rows(1 - place[0], shard)
        out[:, pl.ds(0, width)] = block[:, pl.ds(0, width)]
        if which == "first":
            out[mine, rest] = (terms[chip, mine, :] + theirs[chip, mine, :].astype(F32)).astype(BF16)
            out[other, rest] = jnp.zeros((shard, lanes), BF16)
        else:
            value = terms[chip] + theirs[chip].astype(F32) + block[:, rest].astype(F32)
            out[:, rest] = value.astype(BF16)

    return call(
        kernel, (place, block, terms, theirs), [SMEM_SPEC] + [VMEM_SPEC] * 3,
        jax.ShapeDtypeStruct((span, width + lanes), BF16), VMEM_SPEC, limit=8,
    )


def last_chunk(place, slot, block, second, width, terms, theirs):
    _, span, lanes = terms.shape
    shard, more = span // 2, second.shape[1]

    def kernel(place, block, second, terms, theirs, out):
        chip = lax.div(place[slot], span)
        mine, rest = half_rows(place[0], shard), pl.ds(width, lanes)
        value = (block[:, rest].astype(F32) + terms[chip] + theirs[chip].astype(F32)).astype(BF16)
        out[:, pl.ds(0, width)] = block[mine, pl.ds(0, width)]
        out[:, pl.ds(width, more)] = second[mine, :]
        out[:, pl.ds(width + more, lanes)] = value[:shard]
        out[:, pl.ds(width + more + lanes, lanes)] = value[shard:]

    return call(
        kernel, (place, block, second, terms, theirs), [SMEM_SPEC] + [VMEM_SPEC] * 4,
        jax.ShapeDtypeStruct((shard, width + more + 2 * lanes), BF16), VMEM_SPEC, limit=8,
    )


def finish(place, slot, terms, theirs, block, block_theirs, width, scale):
    _, span, lanes = terms.shape
    shard = span // 2

    def kernel(place, terms, theirs, block, block_theirs, first, second):
        chip = lax.div(place[slot], span)
        mine, rest = half_rows(place[0], shard), cols(width + place[0] * lanes, lanes)
        value = terms[chip, mine, :] + theirs[chip, mine, :].astype(F32)
        value = value + block[:, rest].astype(F32) + block_theirs[:, rest].astype(F32)
        value = (scale * value).T
        first[...] = value[: lanes // 2]
        second[...] = value[lanes // 2 :]

    shape = jax.ShapeDtypeStruct((lanes // 2, shard), F32)
    args = (place, terms, theirs, block, block_theirs)
    return call(kernel, args, [SMEM_SPEC] + [VMEM_SPEC] * (len(args) - 1), [shape] * 2, [VMEM_SPEC] * 2, limit=8)


def side_step(place, distance, attn, gout, mates, down_t, rank, blocks, ring_blocks, x_block, totals, parts, grad_attn, gives, last):
    rows, features = attn.shape
    span = ring_blocks[0].shape[0]
    starts = [sum(blocks[:n]) for n in range(len(blocks))]
    names, args, specs, aliases = [], [], [], {}
    outs, out_specs = [], []

    def give(name, array, spec=VMEM_SPEC):
        names.append(name)
        args.append(array)
        specs.append(spec)

    def produce(name, shape, dtype, spec=VMEM_SPEC, old=None):
        if old is not None:
            aliases[len(args)] = len(outs)
            give(name + "_in", old, spec)
        outs.append((name, jax.ShapeDtypeStruct(shape, dtype)))
        out_specs.append(spec)

    give("place", place, SMEM_SPEC)
    give("attn", attn)
    give("gout", gout)
    give("attn_t", mates[0])
    give("gout_t", mates[1])
    give("down", down_t)
    for n, array in enumerate(ring_blocks):
        give(("ring", n), array)
    if x_block is not None:
        give("x", x_block)
        give("part_old", parts[0])
        give("part_t_old", parts[1])
    if last:
        for n, array in enumerate(gives):
            give(("given", n), array)
    produce("total", (rows, features), F32, old=totals[0])
    if last:
        give("total_t_in", totals[1])
        produce("send", (rows, features + (len(gives) + 2) * span), BF16)
    else:
        produce("total_t", (rows, features), F32, old=totals[1])
    produce("part", (rows, span), F32)
    if not last:
        produce("part_t", (rows, span), F32)
    if x_block is not None:
        produce("grad", (rows, features), BF16, HBM_SPEC, grad_attn)
    if x_block is not None and not last:
        produce("give", (rows, span), BF16)
    out_names = [name for name, _ in outs]

    def kernel(*refs):
        ref = dict(zip(names + [("out", name) for name in out_names], refs))
        grad_v, store = refs[len(names) + len(out_names) :]
        place = ref["place"]
        stores = []

        def put(src, dst):
            copy = pltpu.make_async_copy(src, dst, store.at[len(stores)])
            copy.start()
            stores.append(copy)

        def both(name, at):
            return jnp.concatenate([ref[name][:, at], ref[name + "_t"][:, at]], 0)

        def set_total_t(at, value):
            if last:
                ref[("out", "send")][:, at] = value.astype(BF16)
            else:
                ref[("out", "total_t")][:, at] = value

        if x_block is not None:
            at, there = cols(place[near(distance - 1)], span), pl.ds(starts[3], blocks[3])
            value = matmul(both("attn", at), ref["x"][...])
            ref[("out", "total")][:, there] = ref["total_in"][:, there] + value[:rows]
            value_t = value[rows:]
            if distance > 2:
                value_t = value_t + ref["total_t_in"][:, there]
            set_total_t(there, value_t)
            value = contract_cols(both("gout", there), ref["x"][...])
            grad_v[...] = (value[:rows] + ref["part_old"][...]).astype(BF16)
            put(grad_v, ref[("out", "grad")].at[:, at])
            value = (value[rows:] + ref["part_t_old"][...]).astype(BF16)
            if last:
                for n in range(len(gives)):
                    ref[("out", "send")][:, pl.ds(features + n * span, span)] = ref[("given", n)][...]
                ref[("out", "send")][:, pl.ds(features + len(gives) * span, span)] = value
            else:
                ref[("out", "give")][...] = value
        at = cols(place[near(distance)], span)
        glow = both("gout", pl.ds(features, rank))
        back = matmul(glow, ref["down"][:, at])
        a = both("attn", at)
        for n in range(3):
            there, width = pl.ds(starts[n], blocks[n]), blocks[n]
            piece = ref[("ring", n)][:, pl.ds(0, width)]
            value = matmul(a, piece)
            ref[("out", "total")][:, there] = ref["total_in"][:, there] + value[:rows]
            value_t = value[rows:]
            if distance > 1:
                value_t = value_t + ref["total_t_in"][:, there]
            set_total_t(there, value_t)
            back = back + contract_cols(both("gout", there), piece)
        ref[("out", "part")][...] = back[:rows]
        if last:
            ref[("out", "send")][:, pl.ds(features + (len(gives) + 1) * span, span)] = back[rows:].astype(BF16)
        else:
            ref[("out", "part_t")][...] = back[rows:]
        for copy in stores:
            copy.wait()

    result = call(
        kernel, args, specs, [shape for _, shape in outs], out_specs,
        [pltpu.VMEM((rows, span), BF16), pltpu.SemaphoreType.DMA((2,))], aliases, limit=STEP_LIMIT,
    )
    result = dict(zip(out_names, result))
    return (
        (result["total"], result.get("total_t")), (result["part"], result.get("part_t")), result.get("grad", grad_attn),
        result["send"] if last else result.get("give"),
    )


def step(place, jobs, attn, blocks, grads, total=None, add=None, final=None, updated=None, grad_attn=None, extra=None):
    rows, features = attn.shape
    gout, down_t, rank = grads
    place_span = span_of(jobs)
    starts = [sum(blocks[:n]) for n in range(len(blocks))]
    names, args, specs, aliases = [], [], [], {}

    def give(name, array, spec=VMEM_SPEC):
        names.append(name)
        args.append(array)
        specs.append(spec)

    give("place", place, SMEM_SPEC)
    give("attn", attn)
    give("gout", gout)
    if any(job["part"] is None for job in jobs):
        give("down", down_t)
    if extra is not None:
        give("extra", extra[0])
    if add is not None:
        give("low", add[0])
        give("up", add[1])
    if any(job["final"] for job in jobs):
        give("resid", final[0], HBM_SPEC)
        give("gate", final[1])
    outs, out_specs = [], []

    def produce(name, shape, dtype, spec, old=None):
        if old is not None:
            aliases[len(args)] = len(outs)
            give(name + "_in", old, spec)
        outs.append((name, jax.ShapeDtypeStruct(shape, dtype)))
        out_specs.append(spec)

    if not all(job["final"] for job in jobs):
        produce("total", (rows, features), F32, VMEM_SPEC, total)
    elif total is not None:
        give("total_in", total)
    if any(job["final"] for job in jobs):
        produce("updated", (rows, features), BF16, HBM_SPEC, updated)
    if not all(job["open"] for job in jobs):
        produce("grad", (rows, features), BF16, HBM_SPEC, grad_attn)
    scratch = []
    tiny = pltpu.VMEM((16, 128), BF16)
    for j, job in enumerate(jobs):
        some = job["pieces"][0][0]
        job["halves"] = halves = isinstance(some, tuple)
        job["span"] = span = place_span
        job["width"] = width = sum(blocks[n] for n in job["blocks"])
        job["deep"] = deep = span * len(job["chips"])
        for n, per in enumerate(job["pieces"]):
            for c, array in enumerate(per):
                for h, half in enumerate(array if halves else (array,)):
                    give(("piece", j, n, c, h), half.array if isinstance(half, Part) else half)
        if job["part"] is not None:
            for c, array in enumerate(job["part"]):
                if array is not None:
                    give(("part", j, c), array)
        if job["open"]:
            produce(("open", j), (rows, deep), F32, VMEM_SPEC)
        scratch += [
            pltpu.VMEM((deep, width), BF16) if halves else tiny,
            pltpu.VMEM((rows, width), BF16) if job["final"] else tiny,
            pltpu.VMEM((rows, width), BF16) if job["final"] else tiny,
            tiny if job["open"] else pltpu.VMEM((rows, deep), BF16),
        ]
    n_job = len(scratch)
    scratch += [pltpu.SemaphoreType.DMA((8,)), pltpu.SemaphoreType.DMA((8,))]
    out_names = [name for name, _ in outs]

    def kernel(*refs):
        ref = dict(zip(names + [("out", name) for name in out_names], refs))
        rest = refs[len(names) + len(out_names) :]
        load, store = rest[n_job:]
        place = ref["place"]
        loads, stores = {}, []

        def put(src, dst):
            copy = pltpu.make_async_copy(src, dst, store.at[len(stores)])
            copy.start()
            stores.append(copy)

        for j, job in enumerate(jobs):
            if job["final"]:
                for block in job["blocks"]:
                    here = pl.ds(starts[block] - starts[job["blocks"][0]], blocks[block])
                    src = ref["resid"].at[:, cols(place[2 + block], blocks[block])]
                    loads[j, block] = pltpu.make_async_copy(src, rest[4 * j + 1].at[:, here], load.at[len(loads)])
                    loads[j, block].start()
        if extra is not None and extra[1] is not None:
            span = jobs[0]["span"]
            for n, slot in enumerate(extra[1]):
                put(ref["extra"].at[:, pl.ds(features + n * span, span)], ref[("out", "grad")].at[:, cols(place[slot], span)])
        for j, job in enumerate(jobs):
            frozen_v, resid_v, result_v, back_v = rest[4 * j : 4 * j + 4]
            span = job["span"]
            chip_cols = [cols(place[s], span) for s in job["chips"]]
            back = [None] * len(chip_cols)
            for n, block in enumerate(job["blocks"]):
                width = blocks[block]
                here, there = pl.ds(starts[block] - starts[job["blocks"][0]], width), pl.ds(starts[block], width)
                value = ref["total_in"][:, there] if total is not None else matmul(ref["low"][...], ref["up"][:, there])
                if extra is not None:
                    value = value + ref["extra"][:, there].astype(F32)
                for c, at in enumerate(chip_cols):
                    if job["halves"]:
                        shard = span // 2
                        for h, core in enumerate((place[0], 1 - place[0])):
                            to = pl.ds(pl.multiple_of(c * span + core * shard, 16), shard)
                            half = job["pieces"][n][c][h]
                            row, col = (half.row, half.col) if isinstance(half, Part) else (0, 0)
                            frozen_v[to, here] = ref[("piece", j, n, c, h)][pl.ds(row, shard), pl.ds(col, width)]
                        piece = frozen_v[pl.ds(c * span, span), here]
                    else:
                        piece = ref[("piece", j, n, c, 0)][pl.ds(0, span), :]
                    value = value + matmul(ref["attn"][:, at], piece)
                    term = contract_cols(ref["gout"][:, there], piece)
                    back[c] = term if back[c] is None else back[c] + term
                if job["final"]:
                    loads[j, block].wait()
                    result_v[:, here] = (resid_v[:, here].astype(F32) + ref["gate"][:, there] * value).astype(BF16)
                    put(result_v.at[:, here], ref[("out", "updated")].at[:, cols(place[2 + block], width)])
                else:
                    ref[("out", "total")][:, there] = value
            for c, at in enumerate(chip_cols):
                mine = pl.ds(c * span, span)
                if job["part"] is None:
                    value = back[c] + matmul(ref["gout"][:, pl.ds(features, rank)], ref["down"][:, at])
                else:
                    from_mate = job["part"][c] is None
                    part = ref["extra"][:, pl.ds(features + len(extra[1]) * span, span)].astype(F32) if from_mate else ref[("part", j, c)][...]
                    value = back[c] + part
                if job["open"]:
                    ref[("out", ("open", j))][:, mine] = value
                else:
                    back_v[:, mine] = value.astype(BF16)
                    put(back_v.at[:, mine], ref[("out", "grad")].at[:, at])
        for copy in stores:
            copy.wait()

    result = call(
        kernel, args, specs, [shape for _, shape in outs], out_specs, scratch, aliases,
        weight=12, limit=STEP_LIMIT,
    )
    result = dict(zip(out_names, result))
    opened = [result[("open", j)] for j, job in enumerate(jobs) if job["open"]]
    return result.get("total", total), result.get("updated", updated), result.get("grad", grad_attn), *opened


class Part:
    def __init__(self, array, row=0, col=0):
        self.array, self.row, self.col = array, row, col


def span_of(jobs):
    sizes = []
    for job in jobs:
        some = job["pieces"][0][0]
        sizes.append(2 * some[0].shape[0] if isinstance(some, tuple) else some.shape[0])
    return min(sizes)


def job(chips, blocks, pieces, part=None, open=False, final=False):
    return dict(chips=chips, blocks=blocks, pieces=pieces, part=part, open=open, final=final)


EDGES = dict(
    gout="s",
    k0="s",
    r1="T",
    x1="T",
    q1="rTm",
    s2="Tx",
    k2="x",
    r3="S",
    x3="S",
    q3="Tx",
    s3="Tx",
    k3="x",
    r4="TX",
    x4="s",
    q4="rT",
    send="r",
    q5="e",
)
WHEN = "srs"


def after(value, *others):
    return lax.optimization_barrier((value, *others))[0]


def ring_body(
    table,
    attn,
    resid,
    frozen,
    adapter_down_weight,
    adapter_up_weight,
    timestep_gate,
    guidance_gate,
    timestep_index,
    guidance_index,
    cotangent,
):
    rows, features = attn.shape
    axis_size = lax.axis_size("blk")
    chips = axis_size // 2
    blocks = blocks_of(features)
    me = lax.axis_index("blk")
    device = lax.axis_index("groups") * axis_size + me
    core_pairs = [(i, i ^ 1) for i in range(axis_size)]
    ring = functools.partial(lax.ppermute, axis_name="blk", perm=ring_pairs(chips))
    swap = functools.partial(lax.ppermute, axis_name="blk", perm=core_pairs)
    cross = functools.partial(lax.ppermute, axis_name="groups", perm=[(0, 1), (1, 0)])
    place = lax.dynamic_index_in_dim(jnp.asarray(table), device, 0, False)

    rank = adapter_up_weight.shape[0]
    steps = chips // 2 - 1
    far = near(steps + 1)
    wide = blocks[1]
    def gate(name, value, **have):
        others = [have[k] for k in EDGES.get(name, "") if have.get(k) is not None]
        return after(value, *others) if others else value

    theirs = swap(frozen)
    own = pair(place, cut(place, frozen, blocks), theirs, blocks, [0, 1, 2, 3])
    r, q, s = [None, ring(own[0])], [None], [None, ring(own[2])]
    known = dict(o=own[0], p=own[1], r=r[1], s=s[1])
    attn_t = known["a"] = swap(gate("attn", attn, **known))
    gate_row, gout, low, up, down_t, terms, given = adapter(
        place, timestep_index, guidance_index, attn, gate("adapter", cotangent, **known),
        adapter_down_weight.T, adapter_up_weight, timestep_gate, guidance_gate, blocks, chips,
    )
    terms_t = known["t"] = swap(given)
    first_q = known["f"] = chunk(place, far, own[1], wide, terms, terms_t, "first")
    q.append(ring(first_q))
    known["q"] = q[1]
    gout_t = known["m"] = swap(gate("gout", gout, **known))
    grads = (gout, down_t, rank)
    total, _, grad_attn = step(
        place, [job([OWN], [0, 1, 2, 3], [[block] for block in own])], attn, blocks,
        (gate("k0", gout, **known), down_t, rank), add=(low, up),
    )
    totals, parts, give, gives, x = (total, None), None, None, [], [None]

    def run(n, arrival, **have):
        nonlocal totals, parts, grad_attn, give
        last = n == steps
        totals, parts, grad_attn, give = side_step(
            place, n, attn, gate(f"k{n}", after(gout, arrival), **have), (attn_t, gout_t), down_t, rank, blocks,
            [r[n], q[n], s[n]], x[n - 1], totals, parts, grad_attn, gives, last,
        )
        if give is not None and not last:
            gives.append(give)

    for n in range(1, steps + 1):
        last = n == steps
        prev = dict(T=totals[0], x=x[n - 1], S=s[n - 1], Q=q[n - 1])
        r[n] = gate(f"r{n}", r[n], **{**known, **prev})
        r.append(ring(own_half(place, r[n]) if last else r[n]))
        x.append(cross(gate(f"x{n}", r[n], **prev)))
        if n > 1 and WHEN[n - 2] == "r":
            run(n - 1, r[n], x=x[n - 1], X=x[n - 2])
        q[n] = gate(f"q{n}", q[n], **{**known, "r": r[n], "T": totals[0], "x": x[n - 1]})
        if not last:
            q.append(ring(chunk(place, across(steps + 1 - n), q[n], wide, terms, terms_t, "middle")))
        if n > 1 and WHEN[n - 2] == "q":
            run(n - 1, q[n], x=x[n - 1], X=x[n - 2])
        s[n] = gate(f"s{n}", s[n], **{**known, "q": q[n], "r": r[n], "T": totals[0], "x": x[n - 1]})
        if last:
            q.append(ring(last_chunk(place, across(1), q[n], s[n], wide, terms, terms_t)))
        else:
            s.append(ring(s[n]))
        if WHEN[n - 1] == "s":
            run(n, s[n], x=x[n - 1])

    r_far = gate("r4", r[steps + 1], X=x[steps], T=totals[0], s=s[steps], q=q[steps])
    x_far = cross(gate("x4", r_far, X=x[steps], T=totals[0], s=s[steps]))
    if WHEN[steps - 1] == "r":
        run(steps, r_far, X=x[steps])
    x_before = gate("back", x[steps], r=r_far)
    x_swapped, r_swapped = swap(x_before), swap(r_far)
    swaps = dict(v=x_swapped, w=r_swapped)
    q_far = gate("q4", q[steps + 1], r=r_far, T=totals[0], **swaps)
    if WHEN[steps - 1] == "q":
        run(steps, q_far, X=x[steps])
    extra = swap(gate("send", give, r=r_far, X=x[steps], q=q_far))
    q_swapped = swap(gate("q5", q_far, e=extra, **swaps))
    grad_scale = float(rows * axis_size) ** (-0.5)
    grad_down_t, grad_up = finish(place, OWN, terms, terms_t, q_far, q_swapped, wide + blocks[2], grad_scale)
    x_job = job([near(steps), across(steps)], [3], [[x_before, x_swapped]], part=[parts[0], None])
    s_piece = (Part(q_far, 0, wide), Part(q_swapped, 0, wide))
    far_job = job([far], [0, 1, 2], [[(r_far, r_swapped)], [(q_far, q_swapped)], [s_piece]], open=True, final=True)
    total, updated, grad_attn, part = step(
        place, [x_job, far_job], attn, blocks, (after(gout, grad_down_t), down_t, rank), total=totals[0],
        final=(resid, gate_row), grad_attn=grad_attn, extra=(extra, [across(n) for n in range(1, steps)]),
    )
    x_far = gate("x5", x_far, s=q_far, q=q_far, T=total)
    _, updated, grad_attn = step(
        place, [job([far], [3], [[(x_far, swap(x_far))]], part=[part], final=True)],
        attn, blocks, grads, total=total, final=(resid, gate_row), updated=updated, grad_attn=grad_attn,
    )
    return updated, grad_attn, grad_down_t.T, grad_up.T


def gather_body(
    attn,
    resid,
    frozen,
    adapter_down_weight,
    adapter_up_weight,
    timestep_gate,
    guidance_gate,
    timestep_index,
    guidance_index,
    cotangent,
):
    rows, features = attn.shape
    axis_size = lax.axis_size("blk")
    whole = lax.all_gather(frozen, "blk", axis=0, tiled=True)
    sample = (lax.axis_index("blk") * rows + jnp.arange(rows, dtype=jnp.int32)) // IMAGE_TOKENS
    gate = timestep_gate[timestep_index[sample]] + guidance_gate[guidance_index[sample]]
    down_half = adapter_down_weight.astype(BF16)
    up_half = adapter_up_weight.astype(BF16)
    low = matmul(attn, down_half).astype(BF16)
    gout = (gate * cotangent.astype(F32)).astype(BF16)
    glow = contract_cols(gout, up_half).astype(BF16)
    terms = jnp.concatenate([contract_rows(attn, glow), contract_rows(gout, low)], 1)
    summed = lax.psum_scatter(terms, "blk", scatter_dimension=0, tiled=True)
    grad_scale = float(rows * axis_size) ** (-0.5)
    rank = glow.shape[1]
    base = matmul(attn, whole) + matmul(low, up_half)
    updated = (resid.astype(F32) + gate * base).astype(BF16)
    grad_attn = (contract_cols(gout, whole) + contract_cols(glow, down_half)).astype(BF16)
    return updated, grad_attn, grad_scale * summed[:, :rank], grad_scale * summed[:, rank:]


def solution(mesh):
    def run(attn, resid, frozen, *rest):
        axis_size, groups = mesh.shape["blk"], mesh.shape["groups"]
        rows, span = attn.shape[0] // (axis_size * groups), 2 * frozen.shape[0] // axis_size
        by_ring = groups == 2 and axis_size == 16
        by_ring = by_ring and span % 128 == 0 and frozen.shape[1] % 3072 == 0 and IMAGE_TOKENS % rows == 0
        body = gather_body
        if by_ring:
            table = place_table(groups, axis_size, rows, span, frozen.shape[1])
            body = functools.partial(ring_body, table)
        spec = P(("groups", "blk"), None)
        return jax.shard_map(
            body,
            mesh=mesh,
            in_specs=(spec, spec, P("blk", None), P(), P(), P(), P(), P("groups"), P("groups"), spec),
            out_specs=(spec, spec, spec, spec),
            check_vma=False,
        )(attn, resid, frozen, *rest)

    return run
```

time: 243 us -> 97.8 us (0.40)
  waiting for transfers between devices: 196 us -> 27.1 us
  Pallas kernels: 0 us -> 33.5 us
  matrix products: 29.3 us -> 0 us
  starting transfers between devices: 0.08 us -> 29.2 us
  between operations: 15.6 us -> 2.32 us
  local copies, waits for them, and re-layouts: 0.03 us -> 5.34 us
    all_gather x1 -> x0, waiting for transfers between devices: 97.8 us -> none  [body(): slab_rows = lax.all_gather(frozen, 'blk', axis=0, tiled=True)]
    psum x1 -> x0, waiting for transfers between devices: 97.8 us -> none  [body(): total_down, total_up = lax.psum((term_down, term_up), 'blk')]
    pallas_call x0 -> x15, Pallas kernels: none -> 33.5 us  [call(): pl.pallas_call(kernel, in_specs=specs, out_shape=out_shape, out_specs=out...]
    dot_general x10 -> x0, matrix products: 29.3 us -> none  [the longest x3 11.9 us: contract_cols(): lax.dot_general(left, right, (((1,), (1,)), ((), ())), preferred_element_...]
    ppermute x0 -> x24, starting transfers between devices: none -> 29.2 us  [the longest x3 5.74 us: ring_body(): r.append(ring(own_half(place, r[n]) if last else r[n]))]
    ppermute x0 -> x24, waiting for transfers between devices: none -> 27.1 us  [the longest x1 6.4 us: ring_body(): ring(last_chunk(place, across(1), q[n], s[n], wide, terms, terms_t))]
    unnamed x12 -> x16, local copies, waits for them, and re-layouts: 0.03 us -> 4.65 us
  transfers between devices with their start and end apart: 2 -> 24, of which waited for: 2 -> 8; matrix products, arithmetic and copies ran while one was open for 1% -> 1% of each run, Pallas kernels for 0% -> 31%
where the time goes in v2:
time: 97.8 us; the launch traced here: 97.4 us
  Pallas kernels  33.5 us (34%)
  starting transfers between devices  29.2 us (30%)
  waiting for transfers between devices  27.1 us (28%)
  local copies, waits for them, and re-layouts  5.34 us (5%)
  between operations  2.32 us (2%)
    pallas_call x15, Pallas kernels, call(): pl.pallas_call(kernel, in_specs=specs, out_shape=out_shape, out_specs=out...  33.5 us
    ppermute x1, waiting for transfers between devices, ring_body(): ring(last_chunk(place, across(1), q[n], s[n], wide, terms, terms_t))  6.4 us
    ppermute x3, starting transfers between devices, ring_body(): r.append(ring(own_half(place, r[n]) if last else r[n]))  5.74 us
    ppermute x3, waiting for transfers between devices, ring_body(): r.append(ring(own_half(place, r[n]) if last else r[n]))  5.26 us
    ppermute x3, starting transfers between devices, ring_body(): x.append(cross(gate(f'x{n}', r[n], **prev)))  4.92 us
    unnamed x16, local copies, waits for them, and re-layouts  4.65 us
    ppermute x2, waiting for transfers between devices, ring_body(): s.append(ring(s[n]))  4.56 us
    ppermute x2, starting transfers between devices, ring_body(): r, q, s = ([None, ring(own[0])], [None], [None, ring(own[2])])  4.5 us
  transfers between devices with their start and end apart: 24, of which 8 were waited for; matrix products, arithmetic and copies ran while one was open for 1% of the time, Pallas kernels for 31%

profile of v2, /device:TPU:0, one launch (start us, length us, event | category | flops | bytes accessed | tf_op | source)
XLA Modules:
  0.0 97.4 jit_solution(8997258955299225448)
XLA Ops:
  1.8 1.3 %copy-done.3 = bf16[192,3072]{1,0:T(8,128)(2,1)S(1)} copy-done((bf16[192,3072]{1,0:T(8,128)(2,1)S(1)}, bf16[192,3072]{1,0:T(8,128)(2,1)}, u32[]{:S(2)}) %copy-start.3) | copy-done | bytes 1179672
  4.6 2.9 %collective-permute-start.4 = (bf16[384,768]{1,0:T(8,128)(2,1)S(1)}, bf16[384,768]{1,0:T(8,128)(2,1)S(1)}, u32[]{:S(2)}, u32[]{:S(2)}) collective-permute-start(bf16[384,768]{1,0:T(8,128)(2,1)S(1)} %get-tuple-element.72.refs_8_), channel_id=1, source_target_pairs={{0,2},{1,5},{2,6},{3,1},{6,10},{7,3},{10,14},{11,7},{14,12},{15,11... | collective-permute-start | bytes 1769480 | tf_op jit(solution)/shard_map/ppermute | solution.py:602
  7.5 1.6 %collective-permute-start.3 = (bf16[384,896]{1,0:T(8,128)(2,1)S(1)}, bf16[384,896]{1,0:T(8,128)(2,1)S(1)}, u32[]{:S(2)}, u32[]{:S(2)}) collective-permute-start(bf16[384,896]{1,0:T(8,128)(2,1)S(1)} %get-tuple-element.71.refs_6_), channel_id=1, source_target_pairs={{0,2},{1,5},{2,6},{3,1},{6,10},{7,3},{10,14},{11,7},{14,12},{15,11... | collective-permute-start | bytes 2064392 | tf_op jit(solution)/shard_map/ppermute | solution.py:602
  13.8 2.5 %shard_map.138 = (f32[1,3072]{1,0:T(1,128)S(1)}, bf16[256,3200]{1,0:T(8,128)(2,1)S(1)}, bf16[256,64]{1,0:T(8,128)(2,1)S(1)}, bf16[64,3072]{1,0:T(8,128)(2,1)S(1)...) custom-call(s32[14]{0:T(128)S(1)} %dynamic-slice_bitcast_fusion.place.refs_0_, ...), custom_call_target="tpu_custom_call" | custom-call | bytes 1 | tf_op jit(solution)/shard_map/pallas_call | solution.py:91
  17.0 3.7 %shard_map.142 = (f32[256,3072]{1,0:T(8,128)S(1)}, bf16[256,3072]{1,0:T(8,128)(2,1)}) custom-call(s32[14]{0:T(128)S(1)} %dynamic-slice_bitcast_fusion.place.refs_0_, bf16[256,3072]{1,0:T(8,128)(2,1)S(1)} %copy-done, bf16[256,3200]{1,0:T(8,128)(2,1)S(1)} %get-tuple-element.109.refs_2_, bf16[64,3072]{1,0:T(8,128)(2,1)S(1)} %get-tuple-element.74.refs_3_.refs_5_, ...), custom_call_target="tpu_custom_call" | custom-call | bytes 12 | tf_op jit(solution)/shard_map/pallas_call | solution.py:91
  20.7 2.1 %collective-permute-done.3.refs_6_ = bf16[384,896]{1,0:T(8,128)(2,1)S(1)} collective-permute-done((bf16[384,896]{1,0:T(8,128)(2,1)S(1)}, bf16[384,896]{1,0:T(8,128)(2,1)S(1)}, u32[]{:S(2)}, u32[]{:S(2)}) %collective-permute-start.3) | collective-permute-done | bytes 688160 | tf_op jit(solution)/shard_map/ppermute | solution.py:602
  22.8 2.0 %collective-permute-start.8 = (bf16[384,896]{1,0:T(8,128)(2,1)S(1)}, bf16[384,896]{1,0:T(8,128)(2,1)S(1)}, u32[]{:S(2)}, u32[]{:S(2)}) collective-permute-start(bf16[384,896]{1,0:T(8,128)(2,1)S(1)} %collective-permute-done.3.refs_6_), channel_id=1, source_target_pairs={{0,2},{1,5},{2,6},{3,1},{6,10},{7,3},{10,14},{11,7},{14,12},{15,11... | collective-permute-start | bytes 2064392 | tf_op jit(solution)/shard_map/ppermute | solution.py:635
  25.3 1.6 %collective-permute-start.2 = (bf16[384,640]{1,0:T(8,128)(2,1)S(1)}, bf16[384,640]{1,0:T(8,128)(2,1)S(1)}, u32[]{:S(2)}, u32[]{:S(2)}) collective-permute-start(bf16[384,640]{1,0:T(8,128)(2,1)S(1)} %shard_map.141), channel_id=1, source_target_pairs={{0,2},{1,5},{2,6},{3,1},{6,10},{7,3},{10,14},{11,7},{14,12},{15,11... | collective-permute-start | bytes 1474568 | tf_op jit(solution)/shard_map/ppermute | solution.py:611
  27.0 1.5 %collective-permute-start.12 = (bf16[384,896]{1,0:T(8,128)(2,1)S(1)}, bf16[384,896]{1,0:T(8,128)(2,1)S(1)}, u32[]{:S(2)}, u32[]{:S(2)}) collective-permute-start(bf16[384,896]{1,0:T(8,128)(2,1)S(1)} %collective-permute-done.3.refs_6_), channel_id=1, source_target_pairs={{0,16},{16,0},{1,17},{17,1},{2,18},{18,2},{3,19},{19,3},{4,20},{20... | collective-permute-start | bytes 2064392 | tf_op jit(solution)/shard_map/ppermute | solution.py:636
  28.5 5.3 %collective-permute-done.8.refs_6_ = bf16[384,896]{1,0:T(8,128)(2,1)S(1)} collective-permute-done((bf16[384,896]{1,0:T(8,128)(2,1)S(1)}, bf16[384,896]{1,0:T(8,128)(2,1)S(1)}, u32[]{:S(2)}, u32[]{:S(2)}) %collective-permute-start.8) | collective-permute-done | bytes 688160 | tf_op jit(solution)/shard_map/ppermute | solution.py:635
  33.7 2.0 %collective-permute-start.9 = (bf16[384,896]{1,0:T(8,128)(2,1)S(1)}, bf16[384,896]{1,0:T(8,128)(2,1)S(1)}, u32[]{:S(2)}, u32[]{:S(2)}) collective-permute-start(bf16[384,896]{1,0:T(8,128)(2,1)S(1)} %collective-permute-done.8.refs_6_), channel_id=1, source_target_pairs={{0,2},{1,5},{2,6},{3,1},{6,10},{7,3},{10,14},{11,7},{14,12},{15,11... | collective-permute-start | bytes 2064392 | tf_op jit(solution)/shard_map/ppermute | solution.py:635
  35.7 3.3 %collective-permute-done.2.block.refs_7_ = bf16[384,640]{1,0:T(8,128)(2,1)S(1)} collective-permute-done((bf16[384,640]{1,0:T(8,128)(2,1)S(1)}, bf16[384,640]{1,0:T(8,128)(2,1)S(1)}, u32[]{:S(2)}, u32[]{:S(2)}) %collective-permute-start.2) | collective-permute-done | bytes 491552 | tf_op jit(solution)/shard_map/ppermute | solution.py:611
  39.0 2.0 %collective-permute-start.10 = (bf16[384,768]{1,0:T(8,128)(2,1)S(1)}, bf16[384,768]{1,0:T(8,128)(2,1)S(1)}, u32[]{:S(2)}, u32[]{:S(2)}) collective-permute-start(bf16[384,768]{1,0:T(8,128)(2,1)S(1)} %collective-permute-done.4.refs_8_), channel_id=1, source_target_pairs={{0,2},{1,5},{2,6},{3,1},{6,10},{7,3},{10,14},{11,7},{14,12},{15,11... | collective-permute-start | bytes 1769480 | tf_op jit(solution)/shard_map/ppermute | solution.py:648
  41.6 1.6 %collective-permute-start.6 = (bf16[384,640]{1,0:T(8,128)(2,1)S(1)}, bf16[384,640]{1,0:T(8,128)(2,1)S(1)}, u32[]{:S(2)}, u32[]{:S(2)}) collective-permute-start(bf16[384,640]{1,0:T(8,128)(2,1)S(1)} %shard_map.143), channel_id=1, source_target_pairs={{0,2},{1,5},{2,6},{3,1},{6,10},{7,3},{10,14},{11,7},{14,12},{15,11... | collective-permute-start | bytes 1474568 | tf_op jit(solution)/shard_map/ppermute | solution.py:641
  43.2 1.5 %collective-permute-start.13 = (bf16[384,896]{1,0:T(8,128)(2,1)S(1)}, bf16[384,896]{1,0:T(8,128)(2,1)S(1)}, u32[]{:S(2)}, u32[]{:S(2)}) collective-permute-start(bf16[384,896]{1,0:T(8,128)(2,1)S(1)} %collective-permute-done.8.refs_6_), channel_id=1, source_target_pairs={{0,16},{16,0},{1,17},{17,1},{2,18},{18,2},{3,19},{19,3},{4,20},{20... | collective-permute-start | bytes 2064392 | tf_op jit(solution)/shard_map/ppermute | solution.py:636
  44.7 3.4 %shard_map.145 = (f32[256,3072]{1,0:T(8,128)S(1)}, f32[256,3072]{1,0:T(8,128)S(1)}, f32[256,384]{1,0:T(8,128)S(1)}, f32[256,384]{1,0:T(8,128)S(1)}) custom-call(s32[14]{0:T(128)S(1)} %dynamic-slice_bitcast_fusion.place.refs_0_, bf16[256,3072]{1,0:T(8,128)(2,1)S(1)} %copy-done, ...), custom_call_target="tpu_custom_call", output_to_operand_aliasing={{0}: (9, {})} | custom-call | bytes 1 | tf_op jit(solution)/shard_map/pallas_call | solution.py:91
  48.1 4.6 %collective-permute-done.10.refs_8_ = bf16[384,768]{1,0:T(8,128)(2,1)S(1)} collective-permute-done((bf16[384,768]{1,0:T(8,128)(2,1)S(1)}, bf16[384,768]{1,0:T(8,128)(2,1)S(1)}, u32[]{:S(2)}, u32[]{:S(2)}) %collective-permute-start.10) | collective-permute-done | bytes 589856 | tf_op jit(solution)/shard_map/ppermute | solution.py:648
  52.7 1.9 %collective-permute-start.17 = (bf16[384,896]{1,0:T(8,128)(2,1)S(1)}, bf16[384,896]{1,0:T(8,128)(2,1)S(1)}, u32[]{:S(2)}, u32[]{:S(2)}) collective-permute-start(bf16[384,896]{1,0:T(8,128)(2,1)S(1)} %collective-permute-done.9.whole.refs_6_), channel_id=1, source_target_pairs={{0,16},{16,0},{1,17},{17,1},{2,18},{18,2},{3,19},{19,3},{4,20},{20... | collective-permute-start | bytes 2064392 | tf_op jit(solution)/shard_map/ppermute | solution.py:636
  54.6 1.5 %collective-permute-start.14 = (bf16[384,768]{1,0:T(8,128)(2,1)S(1)}, bf16[384,768]{1,0:T(8,128)(2,1)S(1)}, u32[]{:S(2)}, u32[]{:S(2)}) collective-permute-start(bf16[384,768]{1,0:T(8,128)(2,1)S(1)} %collective-permute-done.10.refs_8_), channel_id=1, source_target_pairs={{0,2},{1,5},{2,6},{3,1},{6,10},{7,3},{10,14},{11,7},{14,12},{15,11... | collective-permute-start | bytes 1769480 | tf_op jit(solution)/shard_map/ppermute | solution.py:648
  56.1 1.8 %collective-permute-done.6.block.refs_7_ = bf16[384,640]{1,0:T(8,128)(2,1)S(1)} collective-permute-done((bf16[384,640]{1,0:T(8,128)(2,1)S(1)}, bf16[384,640]{1,0:T(8,128)(2,1)S(1)}, u32[]{:S(2)}, u32[]{:S(2)}) %collective-permute-start.6) | collective-permute-done | bytes 491552 | tf_op jit(solution)/shard_map/ppermute | solution.py:641
  58.6 2.0 %collective-permute-start.7 = (bf16[384,640]{1,0:T(8,128)(2,1)S(1)}, bf16[384,640]{1,0:T(8,128)(2,1)S(1)}, u32[]{:S(2)}, u32[]{:S(2)}) collective-permute-start(bf16[384,640]{1,0:T(8,128)(2,1)S(1)} %shard_map.144), channel_id=1, source_target_pairs={{0,2},{1,5},{2,6},{3,1},{6,10},{7,3},{10,14},{11,7},{14,12},{15,11... | collective-permute-start | bytes 1474568 | tf_op jit(solution)/shard_map/ppermute | solution.py:641
  61.2 1.8 %collective-permute-start.16 = (bf16[192,896]{1,0:T(8,128)(2,1)S(1)}, bf16[192,896]{1,0:T(8,128)(2,1)S(1)}, u32[]{:S(2)}, u32[]{:S(2)}) collective-permute-start(bf16[192,896]{1,0:T(8,128)(2,1)S(1)} %shard_map.148), channel_id=1, source_target_pairs={{0,2},{1,5},{2,6},{3,1},{6,10},{7,3},{10,14},{11,7},{14,12},{15,11... | collective-permute-start | bytes 1032200 | tf_op jit(solution)/shard_map/ppermute | solution.py:635
  63.0 4.9 %shard_map.146 = (f32[256,3072]{1,0:T(8,128)S(1)}, f32[256,3072]{1,0:T(8,128)S(1)}, f32[256,384]{1,0:T(8,128)S(1)}, f32[256,384]{1,0:T(8,128)S(1)}, bf16[256,307...) custom-call(s32[14]{0:T(128)S(1)} %dynamic-slice_bitcast_fusion.place.r, ...), custom_call_target="tpu_custom_call", output_to_operand_aliasing={{0}: (12, {}), {1}: (13, {}), {4}: (14, {})} | custom-call | bytes 1 | tf_op jit(solution)/shard_map/pallas_call | solution.py:91
  67.9 1.8 %collective-permute-done.7.block.refs_7_ = bf16[384,640]{1,0:T(8,128)(2,1)S(1)} collective-permute-done((bf16[384,640]{1,0:T(8,128)(2,1)S(1)}, bf16[384,640]{1,0:T(8,128)(2,1)S(1)}, u32[]{:S(2)}, u32[]{:S(2)}) %collective-permute-start.7) | collective-permute-done | bytes 491552 | tf_op jit(solution)/shard_map/ppermute | solution.py:641
  69.8 5.2 %shard_map.149 = (f32[256,3072]{1,0:T(8,128)S(1)}, bf16[256,4224]{1,0:T(8,128)(2,1)S(1)}, f32[256,384]{1,0:T(8,128)S(1)}, bf16[256,3072]{1,0:T(8,128)(2,1)}) custom-call(s32[14]{0:T(128)S(1)} %dynamic-slice_bitcast_fusion.place.refs_0_, bf16[256,3072]{1,0:T(8,128)(2,1)S(1)} %copy-done, ...), custom_call_target="tpu_custom_call", output_to_operand_aliasing={{0}: (13, {}), {3}: (15, {})} | custom-call | bytes 1 | tf_op jit(solution)/shard_map/pallas_call | solution.py:91
  75.7 1.8 %collective-permute-start.15 = (bf16[192,1536]{1,0:T(8,128)(2,1)S(1)}, bf16[192,1536]{1,0:T(8,128)(2,1)S(1)}, u32[]{:S(2)}, u32[]{:S(2)}) collective-permute-start(bf16[192,1536]{1,0:T(8,128)(2,1)S(1)} %shard_map.147), channel_id=1, source_target_pairs={{0,2},{1,5},{2,6},{3,1},{6,10},{7,3},{10,14},{11,7},{14,12},{15,11... | collective-permute-start | bytes 1769480 | tf_op jit(solution)/shard_map/ppermute | solution.py:646
  77.7 1.5 %collective-permute-start.22 = (bf16[192,896]{1,0:T(8,128)(2,1)S(1)}, bf16[192,896]{1,0:T(8,128)(2,1)S(1)}, u32[]{:S(2)}, u32[]{:S(2)}) collective-permute-start(bf16[192,896]{1,0:T(8,128)(2,1)S(1)} %collective-permute-done.16.refs_12_), channel_id=1, source_target_pairs={{0,16},{16,0},{1,17},{17,1},{2,18},{18,2},{3,19},{19,3},{4,20},{20... | collective-permute-start | bytes 1032200 | tf_op jit(solution)/shard_map/ppermute | solution.py:653
  79.2 6.4 %collective-permute-done.15.block.refs_14_.refs_16_ = bf16[192,1536]{1,0:T(8,128)(2,1)S(1)} collective-permute-done((bf16[192,1536]{1,0:T(8,128)(2,1)S(1)}, bf16[192,1536]{1,0:T(8,128)(2,1)S(1)}, u32[]{:S(2)}, u32[]{:S(2)}) %collective-permute-start.15) | collective-permute-done | bytes 589856 | tf_op jit(solution)/shard_map/ppermute | solution.py:646
  86.1 1.8 %collective-permute-done.22.refs_8_ = bf16[192,896]{1,0:T(8,128)(2,1)S(1)} collective-permute-done((bf16[192,896]{1,0:T(8,128)(2,1)S(1)}, bf16[192,896]{1,0:T(8,128)(2,1)S(1)}, u32[]{:S(2)}, u32[]{:S(2)}) %collective-permute-start.22) | collective-permute-done | bytes 344096 | tf_op jit(solution)/shard_map/ppermute | solution.py:653
  87.9 1.3 %shard_map.150 = (f32[64,192]{1,0:T(8,128)}, f32[64,192]{1,0:T(8,128)}) custom-call(s32[14]{0:T(128)S(1)} %dynamic-slice_bitcast_fusion.place.refs_0_, f32[8,384,128]{2,1,0:T(8,128)S(1)} %get-tuple-element.64.terms, bf16[8,384,128]{2,1,0:T(8,128)(2,1)S(1)} %collective-permute-done.theirs, ...), custom_call_target="tpu_custom_call" | custom-call | bytes 1 | tf_op jit(solution)/shard_map/pallas_call | solution.py:91
  89.2 5.3 %shard_map.151 = (f32[256,3072]{1,0:T(8,128)S(1)}, bf16[256,3072]{1,0:T(8,128)(2,1)}, bf16[256,3072]{1,0:T(8,128)(2,1)}, f32[256,384]{1,0:T(8,128)S(1)}) custom-call(s32[14]{0:T(128)S(1)} %dynamic-slice_bitcast_fusion.place.refs_0_, bf16[256,3072]{1,0:T(8,128)(2,1)S(1)} %copy-done, ...), custom_call_target="tpu_custom_call", output_to_operand_aliasing={{0}: (7, {}), {2}: (8, {})} | custom-call | bytes 12 | tf_op jit(solution)/shard_map/pallas_call | solution.py:91
  94.6 2.7 %shard_map.152 = (bf16[256,3072]{1,0:T(8,128)(2,1)}, bf16[256,3072]{1,0:T(8,128)(2,1)}) custom-call(s32[14]{0:T(128)S(1)} %dynamic-slice_bitcast_fusion.place.refs_0_, bf16[256,3072]{1,0:T(8,128)(2,1)S(1)} %copy-done, bf16[256,3200]{1,0:T(8,128)(2,1)S(1)} %get-tuple-element.109.refs_2_, ...), custom_call_target="tpu_custom_call", output_to_operand_aliasing={{0}: (6, {}), {1}: (7, {})} | custom-call | bytes 12 | tf_op jit(solution)/shard_map/pallas_call | solution.py:91
  (48 shorter events, 10.5 us)
Async XLA Ops:
  0.6 3.2 %collective-permute-start.1 = (bf16[192,3072]{1,0:T(8,128)(2,1)}, bf16[192,3072]{1,0:T(8,128)(2,1)S(1)}, u32[]{:S(2)}, u32[]{:S(2)}) collective-permute-start(bf16[192,3072]{1,0:T(8,128)(2,1)} %frozen.1), channel_id=1, source_target_pairs={{0,1},{1,0},{2,3},{3,2},{4,5},{5,4},{6,7},{7,6},{8,9},{9,8},{10,11... | collective-permute-start | bytes 3538952 | tf_op jit(solution)/shard_map/ppermute | solution.py:600
  1.8 1.3 %copy-start.3 = (bf16[192,3072]{1,0:T(8,128)(2,1)S(1)}, bf16[192,3072]{1,0:T(8,128)(2,1)}, u32[]{:S(2)}) copy-start(bf16[192,3072]{1,0:T(8,128)(2,1)} %frozen.1) | copy-start | bytes 3538948
  3.1 7.3 %copy-start = (bf16[256,3072]{1,0:T(8,128)(2,1)S(1)}, bf16[256,3072]{1,0:T(8,128)(2,1)}, u32[]{:S(2)}) copy-start(bf16[256,3072]{1,0:T(8,128)(2,1)} %refs_1_.11) | copy-start | bytes 4718596
  3.1 7.3 %copy-start.2 = (bf16[256,3072]{1,0:T(8,128)(2,1)S(1)}, bf16[256,3072]{1,0:T(8,128)(2,1)}, u32[]{:S(2)}) copy-start(bf16[256,3072]{1,0:T(8,128)(2,1)} %cotangent.1) | copy-start | bytes 4718596
  3.1 7.3 %copy-start.7 = (f32[16,3072]{1,0:T(8,128)S(1)}, f32[16,3072]{1,0:T(8,128)}, u32[]{:S(2)}) copy-start(f32[16,3072]{1,0:T(8,128)} %g_gate.1) | copy-start | bytes 589828
  4.6 11.7 %collective-permute-start.4 = (bf16[384,768]{1,0:T(8,128)(2,1)S(1)}, bf16[384,768]{1,0:T(8,128)(2,1)S(1)}, u32[]{:S(2)}, u32[]{:S(2)}) collective-permute-start(bf16[384,768]{1,0:T(8,128)(2,1)S(1)} %get-tuple-element.72.refs_8_), channel_id=1, source_target_pairs={{0,2},{1,5},{2,6},{3,1},{6,10},{7,3},{10,14},{11,7},{14,12},{15,11... | collective-permute-start | bytes 1769480 | tf_op jit(solution)/shard_map/ppermute | solution.py:602
  7.5 15.3 %collective-permute-start.3 = (bf16[384,896]{1,0:T(8,128)(2,1)S(1)}, bf16[384,896]{1,0:T(8,128)(2,1)S(1)}, u32[]{:S(2)}, u32[]{:S(2)}) collective-permute-start(bf16[384,896]{1,0:T(8,128)(2,1)S(1)} %get-tuple-element.71.refs_6_), channel_id=1, source_target_pairs={{0,2},{1,5},{2,6},{3,1},{6,10},{7,3},{10,14},{11,7},{14,12},{15,11... | collective-permute-start | bytes 2064392 | tf_op jit(solution)/shard_map/ppermute | solution.py:602
  10.4 1.1 %copy-start.4 = (f32[3072,64]{0,1:T(8,128)S(1)}, f32[3072,64]{0,1:T(8,128)}, u32[]{:S(2)}) copy-start(f32[3072,64]{0,1:T(8,128)} %param.14) | copy-start | bytes 2359300
  11.5 1.1 %copy-start.5 = (f32[64,3072]{1,0:T(8,128)S(1)}, f32[64,3072]{1,0:T(8,128)}, u32[]{:S(2)}) copy-start(f32[64,3072]{1,0:T(8,128)} %up.1) | copy-start | bytes 2359300
  12.7 1.1 %copy-start.6 = (f32[50,3072]{1,0:T(8,128)S(1)}, f32[50,3072]{1,0:T(8,128)}, u32[]{:S(2)}) copy-start(f32[50,3072]{1,0:T(8,128)} %t_gate.1) | copy-start | bytes 1843204
  16.3 24.6 %collective-permute-start.5 = (bf16[256,3200]{1,0:T(8,128)(2,1)S(1)}, bf16[256,3200]{1,0:T(8,128)(2,1)S(1)}, u32[]{:S(2)}, u32[]{:S(2)}) collective-permute-start(bf16[256,3200]{1,0:T(8,128)(2,1)S(1)} %get-tuple-element.109.refs_2_), channel_id=1, source_target_pairs={{0,1},{1,0},{2,3},{3,2},{4,5},{5,4},{6,7},{7,6},{8,9},{9,8},{10,11... | collective-permute-start | bytes 4915208 | tf_op jit(solution)/shard_map/ppermute | solution.py:613
  16.4 8.4 %collective-permute-start = (bf16[8,384,128]{2,1,0:T(8,128)(2,1)S(1)}, bf16[8,384,128]{2,1,0:T(8,128)(2,1)S(1)}, u32[]{:S(2)}, u32[]{:S(2)}) collective-permute-start(bf16[8,384,128]{2,1,0:T(8,128)(2,1)S(1)} %get-tuple-element.65), channel_id=1, source_target_pairs={{0,1},{1,0},{2,3},{3,2},{4,5},{5,4},{6,7},{7,6},{8,9},{9,8},{10,11... | collective-permute-start | bytes 2359304 | tf_op jit(solution)/shard_map/ppermute | solution.py:609
  16.9 26.3 %collective-permute-start.11 = (bf16[256,3072]{1,0:T(8,128)(2,1)S(1)}, bf16[256,3072]{1,0:T(8,128)(2,1)S(1)}, u32[]{:S(2)}, u32[]{:S(2)}) collective-permute-start(bf16[256,3072]{1,0:T(8,128)(2,1)S(1)} %copy-done), channel_id=1, source_target_pairs={{0,1},{1,0},{2,3},{3,2},{4,5},{5,4},{6,7},{7,6},{8,9},{9,8},{10,11... | collective-permute-start | bytes 4718600 | tf_op jit(solution)/shard_map/ppermute | solution.py:604
  22.8 10.9 %collective-permute-start.8 = (bf16[384,896]{1,0:T(8,128)(2,1)S(1)}, bf16[384,896]{1,0:T(8,128)(2,1)S(1)}, u32[]{:S(2)}, u32[]{:S(2)}) collective-permute-start(bf16[384,896]{1,0:T(8,128)(2,1)S(1)} %collective-permute-done.3.refs_6_), channel_id=1, source_target_pairs={{0,2},{1,5},{2,6},{3,1},{6,10},{7,3},{10,14},{11,7},{14,12},{15,11... | collective-permute-start | bytes 2064392 | tf_op jit(solution)/shard_map/ppermute | solution.py:635
  25.3 13.6 %collective-permute-start.2 = (bf16[384,640]{1,0:T(8,128)(2,1)S(1)}, bf16[384,640]{1,0:T(8,128)(2,1)S(1)}, u32[]{:S(2)}, u32[]{:S(2)}) collective-permute-start(bf16[384,640]{1,0:T(8,128)(2,1)S(1)} %shard_map.141), channel_id=1, source_target_pairs={{0,2},{1,5},{2,6},{3,1},{6,10},{7,3},{10,14},{11,7},{14,12},{15,11... | collective-permute-start | bytes 1474568 | tf_op jit(solution)/shard_map/ppermute | solution.py:611
  27.0 25.7 %collective-permute-start.12 = (bf16[384,896]{1,0:T(8,128)(2,1)S(1)}, bf16[384,896]{1,0:T(8,128)(2,1)S(1)}, u32[]{:S(2)}, u32[]{:S(2)}) collective-permute-start(bf16[384,896]{1,0:T(8,128)(2,1)S(1)} %collective-permute-done.3.refs_6_), channel_id=1, source_target_pairs={{0,16},{16,0},{1,17},{17,1},{2,18},{18,2},{3,19},{19,3},{4,20},{20... | collective-permute-start | bytes 2064392 | tf_op jit(solution)/shard_map/ppermute | solution.py:636
  33.7 19.0 %collective-permute-start.9 = (bf16[384,896]{1,0:T(8,128)(2,1)S(1)}, bf16[384,896]{1,0:T(8,128)(2,1)S(1)}, u32[]{:S(2)}, u32[]{:S(2)}) collective-permute-start(bf16[384,896]{1,0:T(8,128)(2,1)S(1)} %collective-permute-done.8.refs_6_), channel_id=1, source_target_pairs={{0,2},{1,5},{2,6},{3,1},{6,10},{7,3},{10,14},{11,7},{14,12},{15,11... | collective-permute-start | bytes 2064392 | tf_op jit(solution)/shard_map/ppermute | solution.py:635
  39.0 13.7 %collective-permute-start.10 = (bf16[384,768]{1,0:T(8,128)(2,1)S(1)}, bf16[384,768]{1,0:T(8,128)(2,1)S(1)}, u32[]{:S(2)}, u32[]{:S(2)}) collective-permute-start(bf16[384,768]{1,0:T(8,128)(2,1)S(1)} %collective-permute-done.4.refs_8_), channel_id=1, source_target_pairs={{0,2},{1,5},{2,6},{3,1},{6,10},{7,3},{10,14},{11,7},{14,12},{15,11... | collective-permute-start | bytes 1769480 | tf_op jit(solution)/shard_map/ppermute | solution.py:648
  41.6 16.4 %collective-permute-start.6 = (bf16[384,640]{1,0:T(8,128)(2,1)S(1)}, bf16[384,640]{1,0:T(8,128)(2,1)S(1)}, u32[]{:S(2)}, u32[]{:S(2)}) collective-permute-start(bf16[384,640]{1,0:T(8,128)(2,1)S(1)} %shard_map.143), channel_id=1, source_target_pairs={{0,2},{1,5},{2,6},{3,1},{6,10},{7,3},{10,14},{11,7},{14,12},{15,11... | collective-permute-start | bytes 1474568 | tf_op jit(solution)/shard_map/ppermute | solution.py:641
  43.2 19.8 %collective-permute-start.13 = (bf16[384,896]{1,0:T(8,128)(2,1)S(1)}, bf16[384,896]{1,0:T(8,128)(2,1)S(1)}, u32[]{:S(2)}, u32[]{:S(2)}) collective-permute-start(bf16[384,896]{1,0:T(8,128)(2,1)S(1)} %collective-permute-done.8.refs_6_), channel_id=1, source_target_pairs={{0,16},{16,0},{1,17},{17,1},{2,18},{18,2},{3,19},{19,3},{4,20},{20... | collective-permute-start | bytes 2064392 | tf_op jit(solution)/shard_map/ppermute | solution.py:636
  52.7 22.3 %collective-permute-start.17 = (bf16[384,896]{1,0:T(8,128)(2,1)S(1)}, bf16[384,896]{1,0:T(8,128)(2,1)S(1)}, u32[]{:S(2)}, u32[]{:S(2)}) collective-permute-start(bf16[384,896]{1,0:T(8,128)(2,1)S(1)} %collective-permute-done.9.whole.refs_6_), channel_id=1, source_target_pairs={{0,16},{16,0},{1,17},{17,1},{2,18},{18,2},{3,19},{19,3},{4,20},{20... | collective-permute-start | bytes 2064392 | tf_op jit(solution)/shard_map/ppermute | solution.py:636
  54.6 13.3 %collective-permute-start.14 = (bf16[384,768]{1,0:T(8,128)(2,1)S(1)}, bf16[384,768]{1,0:T(8,128)(2,1)S(1)}, u32[]{:S(2)}, u32[]{:S(2)}) collective-permute-start(bf16[384,768]{1,0:T(8,128)(2,1)S(1)} %collective-permute-done.10.refs_8_), channel_id=1, source_target_pairs={{0,2},{1,5},{2,6},{3,1},{6,10},{7,3},{10,14},{11,7},{14,12},{15,11... | collective-permute-start | bytes 1769480 | tf_op jit(solution)/shard_map/ppermute | solution.py:648
  58.6 11.2 %collective-permute-start.7 = (bf16[384,640]{1,0:T(8,128)(2,1)S(1)}, bf16[384,640]{1,0:T(8,128)(2,1)S(1)}, u32[]{:S(2)}, u32[]{:S(2)}) collective-permute-start(bf16[384,640]{1,0:T(8,128)(2,1)S(1)} %shard_map.144), channel_id=1, source_target_pairs={{0,2},{1,5},{2,6},{3,1},{6,10},{7,3},{10,14},{11,7},{14,12},{15,11... | collective-permute-start | bytes 1474568 | tf_op jit(solution)/shard_map/ppermute | solution.py:641
  61.2 13.8 %collective-permute-start.16 = (bf16[192,896]{1,0:T(8,128)(2,1)S(1)}, bf16[192,896]{1,0:T(8,128)(2,1)S(1)}, u32[]{:S(2)}, u32[]{:S(2)}) collective-permute-start(bf16[192,896]{1,0:T(8,128)(2,1)S(1)} %shard_map.148), channel_id=1, source_target_pairs={{0,2},{1,5},{2,6},{3,1},{6,10},{7,3},{10,14},{11,7},{14,12},{15,11... | collective-permute-start | bytes 1032200 | tf_op jit(solution)/shard_map/ppermute | solution.py:635
  75.0 10.7 %collective-permute-start.18 = (bf16[256,4224]{1,0:T(8,128)(2,1)S(1)}, bf16[256,4224]{1,0:T(8,128)(2,1)S(1)}, u32[]{:S(2)}, u32[]{:S(2)}) collective-permute-start(bf16[256,4224]{1,0:T(8,128)(2,1)S(1)} %get-tuple-element.106), channel_id=1, source_target_pairs={{0,1},{1,0},{2,3},{3,2},{4,5},{5,4},{6,7},{7,6},{8,9},{9,8},{10,11... | collective-permute-start | bytes 6488072 | tf_op jit(solution)/shard_map/ppermute | solution.py:662
  75.7 13.6 %copy-start.1 = (bf16[256,3072]{1,0:T(8,128)(2,1)S(1)}, bf16[256,3072]{1,0:T(8,128)(2,1)}, u32[]{:S(2)}) copy-start(bf16[256,3072]{1,0:T(8,128)(2,1)} %refs_3_.1) | copy-start | bytes 4718596
  75.7 9.9 %collective-permute-start.15 = (bf16[192,1536]{1,0:T(8,128)(2,1)S(1)}, bf16[192,1536]{1,0:T(8,128)(2,1)S(1)}, u32[]{:S(2)}, u32[]{:S(2)}) collective-permute-start(bf16[192,1536]{1,0:T(8,128)(2,1)S(1)} %shard_map.147), channel_id=1, source_target_pairs={{0,2},{1,5},{2,6},{3,1},{6,10},{7,3},{10,14},{11,7},{14,12},{15,11... | collective-permute-start | bytes 1769480 | tf_op jit(solution)/shard_map/ppermute | solution.py:646
  77.4 11.8 %collective-permute-start.20 = (bf16[384,896]{1,0:T(8,128)(2,1)S(1)}, bf16[384,896]{1,0:T(8,128)(2,1)S(1)}, u32[]{:S(2)}, u32[]{:S(2)}) collective-permute-start(bf16[384,896]{1,0:T(8,128)(2,1)S(1)} %collective-permute-done.17.refs_9_), channel_id=1, source_target_pairs={{0,1},{1,0},{2,3},{3,2},{4,5},{5,4},{6,7},{7,6},{8,9},{9,8},{10,11... | collective-permute-start | bytes 2064392 | tf_op jit(solution)/shard_map/ppermute | solution.py:657
  77.7 10.2 %collective-permute-start.22 = (bf16[192,896]{1,0:T(8,128)(2,1)S(1)}, bf16[192,896]{1,0:T(8,128)(2,1)S(1)}, u32[]{:S(2)}, u32[]{:S(2)}) collective-permute-start(bf16[192,896]{1,0:T(8,128)(2,1)S(1)} %collective-permute-done.16.refs_12_), channel_id=1, source_target_pairs={{0,16},{16,0},{1,17},{17,1},{2,18},{18,2},{3,19},{19,3},{4,20},{20... | collective-permute-start | bytes 1032200 | tf_op jit(solution)/shard_map/ppermute | solution.py:653
  85.6 2.3 %collective-permute-start.19 = (bf16[192,1536]{1,0:T(8,128)(2,1)S(1)}, bf16[192,1536]{1,0:T(8,128)(2,1)S(1)}, u32[]{:S(2)}, u32[]{:S(2)}) collective-permute-start(bf16[192,1536]{1,0:T(8,128)(2,1)S(1)} %collective-permute-done.15.block.refs_14_.refs_16_), channel_id=1, source_target_pairs={{0,1},{1,0},{2,3},{3,2},{4,5},{5,4},{6,7},{7,6},{8,9},{9,8},{10,11... | collective-permute-start | bytes 1769480 | tf_op jit(solution)/shard_map/ppermute | solution.py:663
  85.6 3.6 %collective-permute-start.21 = (bf16[192,896]{1,0:T(8,128)(2,1)S(1)}, bf16[192,896]{1,0:T(8,128)(2,1)S(1)}, u32[]{:S(2)}, u32[]{:S(2)}) collective-permute-start(bf16[192,896]{1,0:T(8,128)(2,1)S(1)} %collective-permute-done.16.refs_12_), channel_id=1, source_target_pairs={{0,1},{1,0},{2,3},{3,2},{4,5},{5,4},{6,7},{7,6},{8,9},{9,8},{10,11... | collective-permute-start | bytes 1032200 | tf_op jit(solution)/shard_map/ppermute | solution.py:657
  87.9 6.6 %collective-permute-start.23 = (bf16[192,896]{1,0:T(8,128)(2,1)S(1)}, bf16[192,896]{1,0:T(8,128)(2,1)S(1)}, u32[]{:S(2)}, u32[]{:S(2)}) collective-permute-start(bf16[192,896]{1,0:T(8,128)(2,1)S(1)} %collective-permute-done.22.refs_8_), channel_id=1, source_target_pairs={{0,1},{1,0},{2,3},{3,2},{4,5},{5,4},{6,7},{7,6},{8,9},{9,8},{10,11... | collective-permute-start | bytes 1032200 | tf_op jit(solution)/shard_map/ppermute | solution.py:675

commit v3 on v2

--- a/solution.py
+++ b/solution.py
@@ -232,24 +232,6 @@
         kernel, (place, block, second, terms, theirs), [SMEM_SPEC] + [VMEM_SPEC] * 4,
         jax.ShapeDtypeStruct((shard, width + more + 2 * lanes), BF16), VMEM_SPEC, limit=8,
     )
-
-
-def finish(place, slot, terms, theirs, block, block_theirs, width, scale):
-    _, span, lanes = terms.shape
-    shard = span // 2
-
-    def kernel(place, terms, theirs, block, block_theirs, first, second):
-        chip = lax.div(place[slot], span)
-        mine, rest = half_rows(place[0], shard), cols(width + place[0] * lanes, lanes)
-        value = terms[chip, mine, :] + theirs[chip, mine, :].astype(F32)
-        value = value + block[:, rest].astype(F32) + block_theirs[:, rest].astype(F32)
-        value = (scale * value).T
-        first[...] = value[: lanes // 2]
-        second[...] = value[lanes // 2 :]
-
-    shape = jax.ShapeDtypeStruct((lanes // 2, shard), F32)
-    args = (place, terms, theirs, block, block_theirs)
-    return call(kernel, args, [SMEM_SPEC] + [VMEM_SPEC] * (len(args) - 1), [shape] * 2, [VMEM_SPEC] * 2, limit=8)
 
 
 def side_step(place, distance, attn, gout, mates, down_t, rank, blocks, ring_blocks, x_block, totals, parts, grad_attn, gives, last):
@@ -372,7 +354,7 @@
     )
 
 
-def step(place, jobs, attn, blocks, grads, total=None, add=None, final=None, updated=None, grad_attn=None, extra=None):
+def step(place, jobs, attn, blocks, grads, total=None, add=None, final=None, updated=None, grad_attn=None, extra=None, sums=None):
     rows, features = attn.shape
     gout, down_t, rank = grads
     place_span = span_of(jobs)
@@ -414,6 +396,12 @@
         produce("updated", (rows, features), BF16, HBM_SPEC, updated)
     if not all(job["open"] for job in jobs):
         produce("grad", (rows, features), BF16, HBM_SPEC, grad_attn)
+    if sums is not None:
+        for n, array in enumerate(sums[:4]):
+            give(("sums", n), array)
+        lanes = sums[0].shape[2]
+        for n in range(2):
+            produce(("sums", n), (lanes // 2, span_of(jobs) // 2), F32, VMEM_SPEC)
     scratch = []
     tiny = pltpu.VMEM((16, 128), BF16)
     for j, job in enumerate(jobs):
@@ -509,6 +497,15 @@
                 else:
                     back_v[:, mine] = value.astype(BF16)
                     put(back_v.at[:, mine], ref[("out", "grad")].at[:, at])
+        if sums is not None:
+            span = jobs[0]["span"]
+            chip, mine = lax.div(place[OWN], span), half_rows(place[0], span // 2)
+            rest = cols(sums[4] + place[0] * lanes, lanes)
+            value = ref[("sums", 0)][chip, mine, :] + ref[("sums", 1)][chip, mine, :].astype(F32)
+            value = value + ref[("sums", 2)][:, rest].astype(F32) + ref[("sums", 3)][:, rest].astype(F32)
+            value = (sums[5] * value).T
+            ref[("out", ("sums", 0))][...] = value[: lanes // 2]
+            ref[("out", ("sums", 1))][...] = value[lanes // 2 :]
         for copy in stores:
             copy.wait()
 
@@ -518,6 +515,8 @@
     )
     result = dict(zip(out_names, result))
     opened = [result[("open", j)] for j, job in enumerate(jobs) if job["open"]]
+    if sums is not None:
+        opened += [result[("sums", n)] for n in range(2)]
     return result.get("total", total), result.get("updated", updated), result.get("grad", grad_attn), *opened
 
 
@@ -638,42 +637,44 @@
             run(n - 1, r[n], x=x[n - 1], X=x[n - 2])
         q[n] = gate(f"q{n}", q[n], **{**known, "r": r[n], "T": totals[0], "x": x[n - 1]})
         if not last:
-            q.append(ring(chunk(place, across(steps + 1 - n), q[n], wide, terms, terms_t, "middle")))
+            message = chunk(place, across(steps + 1 - n), q[n], wide, terms, terms_t, "middle")
+            q.append(ring(message))
         if n > 1 and WHEN[n - 2] == "q":
-            run(n - 1, q[n], x=x[n - 1], X=x[n - 2])
+            run(n - 1, q[n], x=x[n - 1], X=x[n - 2], c=message)
         s[n] = gate(f"s{n}", s[n], **{**known, "q": q[n], "r": r[n], "T": totals[0], "x": x[n - 1]})
         if last:
-            q.append(ring(last_chunk(place, across(1), q[n], s[n], wide, terms, terms_t)))
+            message = last_chunk(place, across(1), q[n], s[n], wide, terms, terms_t)
+            q.append(ring(message))
         else:
             s.append(ring(s[n]))
         if WHEN[n - 1] == "s":
-            run(n, s[n], x=x[n - 1])
+            run(n, s[n], x=x[n - 1], c=message)
 
     r_far = gate("r4", r[steps + 1], X=x[steps], T=totals[0], s=s[steps], q=q[steps])
     x_far = cross(gate("x4", r_far, X=x[steps], T=totals[0], s=s[steps]))
     if WHEN[steps - 1] == "r":
-        run(steps, r_far, X=x[steps])
+        run(steps, r_far, X=x[steps], c=message)
     x_before = gate("back", x[steps], r=r_far)
     x_swapped, r_swapped = swap(x_before), swap(r_far)
     swaps = dict(v=x_swapped, w=r_swapped)
     q_far = gate("q4", q[steps + 1], r=r_far, T=totals[0], **swaps)
     if WHEN[steps - 1] == "q":
-        run(steps, q_far, X=x[steps])
+        run(steps, q_far, X=x[steps], c=message)
     extra = swap(gate("send", give, r=r_far, X=x[steps], q=q_far))
     q_swapped = swap(gate("q5", q_far, e=extra, **swaps))
-    grad_scale = float(rows * axis_size) ** (-0.5)
-    grad_down_t, grad_up = finish(place, OWN, terms, terms_t, q_far, q_swapped, wide + blocks[2], grad_scale)
     x_job = job([near(steps), across(steps)], [3], [[x_before, x_swapped]], part=[parts[0], None])
-    s_piece = (Part(q_far, 0, wide), Part(q_swapped, 0, wide))
-    far_job = job([far], [0, 1, 2], [[(r_far, r_swapped)], [(q_far, q_swapped)], [s_piece]], open=True, final=True)
+    q_piece, s_piece = (q_far, q_swapped), (Part(q_far, 0, wide), Part(q_swapped, 0, wide))
+    columns = [across(n) for n in range(1, steps)]
+    far_job = job([far], [0, 1, 2], [[(r_far, r_swapped)], [q_piece], [s_piece]], open=True, final=True)
     total, updated, grad_attn, part = step(
-        place, [x_job, far_job], attn, blocks, (after(gout, grad_down_t), down_t, rank), total=totals[0],
-        final=(resid, gate_row), grad_attn=grad_attn, extra=(extra, [across(n) for n in range(1, steps)]),
+        place, [x_job, far_job], attn, blocks, grads, total=totals[0], final=(resid, gate_row), grad_attn=grad_attn,
+        extra=(extra, columns),
     )
     x_far = gate("x5", x_far, s=q_far, q=q_far, T=total)
-    _, updated, grad_attn = step(
+    sums = (terms, terms_t, q_far, q_swapped, wide + blocks[2], float(rows * axis_size) ** (-0.5))
+    _, updated, grad_attn, grad_down_t, grad_up = step(
         place, [job([far], [3], [[(x_far, swap(x_far))]], part=[part], final=True)],
-        attn, blocks, grads, total=total, final=(resid, gate_row), updated=updated, grad_attn=grad_attn,
+        attn, blocks, grads, total=total, final=(resid, gate_row), updated=updated, grad_attn=grad_attn, sums=sums,
     )
     return updated, grad_attn, grad_down_t.T, grad_up.T
 

time: 97.8 us -> 97.3 us (level)
    pallas_call x15 -> x14, Pallas kernels: 33.5 us -> 32.8 us  [call(): pl.pallas_call(kernel, in_specs=specs, out_shape=out_shape, out_specs=out...]
  transfers between devices with their start and end apart: 24 -> 24, of which waited for: 8 -> 9; matrix products, arithmetic and copies ran while one was open for 1% -> 1% of each run, Pallas kernels for 31% -> 30%
where the time goes in v3:
time: 97.3 us; the launch traced here: 97 us
  Pallas kernels  32.8 us (34%)
  starting transfers between devices  29.2 us (30%)
  waiting for transfers between devices  27.3 us (28%)
  local copies, waits for them, and re-layouts  5.34 us (5%)
  between operations  2.31 us (2%)
    pallas_call x14, Pallas kernels, call(): pl.pallas_call(kernel, in_specs=specs, out_shape=out_shape, out_specs=out...  32.8 us
    ppermute x3, waiting for transfers between devices, ring_body(): q.append(ring(message))  10 us
    ppermute x3, starting transfers between devices, ring_body(): r.append(ring(own_half(place, r[n]) if last else r[n]))  5.74 us
    ppermute x3, starting transfers between devices, ring_body(): q.append(ring(message))  5.42 us
    ppermute x3, waiting for transfers between devices, ring_body(): r.append(ring(own_half(place, r[n]) if last else r[n]))  5.26 us
    ppermute x3, starting transfers between devices, ring_body(): x.append(cross(gate(f'x{n}', r[n], **prev)))  4.92 us
    unnamed x16, local copies, waits for them, and re-layouts  4.65 us
    ppermute x2, waiting for transfers between devices, ring_body(): s.append(ring(s[n]))  4.57 us
  transfers between devices with their start and end apart: 24, of which 9 were waited for; matrix products, arithmetic and copies ran while one was open for 1% of the time, Pallas kernels for 30%

profile of v3, /device:TPU:0, one launch (start us, length us, event | category | flops | bytes accessed | tf_op | source)
XLA Modules:
  0.0 97.0 jit_solution(15794911325267878240)
XLA Ops:
  1.8 1.3 %copy-done.3 = bf16[192,3072]{1,0:T(8,128)(2,1)S(1)} copy-done((bf16[192,3072]{1,0:T(8,128)(2,1)S(1)}, bf16[192,3072]{1,0:T(8,128)(2,1)}, u32[]{:S(2)}) %copy-start.3) | copy-done | bytes 1179672
  4.6 2.9 %collective-permute-start.1 = (bf16[384,768]{1,0:T(8,128)(2,1)S(1)}, bf16[384,768]{1,0:T(8,128)(2,1)S(1)}, u32[]{:S(2)}, u32[]{:S(2)}) collective-permute-start(bf16[384,768]{1,0:T(8,128)(2,1)S(1)} %get-tuple-element.68.refs_8_), channel_id=1, source_target_pairs={{0,2},{1,5},{2,6},{3,1},{6,10},{7,3},{10,14},{11,7},{14,12},{15,11... | collective-permute-start | bytes 1769480 | tf_op jit(solution)/shard_map/ppermute | solution.py:601
  7.5 1.6 %collective-permute-start.5 = (bf16[384,896]{1,0:T(8,128)(2,1)S(1)}, bf16[384,896]{1,0:T(8,128)(2,1)S(1)}, u32[]{:S(2)}, u32[]{:S(2)}) collective-permute-start(bf16[384,896]{1,0:T(8,128)(2,1)S(1)} %get-tuple-element.70.refs_6_), channel_id=1, source_target_pairs={{0,2},{1,5},{2,6},{3,1},{6,10},{7,3},{10,14},{11,7},{14,12},{15,11... | collective-permute-start | bytes 2064392 | tf_op jit(solution)/shard_map/ppermute | solution.py:601
  11.5 1.1 %copy-done.5 = f32[64,3072]{1,0:T(8,128)S(1)} copy-done((f32[64,3072]{1,0:T(8,128)S(1)}, f32[64,3072]{1,0:T(8,128)}, u32[]{:S(2)}) %copy-start.5) | copy-done | bytes 786456
  13.8 2.5 %shard_map.138 = (f32[1,3072]{1,0:T(1,128)S(1)}, bf16[256,3200]{1,0:T(8,128)(2,1)S(1)}, bf16[256,64]{1,0:T(8,128)(2,1)S(1)}, bf16[64,3072]{1,0:T(8,128)(2,1)S(1)...) custom-call(s32[14]{0:T(128)S(1)} %dynamic-slice_bitcast_fusion.place.refs_0_, ...), custom_call_target="tpu_custom_call" | custom-call | bytes 1 | tf_op jit(solution)/shard_map/pallas_call | solution.py:91
  17.0 3.7 %shard_map.141 = (f32[256,3072]{1,0:T(8,128)S(1)}, bf16[256,3072]{1,0:T(8,128)(2,1)}) custom-call(s32[14]{0:T(128)S(1)} %dynamic-slice_bitcast_fusion.place.refs_0_, bf16[256,3072]{1,0:T(8,128)(2,1)S(1)} %copy-done, bf16[256,3200]{1,0:T(8,128)(2,1)S(1)} %get-tuple-element.93.refs_2_, bf16[64,3072]{1,0:T(8,128)(2,1)S(1)} %get-tuple-element.63.refs_3_.refs_5_, ...), custom_call_target="tpu_custom_call" | custom-call | bytes 12 | tf_op jit(solution)/shard_map/pallas_call | solution.py:91
  20.7 2.1 %collective-permute-done.5.refs_6_ = bf16[384,896]{1,0:T(8,128)(2,1)S(1)} collective-permute-done((bf16[384,896]{1,0:T(8,128)(2,1)S(1)}, bf16[384,896]{1,0:T(8,128)(2,1)S(1)}, u32[]{:S(2)}, u32[]{:S(2)}) %collective-permute-start.5) | collective-permute-done | bytes 688160 | tf_op jit(solution)/shard_map/ppermute | solution.py:601
  22.8 2.0 %collective-permute-start.10 = (bf16[384,896]{1,0:T(8,128)(2,1)S(1)}, bf16[384,896]{1,0:T(8,128)(2,1)S(1)}, u32[]{:S(2)}, u32[]{:S(2)}) collective-permute-start(bf16[384,896]{1,0:T(8,128)(2,1)S(1)} %collective-permute-done.5.refs_6_), channel_id=1, source_target_pairs={{0,2},{1,5},{2,6},{3,1},{6,10},{7,3},{10,14},{11,7},{14,12},{15,11... | collective-permute-start | bytes 2064392 | tf_op jit(solution)/shard_map/ppermute | solution.py:634
  25.3 1.6 %collective-permute-start.7 = (bf16[384,640]{1,0:T(8,128)(2,1)S(1)}, bf16[384,640]{1,0:T(8,128)(2,1)S(1)}, u32[]{:S(2)}, u32[]{:S(2)}) collective-permute-start(bf16[384,640]{1,0:T(8,128)(2,1)S(1)} %shard_map.142), channel_id=1, source_target_pairs={{0,2},{1,5},{2,6},{3,1},{6,10},{7,3},{10,14},{11,7},{14,12},{15,11... | collective-permute-start | bytes 1474568 | tf_op jit(solution)/shard_map/ppermute | solution.py:610
  27.0 1.5 %collective-permute-start.8 = (bf16[384,896]{1,0:T(8,128)(2,1)S(1)}, bf16[384,896]{1,0:T(8,128)(2,1)S(1)}, u32[]{:S(2)}, u32[]{:S(2)}) collective-permute-start(bf16[384,896]{1,0:T(8,128)(2,1)S(1)} %collective-permute-done.5.refs_6_), channel_id=1, source_target_pairs={{0,16},{16,0},{1,17},{17,1},{2,18},{18,2},{3,19},{19,3},{4,20},{20... | collective-permute-start | bytes 2064392 | tf_op jit(solution)/shard_map/ppermute | solution.py:635
  28.5 5.3 %collective-permute-done.10.refs_6_ = bf16[384,896]{1,0:T(8,128)(2,1)S(1)} collective-permute-done((bf16[384,896]{1,0:T(8,128)(2,1)S(1)}, bf16[384,896]{1,0:T(8,128)(2,1)S(1)}, u32[]{:S(2)}, u32[]{:S(2)}) %collective-permute-start.10) | collective-permute-done | bytes 688160 | tf_op jit(solution)/shard_map/ppermute | solution.py:634
  33.7 2.0 %collective-permute-start.11 = (bf16[384,896]{1,0:T(8,128)(2,1)S(1)}, bf16[384,896]{1,0:T(8,128)(2,1)S(1)}, u32[]{:S(2)}, u32[]{:S(2)}) collective-permute-start(bf16[384,896]{1,0:T(8,128)(2,1)S(1)} %collective-permute-done.10.refs_6_), channel_id=1, source_target_pairs={{0,2},{1,5},{2,6},{3,1},{6,10},{7,3},{10,14},{11,7},{14,12},{15,11... | collective-permute-start | bytes 2064392 | tf_op jit(solution)/shard_map/ppermute | solution.py:634
  35.7 3.3 %collective-permute-done.7.refs_7_.block = bf16[384,640]{1,0:T(8,128)(2,1)S(1)} collective-permute-done((bf16[384,640]{1,0:T(8,128)(2,1)S(1)}, bf16[384,640]{1,0:T(8,128)(2,1)S(1)}, u32[]{:S(2)}, u32[]{:S(2)}) %collective-permute-start.7) | collective-permute-done | bytes 491552 | tf_op jit(solution)/shard_map/ppermute | solution.py:610
  39.0 2.0 %collective-permute-start.2 = (bf16[384,768]{1,0:T(8,128)(2,1)S(1)}, bf16[384,768]{1,0:T(8,128)(2,1)S(1)}, u32[]{:S(2)}, u32[]{:S(2)}) collective-permute-start(bf16[384,768]{1,0:T(8,128)(2,1)S(1)} %collective-permute-done.1.refs_8_), channel_id=1, source_target_pairs={{0,2},{1,5},{2,6},{3,1},{6,10},{7,3},{10,14},{11,7},{14,12},{15,11... | collective-permute-start | bytes 1769480 | tf_op jit(solution)/shard_map/ppermute | solution.py:649
  41.6 1.6 %collective-permute-start.13 = (bf16[384,640]{1,0:T(8,128)(2,1)S(1)}, bf16[384,640]{1,0:T(8,128)(2,1)S(1)}, u32[]{:S(2)}, u32[]{:S(2)}) collective-permute-start(bf16[384,640]{1,0:T(8,128)(2,1)S(1)} %shard_map.144), channel_id=1, source_target_pairs={{0,2},{1,5},{2,6},{3,1},{6,10},{7,3},{10,14},{11,7},{14,12},{15,11... | collective-permute-start | bytes 1474568 | tf_op jit(solution)/shard_map/ppermute | solution.py:641
  43.2 1.5 %collective-permute-start.12 = (bf16[384,896]{1,0:T(8,128)(2,1)S(1)}, bf16[384,896]{1,0:T(8,128)(2,1)S(1)}, u32[]{:S(2)}, u32[]{:S(2)}) collective-permute-start(bf16[384,896]{1,0:T(8,128)(2,1)S(1)} %collective-permute-done.10.refs_6_), channel_id=1, source_target_pairs={{0,16},{16,0},{1,17},{17,1},{2,18},{18,2},{3,19},{19,3},{4,20},{20... | collective-permute-start | bytes 2064392 | tf_op jit(solution)/shard_map/ppermute | solution.py:635
  44.7 3.4 %shard_map.143 = (f32[256,3072]{1,0:T(8,128)S(1)}, f32[256,3072]{1,0:T(8,128)S(1)}, f32[256,384]{1,0:T(8,128)S(1)}, f32[256,384]{1,0:T(8,128)S(1)}) custom-call(s32[14]{0:T(128)S(1)} %dynamic-slice_bitcast_fusion.place.refs_0_, bf16[256,3072]{1,0:T(8,128)(2,1)S(1)} %copy-done, ...), custom_call_target="tpu_custom_call", output_to_operand_aliasing={{0}: (9, {})} | custom-call | bytes 1 | tf_op jit(solution)/shard_map/pallas_call | solution.py:91
  48.1 4.6 %collective-permute-done.2.refs_8_ = bf16[384,768]{1,0:T(8,128)(2,1)S(1)} collective-permute-done((bf16[384,768]{1,0:T(8,128)(2,1)S(1)}, bf16[384,768]{1,0:T(8,128)(2,1)S(1)}, u32[]{:S(2)}, u32[]{:S(2)}) %collective-permute-start.2) | collective-permute-done | bytes 589856 | tf_op jit(solution)/shard_map/ppermute | solution.py:649
  52.7 1.9 %collective-permute-start.16 = (bf16[384,896]{1,0:T(8,128)(2,1)S(1)}, bf16[384,896]{1,0:T(8,128)(2,1)S(1)}, u32[]{:S(2)}, u32[]{:S(2)}) collective-permute-start(bf16[384,896]{1,0:T(8,128)(2,1)S(1)} %collective-permute-done.11.refs_6_.whole), channel_id=1, source_target_pairs={{0,16},{16,0},{1,17},{17,1},{2,18},{18,2},{3,19},{19,3},{4,20},{20... | collective-permute-start | bytes 2064392 | tf_op jit(solution)/shard_map/ppermute | solution.py:635
  54.6 1.5 %collective-permute-start.9 = (bf16[384,768]{1,0:T(8,128)(2,1)S(1)}, bf16[384,768]{1,0:T(8,128)(2,1)S(1)}, u32[]{:S(2)}, u32[]{:S(2)}) collective-permute-start(bf16[384,768]{1,0:T(8,128)(2,1)S(1)} %collective-permute-done.2.refs_8_), channel_id=1, source_target_pairs={{0,2},{1,5},{2,6},{3,1},{6,10},{7,3},{10,14},{11,7},{14,12},{15,11... | collective-permute-start | bytes 1769480 | tf_op jit(solution)/shard_map/ppermute | solution.py:649
  56.1 1.8 %collective-permute-done.13.refs_7_.block = bf16[384,640]{1,0:T(8,128)(2,1)S(1)} collective-permute-done((bf16[384,640]{1,0:T(8,128)(2,1)S(1)}, bf16[384,640]{1,0:T(8,128)(2,1)S(1)}, u32[]{:S(2)}, u32[]{:S(2)}) %collective-permute-start.13) | collective-permute-done | bytes 491552 | tf_op jit(solution)/shard_map/ppermute | solution.py:641
  58.6 2.0 %collective-permute-start.14 = (bf16[384,640]{1,0:T(8,128)(2,1)S(1)}, bf16[384,640]{1,0:T(8,128)(2,1)S(1)}, u32[]{:S(2)}, u32[]{:S(2)}) collective-permute-start(bf16[384,640]{1,0:T(8,128)(2,1)S(1)} %shard_map.146), channel_id=1, source_target_pairs={{0,2},{1,5},{2,6},{3,1},{6,10},{7,3},{10,14},{11,7},{14,12},{15,11... | collective-permute-start | bytes 1474568 | tf_op jit(solution)/shard_map/ppermute | solution.py:641
  61.2 1.8 %collective-permute-start.15 = (bf16[192,896]{1,0:T(8,128)(2,1)S(1)}, bf16[192,896]{1,0:T(8,128)(2,1)S(1)}, u32[]{:S(2)}, u32[]{:S(2)}) collective-permute-start(bf16[192,896]{1,0:T(8,128)(2,1)S(1)} %shard_map.148), channel_id=1, source_target_pairs={{0,2},{1,5},{2,6},{3,1},{6,10},{7,3},{10,14},{11,7},{14,12},{15,11... | collective-permute-start | bytes 1032200 | tf_op jit(solution)/shard_map/ppermute | solution.py:634
  63.0 4.9 %shard_map.145 = (f32[256,3072]{1,0:T(8,128)S(1)}, f32[256,3072]{1,0:T(8,128)S(1)}, f32[256,384]{1,0:T(8,128)S(1)}, f32[256,384]{1,0:T(8,128)S(1)}, bf16[256,307...) custom-call(s32[14]{0:T(128)S(1)} %dynamic-slice_bitcast_fusion.place.r, ...), custom_call_target="tpu_custom_call", output_to_operand_aliasing={{0}: (12, {}), {1}: (13, {}), {4}: (14, {})} | custom-call | bytes 1 | tf_op jit(solution)/shard_map/pallas_call | solution.py:91
  67.9 1.8 %collective-permute-done.14.refs_7_.block = bf16[384,640]{1,0:T(8,128)(2,1)S(1)} collective-permute-done((bf16[384,640]{1,0:T(8,128)(2,1)S(1)}, bf16[384,640]{1,0:T(8,128)(2,1)S(1)}, u32[]{:S(2)}, u32[]{:S(2)}) %collective-permute-start.14) | collective-permute-done | bytes 491552 | tf_op jit(solution)/shard_map/ppermute | solution.py:641
  69.8 5.2 %shard_map.147 = (f32[256,3072]{1,0:T(8,128)S(1)}, bf16[256,4224]{1,0:T(8,128)(2,1)S(1)}, f32[256,384]{1,0:T(8,128)S(1)}, bf16[256,3072]{1,0:T(8,128)(2,1)}) custom-call(s32[14]{0:T(128)S(1)} %dynamic-slice_bitcast_fusion.place.refs_0_, bf16[256,3072]{1,0:T(8,128)(2,1)S(1)} %copy-done, ...), custom_call_target="tpu_custom_call", output_to_operand_aliasing={{0}: (13, {}), {3}: (15, {})} | custom-call | bytes 1 | tf_op jit(solution)/shard_map/pallas_call | solution.py:91
  75.7 1.8 %collective-permute-start.20 = (bf16[192,1536]{1,0:T(8,128)(2,1)S(1)}, bf16[192,1536]{1,0:T(8,128)(2,1)S(1)}, u32[]{:S(2)}, u32[]{:S(2)}) collective-permute-start(bf16[192,1536]{1,0:T(8,128)(2,1)S(1)} %shard_map.149), channel_id=1, source_target_pairs={{0,2},{1,5},{2,6},{3,1},{6,10},{7,3},{10,14},{11,7},{14,12},{15,11... | collective-permute-start | bytes 1769480 | tf_op jit(solution)/shard_map/ppermute | solution.py:647
  77.7 1.5 %collective-permute-start.22 = (bf16[192,896]{1,0:T(8,128)(2,1)S(1)}, bf16[192,896]{1,0:T(8,128)(2,1)S(1)}, u32[]{:S(2)}, u32[]{:S(2)}) collective-permute-start(bf16[192,896]{1,0:T(8,128)(2,1)S(1)} %collective-permute-done.15.refs_12_), channel_id=1, source_target_pairs={{0,16},{16,0},{1,17},{17,1},{2,18},{18,2},{3,19},{19,3},{4,20},{20... | collective-permute-start | bytes 1032200 | tf_op jit(solution)/shard_map/ppermute | solution.py:654
  79.2 6.4 %collective-permute-done.20.refs_14_.refs_16_.refs_10_ = bf16[192,1536]{1,0:T(8,128)(2,1)S(1)} collective-permute-done((bf16[192,1536]{1,0:T(8,128)(2,1)S(1)}, bf16[192,1536]{1,0:T(8,128)(2,1)S(1)}, u32[]{:S(2)}, u32[]{:S(2)}) %collective-permute-start.20) | collective-permute-done | bytes 589856 | tf_op jit(solution)/shard_map/ppermute | solution.py:647
  86.1 1.8 %collective-permute-done.22.refs_12_ = bf16[192,896]{1,0:T(8,128)(2,1)S(1)} collective-permute-done((bf16[192,896]{1,0:T(8,128)(2,1)S(1)}, bf16[192,896]{1,0:T(8,128)(2,1)S(1)}, u32[]{:S(2)}, u32[]{:S(2)}) %collective-permute-start.22) | collective-permute-done | bytes 344096 | tf_op jit(solution)/shard_map/ppermute | solution.py:654
  88.1 5.3 %shard_map.150 = (f32[256,3072]{1,0:T(8,128)S(1)}, bf16[256,3072]{1,0:T(8,128)(2,1)}, bf16[256,3072]{1,0:T(8,128)(2,1)}, f32[256,384]{1,0:T(8,128)S(1)}) custom-call(s32[14]{0:T(128)S(1)} %dynamic-slice_bitcast_fusion.place.refs_0_, bf16[256,3072]{1,0:T(8,128)(2,1)S(1)} %copy-done, ...), custom_call_target="tpu_custom_call", output_to_operand_aliasing={{0}: (7, {}), {2}: (8, {})} | custom-call | bytes 12 | tf_op jit(solution)/shard_map/pallas_call | solution.py:91
  93.4 3.4 %shard_map.151 = (bf16[256,3072]{1,0:T(8,128)(2,1)}, bf16[256,3072]{1,0:T(8,128)(2,1)}, f32[64,192]{1,0:T(8,128)}, f32[64,192]{1,0:T(8,128)}) custom-call(s32[14]{0:T(128)S(1)} %dynamic-slice_bitcast_fusion.place.refs_0_, bf16[256,3072]{1,0:T(8,128)(2,1)S(1)} %copy-done, ...), custom_call_target="tpu_custom_call", output_to_operand_aliasing={{0}: (6, {}), {1}: (7, {})} | custom-call | bytes 12 | tf_op jit(solution)/shard_map/pallas_call | solution.py:91
  (47 shorter events, 9.6 us)
Async XLA Ops:
  0.6 3.2 %collective-permute-start = (bf16[192,3072]{1,0:T(8,128)(2,1)}, bf16[192,3072]{1,0:T(8,128)(2,1)S(1)}, u32[]{:S(2)}, u32[]{:S(2)}) collective-permute-start(bf16[192,3072]{1,0:T(8,128)(2,1)} %frozen.1), channel_id=1, source_target_pairs={{0,1},{1,0},{2,3},{3,2},{4,5},{5,4},{6,7},{7,6},{8,9},{9,8},{10,11... | collective-permute-start | bytes 3538952 | tf_op jit(solution)/shard_map/ppermute | solution.py:599
  1.8 1.3 %copy-start.3 = (bf16[192,3072]{1,0:T(8,128)(2,1)S(1)}, bf16[192,3072]{1,0:T(8,128)(2,1)}, u32[]{:S(2)}) copy-start(bf16[192,3072]{1,0:T(8,128)(2,1)} %frozen.1) | copy-start | bytes 3538948
  3.1 7.3 %copy-start = (bf16[256,3072]{1,0:T(8,128)(2,1)S(1)}, bf16[256,3072]{1,0:T(8,128)(2,1)}, u32[]{:S(2)}) copy-start(bf16[256,3072]{1,0:T(8,128)(2,1)} %refs_1_.11) | copy-start | bytes 4718596
  3.1 7.3 %copy-start.2 = (bf16[256,3072]{1,0:T(8,128)(2,1)S(1)}, bf16[256,3072]{1,0:T(8,128)(2,1)}, u32[]{:S(2)}) copy-start(bf16[256,3072]{1,0:T(8,128)(2,1)} %cotangent.1) | copy-start | bytes 4718596
  3.1 7.3 %copy-start.7 = (f32[16,3072]{1,0:T(8,128)S(1)}, f32[16,3072]{1,0:T(8,128)}, u32[]{:S(2)}) copy-start(f32[16,3072]{1,0:T(8,128)} %g_gate.1) | copy-start | bytes 589828
  4.6 11.7 %collective-permute-start.1 = (bf16[384,768]{1,0:T(8,128)(2,1)S(1)}, bf16[384,768]{1,0:T(8,128)(2,1)S(1)}, u32[]{:S(2)}, u32[]{:S(2)}) collective-permute-start(bf16[384,768]{1,0:T(8,128)(2,1)S(1)} %get-tuple-element.68.refs_8_), channel_id=1, source_target_pairs={{0,2},{1,5},{2,6},{3,1},{6,10},{7,3},{10,14},{11,7},{14,12},{15,11... | collective-permute-start | bytes 1769480 | tf_op jit(solution)/shard_map/ppermute | solution.py:601
  7.5 15.3 %collective-permute-start.5 = (bf16[384,896]{1,0:T(8,128)(2,1)S(1)}, bf16[384,896]{1,0:T(8,128)(2,1)S(1)}, u32[]{:S(2)}, u32[]{:S(2)}) collective-permute-start(bf16[384,896]{1,0:T(8,128)(2,1)S(1)} %get-tuple-element.70.refs_6_), channel_id=1, source_target_pairs={{0,2},{1,5},{2,6},{3,1},{6,10},{7,3},{10,14},{11,7},{14,12},{15,11... | collective-permute-start | bytes 2064392 | tf_op jit(solution)/shard_map/ppermute | solution.py:601
  10.4 1.1 %copy-start.4 = (f32[3072,64]{0,1:T(8,128)S(1)}, f32[3072,64]{0,1:T(8,128)}, u32[]{:S(2)}) copy-start(f32[3072,64]{0,1:T(8,128)} %param.14) | copy-start | bytes 2359300
  11.5 1.1 %copy-start.5 = (f32[64,3072]{1,0:T(8,128)S(1)}, f32[64,3072]{1,0:T(8,128)}, u32[]{:S(2)}) copy-start(f32[64,3072]{1,0:T(8,128)} %up.1) | copy-start | bytes 2359300
  12.7 1.1 %copy-start.6 = (f32[50,3072]{1,0:T(8,128)S(1)}, f32[50,3072]{1,0:T(8,128)}, u32[]{:S(2)}) copy-start(f32[50,3072]{1,0:T(8,128)} %t_gate.1) | copy-start | bytes 1843204
  16.3 24.6 %collective-permute-start.4 = (bf16[256,3200]{1,0:T(8,128)(2,1)S(1)}, bf16[256,3200]{1,0:T(8,128)(2,1)S(1)}, u32[]{:S(2)}, u32[]{:S(2)}) collective-permute-start(bf16[256,3200]{1,0:T(8,128)(2,1)S(1)} %get-tuple-element.93.refs_2_), channel_id=1, source_target_pairs={{0,1},{1,0},{2,3},{3,2},{4,5},{5,4},{6,7},{7,6},{8,9},{9,8},{10,11... | collective-permute-start | bytes 4915208 | tf_op jit(solution)/shard_map/ppermute | solution.py:612
  16.4 8.4 %collective-permute-start.6 = (bf16[8,384,128]{2,1,0:T(8,128)(2,1)S(1)}, bf16[8,384,128]{2,1,0:T(8,128)(2,1)S(1)}, u32[]{:S(2)}, u32[]{:S(2)}) collective-permute-start(bf16[8,384,128]{2,1,0:T(8,128)(2,1)S(1)} %get-tuple-element.78), channel_id=1, source_target_pairs={{0,1},{1,0},{2,3},{3,2},{4,5},{5,4},{6,7},{7,6},{8,9},{9,8},{10,11... | collective-permute-start | bytes 2359304 | tf_op jit(solution)/shard_map/ppermute | solution.py:608
  16.9 26.3 %collective-permute-start.3 = (bf16[256,3072]{1,0:T(8,128)(2,1)S(1)}, bf16[256,3072]{1,0:T(8,128)(2,1)S(1)}, u32[]{:S(2)}, u32[]{:S(2)}) collective-permute-start(bf16[256,3072]{1,0:T(8,128)(2,1)S(1)} %copy-done), channel_id=1, source_target_pairs={{0,1},{1,0},{2,3},{3,2},{4,5},{5,4},{6,7},{7,6},{8,9},{9,8},{10,11... | collective-permute-start | bytes 4718600 | tf_op jit(solution)/shard_map/ppermute | solution.py:603
  22.8 10.9 %collective-permute-start.10 = (bf16[384,896]{1,0:T(8,128)(2,1)S(1)}, bf16[384,896]{1,0:T(8,128)(2,1)S(1)}, u32[]{:S(2)}, u32[]{:S(2)}) collective-permute-start(bf16[384,896]{1,0:T(8,128)(2,1)S(1)} %collective-permute-done.5.refs_6_), channel_id=1, source_target_pairs={{0,2},{1,5},{2,6},{3,1},{6,10},{7,3},{10,14},{11,7},{14,12},{15,11... | collective-permute-start | bytes 2064392 | tf_op jit(solution)/shard_map/ppermute | solution.py:634
  25.3 13.6 %collective-permute-start.7 = (bf16[384,640]{1,0:T(8,128)(2,1)S(1)}, bf16[384,640]{1,0:T(8,128)(2,1)S(1)}, u32[]{:S(2)}, u32[]{:S(2)}) collective-permute-start(bf16[384,640]{1,0:T(8,128)(2,1)S(1)} %shard_map.142), channel_id=1, source_target_pairs={{0,2},{1,5},{2,6},{3,1},{6,10},{7,3},{10,14},{11,7},{14,12},{15,11... | collective-permute-start | bytes 1474568 | tf_op jit(solution)/shard_map/ppermute | solution.py:610
  27.0 25.7 %collective-permute-start.8 = (bf16[384,896]{1,0:T(8,128)(2,1)S(1)}, bf16[384,896]{1,0:T(8,128)(2,1)S(1)}, u32[]{:S(2)}, u32[]{:S(2)}) collective-permute-start(bf16[384,896]{1,0:T(8,128)(2,1)S(1)} %collective-permute-done.5.refs_6_), channel_id=1, source_target_pairs={{0,16},{16,0},{1,17},{17,1},{2,18},{18,2},{3,19},{19,3},{4,20},{20... | collective-permute-start | bytes 2064392 | tf_op jit(solution)/shard_map/ppermute | solution.py:635
  33.7 19.0 %collective-permute-start.11 = (bf16[384,896]{1,0:T(8,128)(2,1)S(1)}, bf16[384,896]{1,0:T(8,128)(2,1)S(1)}, u32[]{:S(2)}, u32[]{:S(2)}) collective-permute-start(bf16[384,896]{1,0:T(8,128)(2,1)S(1)} %collective-permute-done.10.refs_6_), channel_id=1, source_target_pairs={{0,2},{1,5},{2,6},{3,1},{6,10},{7,3},{10,14},{11,7},{14,12},{15,11... | collective-permute-start | bytes 2064392 | tf_op jit(solution)/shard_map/ppermute | solution.py:634
  39.0 13.7 %collective-permute-start.2 = (bf16[384,768]{1,0:T(8,128)(2,1)S(1)}, bf16[384,768]{1,0:T(8,128)(2,1)S(1)}, u32[]{:S(2)}, u32[]{:S(2)}) collective-permute-start(bf16[384,768]{1,0:T(8,128)(2,1)S(1)} %collective-permute-done.1.refs_8_), channel_id=1, source_target_pairs={{0,2},{1,5},{2,6},{3,1},{6,10},{7,3},{10,14},{11,7},{14,12},{15,11... | collective-permute-start | bytes 1769480 | tf_op jit(solution)/shard_map/ppermute | solution.py:649
  41.6 16.4 %collective-permute-start.13 = (bf16[384,640]{1,0:T(8,128)(2,1)S(1)}, bf16[384,640]{1,0:T(8,128)(2,1)S(1)}, u32[]{:S(2)}, u32[]{:S(2)}) collective-permute-start(bf16[384,640]{1,0:T(8,128)(2,1)S(1)} %shard_map.144), channel_id=1, source_target_pairs={{0,2},{1,5},{2,6},{3,1},{6,10},{7,3},{10,14},{11,7},{14,12},{15,11... | collective-permute-start | bytes 1474568 | tf_op jit(solution)/shard_map/ppermute | solution.py:641
  43.2 19.8 %collective-permute-start.12 = (bf16[384,896]{1,0:T(8,128)(2,1)S(1)}, bf16[384,896]{1,0:T(8,128)(2,1)S(1)}, u32[]{:S(2)}, u32[]{:S(2)}) collective-permute-start(bf16[384,896]{1,0:T(8,128)(2,1)S(1)} %collective-permute-done.10.refs_6_), channel_id=1, source_target_pairs={{0,16},{16,0},{1,17},{17,1},{2,18},{18,2},{3,19},{19,3},{4,20},{20... | collective-permute-start | bytes 2064392 | tf_op jit(solution)/shard_map/ppermute | solution.py:635
  52.7 22.3 %collective-permute-start.16 = (bf16[384,896]{1,0:T(8,128)(2,1)S(1)}, bf16[384,896]{1,0:T(8,128)(2,1)S(1)}, u32[]{:S(2)}, u32[]{:S(2)}) collective-permute-start(bf16[384,896]{1,0:T(8,128)(2,1)S(1)} %collective-permute-done.11.refs_6_.whole), channel_id=1, source_target_pairs={{0,16},{16,0},{1,17},{17,1},{2,18},{18,2},{3,19},{19,3},{4,20},{20... | collective-permute-start | bytes 2064392 | tf_op jit(solution)/shard_map/ppermute | solution.py:635
  54.6 13.3 %collective-permute-start.9 = (bf16[384,768]{1,0:T(8,128)(2,1)S(1)}, bf16[384,768]{1,0:T(8,128)(2,1)S(1)}, u32[]{:S(2)}, u32[]{:S(2)}) collective-permute-start(bf16[384,768]{1,0:T(8,128)(2,1)S(1)} %collective-permute-done.2.refs_8_), channel_id=1, source_target_pairs={{0,2},{1,5},{2,6},{3,1},{6,10},{7,3},{10,14},{11,7},{14,12},{15,11... | collective-permute-start | bytes 1769480 | tf_op jit(solution)/shard_map/ppermute | solution.py:649
  58.6 11.2 %collective-permute-start.14 = (bf16[384,640]{1,0:T(8,128)(2,1)S(1)}, bf16[384,640]{1,0:T(8,128)(2,1)S(1)}, u32[]{:S(2)}, u32[]{:S(2)}) collective-permute-start(bf16[384,640]{1,0:T(8,128)(2,1)S(1)} %shard_map.146), channel_id=1, source_target_pairs={{0,2},{1,5},{2,6},{3,1},{6,10},{7,3},{10,14},{11,7},{14,12},{15,11... | collective-permute-start | bytes 1474568 | tf_op jit(solution)/shard_map/ppermute | solution.py:641
  61.2 13.8 %collective-permute-start.15 = (bf16[192,896]{1,0:T(8,128)(2,1)S(1)}, bf16[192,896]{1,0:T(8,128)(2,1)S(1)}, u32[]{:S(2)}, u32[]{:S(2)}) collective-permute-start(bf16[192,896]{1,0:T(8,128)(2,1)S(1)} %shard_map.148), channel_id=1, source_target_pairs={{0,2},{1,5},{2,6},{3,1},{6,10},{7,3},{10,14},{11,7},{14,12},{15,11... | collective-permute-start | bytes 1032200 | tf_op jit(solution)/shard_map/ppermute | solution.py:634
  75.0 13.2 %copy-start.1 = (bf16[256,3072]{1,0:T(8,128)(2,1)S(1)}, bf16[256,3072]{1,0:T(8,128)(2,1)}, u32[]{:S(2)}) copy-start(bf16[256,3072]{1,0:T(8,128)(2,1)} %refs_3_.1) | copy-start | bytes 4718596
  75.0 10.6 %collective-permute-start.17 = (bf16[256,4224]{1,0:T(8,128)(2,1)S(1)}, bf16[256,4224]{1,0:T(8,128)(2,1)S(1)}, u32[]{:S(2)}, u32[]{:S(2)}) collective-permute-start(bf16[256,4224]{1,0:T(8,128)(2,1)S(1)} %get-tuple-element.104), channel_id=1, source_target_pairs={{0,1},{1,0},{2,3},{3,2},{4,5},{5,4},{6,7},{7,6},{8,9},{9,8},{10,11... | collective-permute-start | bytes 6488072 | tf_op jit(solution)/shard_map/ppermute | solution.py:663
  75.7 9.9 %collective-permute-start.20 = (bf16[192,1536]{1,0:T(8,128)(2,1)S(1)}, bf16[192,1536]{1,0:T(8,128)(2,1)S(1)}, u32[]{:S(2)}, u32[]{:S(2)}) collective-permute-start(bf16[192,1536]{1,0:T(8,128)(2,1)S(1)} %shard_map.149), channel_id=1, source_target_pairs={{0,2},{1,5},{2,6},{3,1},{6,10},{7,3},{10,14},{11,7},{14,12},{15,11... | collective-permute-start | bytes 1769480 | tf_op jit(solution)/shard_map/ppermute | solution.py:647
  77.4 10.7 %collective-permute-start.18 = (bf16[384,896]{1,0:T(8,128)(2,1)S(1)}, bf16[384,896]{1,0:T(8,128)(2,1)S(1)}, u32[]{:S(2)}, u32[]{:S(2)}) collective-permute-start(bf16[384,896]{1,0:T(8,128)(2,1)S(1)} %collective-permute-done.16.refs_9_), channel_id=1, source_target_pairs={{0,1},{1,0},{2,3},{3,2},{4,5},{5,4},{6,7},{7,6},{8,9},{9,8},{10,11... | collective-permute-start | bytes 2064392 | tf_op jit(solution)/shard_map/ppermute | solution.py:658
  77.7 10.2 %collective-permute-start.22 = (bf16[192,896]{1,0:T(8,128)(2,1)S(1)}, bf16[192,896]{1,0:T(8,128)(2,1)S(1)}, u32[]{:S(2)}, u32[]{:S(2)}) collective-permute-start(bf16[192,896]{1,0:T(8,128)(2,1)S(1)} %collective-permute-done.15.refs_12_), channel_id=1, source_target_pairs={{0,16},{16,0},{1,17},{17,1},{2,18},{18,2},{3,19},{19,3},{4,20},{20... | collective-permute-start | bytes 1032200 | tf_op jit(solution)/shard_map/ppermute | solution.py:654
  85.6 2.5 %collective-permute-start.21 = (bf16[192,1536]{1,0:T(8,128)(2,1)S(1)}, bf16[192,1536]{1,0:T(8,128)(2,1)S(1)}, u32[]{:S(2)}, u32[]{:S(2)}) collective-permute-start(bf16[192,1536]{1,0:T(8,128)(2,1)S(1)} %collective-permute-done.20.refs_14_.refs_16_.refs_10_), channel_id=1, source_target_pairs={{0,1},{1,0},{2,3},{3,2},{4,5},{5,4},{6,7},{7,6},{8,9},{9,8},{10,11... | collective-permute-start | bytes 1769480 | tf_op jit(solution)/shard_map/ppermute | solution.py:664
  85.6 2.5 %collective-permute-start.19 = (bf16[192,896]{1,0:T(8,128)(2,1)S(1)}, bf16[192,896]{1,0:T(8,128)(2,1)S(1)}, u32[]{:S(2)}, u32[]{:S(2)}) collective-permute-start(bf16[192,896]{1,0:T(8,128)(2,1)S(1)} %collective-permute-done.15.refs_12_), channel_id=1, source_target_pairs={{0,1},{1,0},{2,3},{3,2},{4,5},{5,4},{6,7},{7,6},{8,9},{9,8},{10,11... | collective-permute-start | bytes 1032200 | tf_op jit(solution)/shard_map/ppermute | solution.py:658
  87.9 5.5 %collective-permute-start.23 = (bf16[192,896]{1,0:T(8,128)(2,1)S(1)}, bf16[192,896]{1,0:T(8,128)(2,1)S(1)}, u32[]{:S(2)}, u32[]{:S(2)}) collective-permute-start(bf16[192,896]{1,0:T(8,128)(2,1)S(1)} %collective-permute-done.22.refs_12_), channel_id=1, source_target_pairs={{0,1},{1,0},{2,3},{3,2},{4,5},{5,4},{6,7},{7,6},{8,9},{9,8},{10,11... | collective-permute-start | bytes 1032200 | tf_op jit(solution)/shard_map/ppermute | solution.py:676

commit v4 on v3

--- a/solution.py
+++ b/solution.py
@@ -377,7 +377,8 @@
         give("low", add[0])
         give("up", add[1])
     if any(job["final"] for job in jobs):
-        give("resid", final[0], HBM_SPEC)
+        if not all(job["folded"] for job in jobs):
+            give("resid", final[0], HBM_SPEC)
         give("gate", final[1])
     outs, out_specs = [], []
 
@@ -422,7 +423,7 @@
             produce(("open", j), (rows, deep), F32, VMEM_SPEC)
         scratch += [
             pltpu.VMEM((deep, width), BF16) if halves else tiny,
-            pltpu.VMEM((rows, width), BF16) if job["final"] else tiny,
+            pltpu.VMEM((rows, width), BF16) if job["final"] != job["folded"] else tiny,
             pltpu.VMEM((rows, width), BF16) if job["final"] else tiny,
             tiny if job["open"] else pltpu.VMEM((rows, deep), BF16),
         ]
@@ -443,7 +444,7 @@
             stores.append(copy)
 
         for j, job in enumerate(jobs):
-            if job["final"]:
+            if job["final"] != job["folded"]:
                 for block in job["blocks"]:
                     here = pl.ds(starts[block] - starts[job["blocks"][0]], blocks[block])
                     src = ref["resid"].at[:, cols(place[2 + block], blocks[block])]
@@ -461,7 +462,10 @@
             for n, block in enumerate(job["blocks"]):
                 width = blocks[block]
                 here, there = pl.ds(starts[block] - starts[job["blocks"][0]], width), pl.ds(starts[block], width)
-                value = ref["total_in"][:, there] if total is not None else matmul(ref["low"][...], ref["up"][:, there])
+                if job["final"] and job["folded"]:
+                    value = 0.0
+                else:
+                    value = ref["total_in"][:, there] if total is not None else matmul(ref["low"][...], ref["up"][:, there])
                 if extra is not None:
                     value = value + ref["extra"][:, there].astype(F32)
                 for c, at in enumerate(chip_cols):
@@ -479,10 +483,17 @@
                     term = contract_cols(ref["gout"][:, there], piece)
                     back[c] = term if back[c] is None else back[c] + term
                 if job["final"]:
-                    loads[j, block].wait()
-                    result_v[:, here] = (resid_v[:, here].astype(F32) + ref["gate"][:, there] * value).astype(BF16)
+                    if job["folded"]:
+                        start = ref["total_in"][:, there]
+                    else:
+                        loads[j, block].wait()
+                        start = resid_v[:, here].astype(F32)
+                    result_v[:, here] = (start + ref["gate"][:, there] * value).astype(BF16)
                     put(result_v.at[:, here], ref[("out", "updated")].at[:, cols(place[2 + block], width)])
                 else:
+                    if job["folded"]:
+                        loads[j, block].wait()
+                        value = resid_v[:, here].astype(F32) + ref["gate"][:, there] * value
                     ref[("out", "total")][:, there] = value
             for c, at in enumerate(chip_cols):
                 mine = pl.ds(c * span, span)
@@ -533,8 +544,8 @@
     return min(sizes)
 
 
-def job(chips, blocks, pieces, part=None, open=False, final=False):
-    return dict(chips=chips, blocks=blocks, pieces=pieces, part=part, open=open, final=final)
+def job(chips, blocks, pieces, part=None, open=False, final=False, folded=False):
+    return dict(chips=chips, blocks=blocks, pieces=pieces, part=part, open=open, final=final, folded=folded)
 
 
 EDGES = dict(
@@ -662,7 +673,7 @@
         run(steps, q_far, X=x[steps], c=message)
     extra = swap(gate("send", give, r=r_far, X=x[steps], q=q_far))
     q_swapped = swap(gate("q5", q_far, e=extra, **swaps))
-    x_job = job([near(steps), across(steps)], [3], [[x_before, x_swapped]], part=[parts[0], None])
+    x_job = job([near(steps), across(steps)], [3], [[x_before, x_swapped]], part=[parts[0], None], folded=True)
     q_piece, s_piece = (q_far, q_swapped), (Part(q_far, 0, wide), Part(q_swapped, 0, wide))
     columns = [across(n) for n in range(1, steps)]
     far_job = job([far], [0, 1, 2], [[(r_far, r_swapped)], [q_piece], [s_piece]], open=True, final=True)
@@ -673,7 +684,7 @@
     x_far = gate("x5", x_far, s=q_far, q=q_far, T=total)
     sums = (terms, terms_t, q_far, q_swapped, wide + blocks[2], float(rows * axis_size) ** (-0.5))
     _, updated, grad_attn, grad_down_t, grad_up = step(
-        place, [job([far], [3], [[(x_far, swap(x_far))]], part=[part], final=True)],
+        place, [job([far], [3], [[(x_far, swap(x_far))]], part=[part], final=True, folded=True)],
         attn, blocks, grads, total=total, final=(resid, gate_row), updated=updated, grad_attn=grad_attn, sums=sums,
     )
     return updated, grad_attn, grad_down_t.T, grad_up.T

time: 97.3 us -> 96.9 us (level)
  no operation moved by 1% of the time
where the time goes in v4:
time: 96.9 us; the launch traced here: 96.6 us
  Pallas kernels  32.4 us (33%)
  starting transfers between devices  29.2 us (30%)
  waiting for transfers between devices  27.3 us (28%)
  local copies, waits for them, and re-layouts  5.34 us (6%)
  between operations  2.31 us (2%)
    pallas_call x14, Pallas kernels, call(): pl.pallas_call(kernel, in_specs=specs, out_shape=out_shape, out_specs=out...  32.4 us
    ppermute x3, waiting for transfers between devices, ring_body(): q.append(ring(message))  10.1 us
    ppermute x3, starting transfers between devices, ring_body(): r.append(ring(own_half(place, r[n]) if last else r[n]))  5.74 us
    ppermute x3, starting transfers between devices, ring_body(): q.append(ring(message))  5.42 us
    ppermute x3, waiting for transfers between devices, ring_body(): r.append(ring(own_half(place, r[n]) if last else r[n]))  5.26 us
    ppermute x3, starting transfers between devices, ring_body(): x.append(cross(gate(f'x{n}', r[n], **prev)))  4.92 us
    unnamed x16, local copies, waits for them, and re-layouts  4.65 us
    ppermute x2, waiting for transfers between devices, ring_body(): s.append(ring(s[n]))  4.57 us
  transfers between devices with their start and end apart: 24, of which 9 were waited for; matrix products, arithmetic and copies ran while one was open for 1% of the time, Pallas kernels for 30%

profile of v4, /device:TPU:0, one launch (start us, length us, event | category | flops | bytes accessed | tf_op | source)
XLA Modules:
  0.0 96.6 jit_solution(8781343948021005072)
XLA Ops:
  1.8 1.3 %copy-done.3 = bf16[192,3072]{1,0:T(8,128)(2,1)S(1)} copy-done((bf16[192,3072]{1,0:T(8,128)(2,1)S(1)}, bf16[192,3072]{1,0:T(8,128)(2,1)}, u32[]{:S(2)}) %copy-start.3) | copy-done | bytes 1179672
  4.6 2.9 %collective-permute-start.1 = (bf16[384,768]{1,0:T(8,128)(2,1)S(1)}, bf16[384,768]{1,0:T(8,128)(2,1)S(1)}, u32[]{:S(2)}, u32[]{:S(2)}) collective-permute-start(bf16[384,768]{1,0:T(8,128)(2,1)S(1)} %get-tuple-element.68.refs_8_), channel_id=1, source_target_pairs={{0,2},{1,5},{2,6},{3,1},{6,10},{7,3},{10,14},{11,7},{14,12},{15,11... | collective-permute-start | bytes 1769480 | tf_op jit(solution)/shard_map/ppermute | solution.py:612
  7.5 1.6 %collective-permute-start.5 = (bf16[384,896]{1,0:T(8,128)(2,1)S(1)}, bf16[384,896]{1,0:T(8,128)(2,1)S(1)}, u32[]{:S(2)}, u32[]{:S(2)}) collective-permute-start(bf16[384,896]{1,0:T(8,128)(2,1)S(1)} %get-tuple-element.70.refs_6_), channel_id=1, source_target_pairs={{0,2},{1,5},{2,6},{3,1},{6,10},{7,3},{10,14},{11,7},{14,12},{15,11... | collective-permute-start | bytes 2064392 | tf_op jit(solution)/shard_map/ppermute | solution.py:612
  11.5 1.1 %copy-done.5 = f32[64,3072]{1,0:T(8,128)S(1)} copy-done((f32[64,3072]{1,0:T(8,128)S(1)}, f32[64,3072]{1,0:T(8,128)}, u32[]{:S(2)}) %copy-start.5) | copy-done | bytes 786456
  13.8 2.5 %shard_map.138 = (f32[1,3072]{1,0:T(1,128)S(1)}, bf16[256,3200]{1,0:T(8,128)(2,1)S(1)}, bf16[256,64]{1,0:T(8,128)(2,1)S(1)}, bf16[64,3072]{1,0:T(8,128)(2,1)S(1)...) custom-call(s32[14]{0:T(128)S(1)} %dynamic-slice_bitcast_fusion.place.refs_0_, ...), custom_call_target="tpu_custom_call" | custom-call | bytes 1 | tf_op jit(solution)/shard_map/pallas_call | solution.py:91
  17.0 3.7 %shard_map.141 = (f32[256,3072]{1,0:T(8,128)S(1)}, bf16[256,3072]{1,0:T(8,128)(2,1)}) custom-call(s32[14]{0:T(128)S(1)} %dynamic-slice_bitcast_fusion.place.refs_0_, bf16[256,3072]{1,0:T(8,128)(2,1)S(1)} %copy-done, bf16[256,3200]{1,0:T(8,128)(2,1)S(1)} %get-tuple-element.93.refs_2_, bf16[64,3072]{1,0:T(8,128)(2,1)S(1)} %get-tuple-element.63.refs_3_.refs_5_, ...), custom_call_target="tpu_custom_call" | custom-call | bytes 12 | tf_op jit(solution)/shard_map/pallas_call | solution.py:91
  20.7 2.1 %collective-permute-done.5.refs_6_ = bf16[384,896]{1,0:T(8,128)(2,1)S(1)} collective-permute-done((bf16[384,896]{1,0:T(8,128)(2,1)S(1)}, bf16[384,896]{1,0:T(8,128)(2,1)S(1)}, u32[]{:S(2)}, u32[]{:S(2)}) %collective-permute-start.5) | collective-permute-done | bytes 688160 | tf_op jit(solution)/shard_map/ppermute | solution.py:612
  22.8 2.0 %collective-permute-start.10 = (bf16[384,896]{1,0:T(8,128)(2,1)S(1)}, bf16[384,896]{1,0:T(8,128)(2,1)S(1)}, u32[]{:S(2)}, u32[]{:S(2)}) collective-permute-start(bf16[384,896]{1,0:T(8,128)(2,1)S(1)} %collective-permute-done.5.refs_6_), channel_id=1, source_target_pairs={{0,2},{1,5},{2,6},{3,1},{6,10},{7,3},{10,14},{11,7},{14,12},{15,11... | collective-permute-start | bytes 2064392 | tf_op jit(solution)/shard_map/ppermute | solution.py:645
  25.3 1.6 %collective-permute-start.7 = (bf16[384,640]{1,0:T(8,128)(2,1)S(1)}, bf16[384,640]{1,0:T(8,128)(2,1)S(1)}, u32[]{:S(2)}, u32[]{:S(2)}) collective-permute-start(bf16[384,640]{1,0:T(8,128)(2,1)S(1)} %shard_map.142), channel_id=1, source_target_pairs={{0,2},{1,5},{2,6},{3,1},{6,10},{7,3},{10,14},{11,7},{14,12},{15,11... | collective-permute-start | bytes 1474568 | tf_op jit(solution)/shard_map/ppermute | solution.py:621
  27.0 1.5 %collective-permute-start.8 = (bf16[384,896]{1,0:T(8,128)(2,1)S(1)}, bf16[384,896]{1,0:T(8,128)(2,1)S(1)}, u32[]{:S(2)}, u32[]{:S(2)}) collective-permute-start(bf16[384,896]{1,0:T(8,128)(2,1)S(1)} %collective-permute-done.5.refs_6_), channel_id=1, source_target_pairs={{0,16},{16,0},{1,17},{17,1},{2,18},{18,2},{3,19},{19,3},{4,20},{20... | collective-permute-start | bytes 2064392 | tf_op jit(solution)/shard_map/ppermute | solution.py:646
  28.5 5.3 %collective-permute-done.10.refs_6_ = bf16[384,896]{1,0:T(8,128)(2,1)S(1)} collective-permute-done((bf16[384,896]{1,0:T(8,128)(2,1)S(1)}, bf16[384,896]{1,0:T(8,128)(2,1)S(1)}, u32[]{:S(2)}, u32[]{:S(2)}) %collective-permute-start.10) | collective-permute-done | bytes 688160 | tf_op jit(solution)/shard_map/ppermute | solution.py:645
  33.7 2.0 %collective-permute-start.11 = (bf16[384,896]{1,0:T(8,128)(2,1)S(1)}, bf16[384,896]{1,0:T(8,128)(2,1)S(1)}, u32[]{:S(2)}, u32[]{:S(2)}) collective-permute-start(bf16[384,896]{1,0:T(8,128)(2,1)S(1)} %collective-permute-done.10.refs_6_), channel_id=1, source_target_pairs={{0,2},{1,5},{2,6},{3,1},{6,10},{7,3},{10,14},{11,7},{14,12},{15,11... | collective-permute-start | bytes 2064392 | tf_op jit(solution)/shard_map/ppermute | solution.py:645
  35.7 3.3 %collective-permute-done.7.refs_7_.block = bf16[384,640]{1,0:T(8,128)(2,1)S(1)} collective-permute-done((bf16[384,640]{1,0:T(8,128)(2,1)S(1)}, bf16[384,640]{1,0:T(8,128)(2,1)S(1)}, u32[]{:S(2)}, u32[]{:S(2)}) %collective-permute-start.7) | collective-permute-done | bytes 491552 | tf_op jit(solution)/shard_map/ppermute | solution.py:621
  39.0 2.0 %collective-permute-start.2 = (bf16[384,768]{1,0:T(8,128)(2,1)S(1)}, bf16[384,768]{1,0:T(8,128)(2,1)S(1)}, u32[]{:S(2)}, u32[]{:S(2)}) collective-permute-start(bf16[384,768]{1,0:T(8,128)(2,1)S(1)} %collective-permute-done.1.refs_8_), channel_id=1, source_target_pairs={{0,2},{1,5},{2,6},{3,1},{6,10},{7,3},{10,14},{11,7},{14,12},{15,11... | collective-permute-start | bytes 1769480 | tf_op jit(solution)/shard_map/ppermute | solution.py:660
  41.6 1.6 %collective-permute-start.13 = (bf16[384,640]{1,0:T(8,128)(2,1)S(1)}, bf16[384,640]{1,0:T(8,128)(2,1)S(1)}, u32[]{:S(2)}, u32[]{:S(2)}) collective-permute-start(bf16[384,640]{1,0:T(8,128)(2,1)S(1)} %shard_map.144), channel_id=1, source_target_pairs={{0,2},{1,5},{2,6},{3,1},{6,10},{7,3},{10,14},{11,7},{14,12},{15,11... | collective-permute-start | bytes 1474568 | tf_op jit(solution)/shard_map/ppermute | solution.py:652
  43.2 1.5 %collective-permute-start.12 = (bf16[384,896]{1,0:T(8,128)(2,1)S(1)}, bf16[384,896]{1,0:T(8,128)(2,1)S(1)}, u32[]{:S(2)}, u32[]{:S(2)}) collective-permute-start(bf16[384,896]{1,0:T(8,128)(2,1)S(1)} %collective-permute-done.10.refs_6_), channel_id=1, source_target_pairs={{0,16},{16,0},{1,17},{17,1},{2,18},{18,2},{3,19},{19,3},{4,20},{20... | collective-permute-start | bytes 2064392 | tf_op jit(solution)/shard_map/ppermute | solution.py:646
  44.7 3.4 %shard_map.143 = (f32[256,3072]{1,0:T(8,128)S(1)}, f32[256,3072]{1,0:T(8,128)S(1)}, f32[256,384]{1,0:T(8,128)S(1)}, f32[256,384]{1,0:T(8,128)S(1)}) custom-call(s32[14]{0:T(128)S(1)} %dynamic-slice_bitcast_fusion.place.refs_0_, bf16[256,3072]{1,0:T(8,128)(2,1)S(1)} %copy-done, ...), custom_call_target="tpu_custom_call", output_to_operand_aliasing={{0}: (9, {})} | custom-call | bytes 1 | tf_op jit(solution)/shard_map/pallas_call | solution.py:91
  48.1 4.6 %collective-permute-done.2.refs_8_ = bf16[384,768]{1,0:T(8,128)(2,1)S(1)} collective-permute-done((bf16[384,768]{1,0:T(8,128)(2,1)S(1)}, bf16[384,768]{1,0:T(8,128)(2,1)S(1)}, u32[]{:S(2)}, u32[]{:S(2)}) %collective-permute-start.2) | collective-permute-done | bytes 589856 | tf_op jit(solution)/shard_map/ppermute | solution.py:660
  52.7 1.9 %collective-permute-start.16 = (bf16[384,896]{1,0:T(8,128)(2,1)S(1)}, bf16[384,896]{1,0:T(8,128)(2,1)S(1)}, u32[]{:S(2)}, u32[]{:S(2)}) collective-permute-start(bf16[384,896]{1,0:T(8,128)(2,1)S(1)} %collective-permute-done.11.refs_6_.whole), channel_id=1, source_target_pairs={{0,16},{16,0},{1,17},{17,1},{2,18},{18,2},{3,19},{19,3},{4,20},{20... | collective-permute-start | bytes 2064392 | tf_op jit(solution)/shard_map/ppermute | solution.py:646
  54.6 1.5 %collective-permute-start.9 = (bf16[384,768]{1,0:T(8,128)(2,1)S(1)}, bf16[384,768]{1,0:T(8,128)(2,1)S(1)}, u32[]{:S(2)}, u32[]{:S(2)}) collective-permute-start(bf16[384,768]{1,0:T(8,128)(2,1)S(1)} %collective-permute-done.2.refs_8_), channel_id=1, source_target_pairs={{0,2},{1,5},{2,6},{3,1},{6,10},{7,3},{10,14},{11,7},{14,12},{15,11... | collective-permute-start | bytes 1769480 | tf_op jit(solution)/shard_map/ppermute | solution.py:660
  56.1 1.8 %collective-permute-done.13.refs_7_.block = bf16[384,640]{1,0:T(8,128)(2,1)S(1)} collective-permute-done((bf16[384,640]{1,0:T(8,128)(2,1)S(1)}, bf16[384,640]{1,0:T(8,128)(2,1)S(1)}, u32[]{:S(2)}, u32[]{:S(2)}) %collective-permute-start.13) | collective-permute-done | bytes 491552 | tf_op jit(solution)/shard_map/ppermute | solution.py:652
  58.6 2.0 %collective-permute-start.14 = (bf16[384,640]{1,0:T(8,128)(2,1)S(1)}, bf16[384,640]{1,0:T(8,128)(2,1)S(1)}, u32[]{:S(2)}, u32[]{:S(2)}) collective-permute-start(bf16[384,640]{1,0:T(8,128)(2,1)S(1)} %shard_map.146), channel_id=1, source_target_pairs={{0,2},{1,5},{2,6},{3,1},{6,10},{7,3},{10,14},{11,7},{14,12},{15,11... | collective-permute-start | bytes 1474568 | tf_op jit(solution)/shard_map/ppermute | solution.py:652
  61.2 1.8 %collective-permute-start.15 = (bf16[192,896]{1,0:T(8,128)(2,1)S(1)}, bf16[192,896]{1,0:T(8,128)(2,1)S(1)}, u32[]{:S(2)}, u32[]{:S(2)}) collective-permute-start(bf16[192,896]{1,0:T(8,128)(2,1)S(1)} %shard_map.148), channel_id=1, source_target_pairs={{0,2},{1,5},{2,6},{3,1},{6,10},{7,3},{10,14},{11,7},{14,12},{15,11... | collective-permute-start | bytes 1032200 | tf_op jit(solution)/shard_map/ppermute | solution.py:645
  63.0 4.9 %shard_map.145 = (f32[256,3072]{1,0:T(8,128)S(1)}, f32[256,3072]{1,0:T(8,128)S(1)}, f32[256,384]{1,0:T(8,128)S(1)}, f32[256,384]{1,0:T(8,128)S(1)}, bf16[256,307...) custom-call(s32[14]{0:T(128)S(1)} %dynamic-slice_bitcast_fusion.place.r, ...), custom_call_target="tpu_custom_call", output_to_operand_aliasing={{0}: (12, {}), {1}: (13, {}), {4}: (14, {})} | custom-call | bytes 1 | tf_op jit(solution)/shard_map/pallas_call | solution.py:91
  67.9 1.9 %collective-permute-done.14.refs_7_.block = bf16[384,640]{1,0:T(8,128)(2,1)S(1)} collective-permute-done((bf16[384,640]{1,0:T(8,128)(2,1)S(1)}, bf16[384,640]{1,0:T(8,128)(2,1)S(1)}, u32[]{:S(2)}, u32[]{:S(2)}) %collective-permute-start.14) | collective-permute-done | bytes 491552 | tf_op jit(solution)/shard_map/ppermute | solution.py:652
  69.8 5.2 %shard_map.147 = (f32[256,3072]{1,0:T(8,128)S(1)}, bf16[256,4224]{1,0:T(8,128)(2,1)S(1)}, f32[256,384]{1,0:T(8,128)S(1)}, bf16[256,3072]{1,0:T(8,128)(2,1)}) custom-call(s32[14]{0:T(128)S(1)} %dynamic-slice_bitcast_fusion.place.refs_0_, bf16[256,3072]{1,0:T(8,128)(2,1)S(1)} %copy-done, ...), custom_call_target="tpu_custom_call", output_to_operand_aliasing={{0}: (13, {}), {3}: (15, {})} | custom-call | bytes 1 | tf_op jit(solution)/shard_map/pallas_call | solution.py:91
  75.7 1.8 %collective-permute-start.20 = (bf16[192,1536]{1,0:T(8,128)(2,1)S(1)}, bf16[192,1536]{1,0:T(8,128)(2,1)S(1)}, u32[]{:S(2)}, u32[]{:S(2)}) collective-permute-start(bf16[192,1536]{1,0:T(8,128)(2,1)S(1)} %shard_map.149), channel_id=1, source_target_pairs={{0,2},{1,5},{2,6},{3,1},{6,10},{7,3},{10,14},{11,7},{14,12},{15,11... | collective-permute-start | bytes 1769480 | tf_op jit(solution)/shard_map/ppermute | solution.py:658
  77.7 1.5 %collective-permute-start.22 = (bf16[192,896]{1,0:T(8,128)(2,1)S(1)}, bf16[192,896]{1,0:T(8,128)(2,1)S(1)}, u32[]{:S(2)}, u32[]{:S(2)}) collective-permute-start(bf16[192,896]{1,0:T(8,128)(2,1)S(1)} %collective-permute-done.15.refs_12_), channel_id=1, source_target_pairs={{0,16},{16,0},{1,17},{17,1},{2,18},{18,2},{3,19},{19,3},{4,20},{20... | collective-permute-start | bytes 1032200 | tf_op jit(solution)/shard_map/ppermute | solution.py:665
  79.2 6.4 %collective-permute-done.20.refs_14_.refs_16_.refs_9_ = bf16[192,1536]{1,0:T(8,128)(2,1)S(1)} collective-permute-done((bf16[192,1536]{1,0:T(8,128)(2,1)S(1)}, bf16[192,1536]{1,0:T(8,128)(2,1)S(1)}, u32[]{:S(2)}, u32[]{:S(2)}) %collective-permute-start.20) | collective-permute-done | bytes 589856 | tf_op jit(solution)/shard_map/ppermute | solution.py:658
  86.1 1.8 %collective-permute-done.22.refs_11_ = bf16[192,896]{1,0:T(8,128)(2,1)S(1)} collective-permute-done((bf16[192,896]{1,0:T(8,128)(2,1)S(1)}, bf16[192,896]{1,0:T(8,128)(2,1)S(1)}, u32[]{:S(2)}, u32[]{:S(2)}) %collective-permute-start.22) | collective-permute-done | bytes 344096 | tf_op jit(solution)/shard_map/ppermute | solution.py:665
  88.1 5.5 %shard_map.150 = (f32[256,3072]{1,0:T(8,128)S(1)}, bf16[256,3072]{1,0:T(8,128)(2,1)}, bf16[256,3072]{1,0:T(8,128)(2,1)}, f32[256,384]{1,0:T(8,128)S(1)}) custom-call(s32[14]{0:T(128)S(1)} %dynamic-slice_bitcast_fusion.place.refs_0_, bf16[256,3072]{1,0:T(8,128)(2,1)S(1)} %copy-done, ...), custom_call_target="tpu_custom_call", output_to_operand_aliasing={{0}: (7, {}), {2}: (8, {})} | custom-call | bytes 12 | tf_op jit(solution)/shard_map/pallas_call | solution.py:91
  93.6 2.8 %shard_map.151 = (bf16[256,3072]{1,0:T(8,128)(2,1)}, bf16[256,3072]{1,0:T(8,128)(2,1)}, f32[64,192]{1,0:T(8,128)}, f32[64,192]{1,0:T(8,128)}) custom-call(s32[14]{0:T(128)S(1)} %dynamic-slice_bitcast_fusion.place.refs_0_, bf16[256,3072]{1,0:T(8,128)(2,1)S(1)} %copy-done, ...), custom_call_target="tpu_custom_call", output_to_operand_aliasing={{0}: (5, {}), {1}: (6, {})} | custom-call | bytes 12 | tf_op jit(solution)/shard_map/pallas_call | solution.py:91
  (47 shorter events, 9.6 us)
Async XLA Ops:
  0.6 3.2 %collective-permute-start = (bf16[192,3072]{1,0:T(8,128)(2,1)}, bf16[192,3072]{1,0:T(8,128)(2,1)S(1)}, u32[]{:S(2)}, u32[]{:S(2)}) collective-permute-start(bf16[192,3072]{1,0:T(8,128)(2,1)} %frozen.1), channel_id=1, source_target_pairs={{0,1},{1,0},{2,3},{3,2},{4,5},{5,4},{6,7},{7,6},{8,9},{9,8},{10,11... | collective-permute-start | bytes 3538952 | tf_op jit(solution)/shard_map/ppermute | solution.py:610
  1.8 1.3 %copy-start.3 = (bf16[192,3072]{1,0:T(8,128)(2,1)S(1)}, bf16[192,3072]{1,0:T(8,128)(2,1)}, u32[]{:S(2)}) copy-start(bf16[192,3072]{1,0:T(8,128)(2,1)} %frozen.1) | copy-start | bytes 3538948
  3.1 7.3 %copy-start = (bf16[256,3072]{1,0:T(8,128)(2,1)S(1)}, bf16[256,3072]{1,0:T(8,128)(2,1)}, u32[]{:S(2)}) copy-start(bf16[256,3072]{1,0:T(8,128)(2,1)} %refs_1_.11) | copy-start | bytes 4718596
  3.1 7.3 %copy-start.2 = (bf16[256,3072]{1,0:T(8,128)(2,1)S(1)}, bf16[256,3072]{1,0:T(8,128)(2,1)}, u32[]{:S(2)}) copy-start(bf16[256,3072]{1,0:T(8,128)(2,1)} %cotangent.1) | copy-start | bytes 4718596
  3.1 7.3 %copy-start.7 = (f32[16,3072]{1,0:T(8,128)S(1)}, f32[16,3072]{1,0:T(8,128)}, u32[]{:S(2)}) copy-start(f32[16,3072]{1,0:T(8,128)} %g_gate.1) | copy-start | bytes 589828
  4.6 11.7 %collective-permute-start.1 = (bf16[384,768]{1,0:T(8,128)(2,1)S(1)}, bf16[384,768]{1,0:T(8,128)(2,1)S(1)}, u32[]{:S(2)}, u32[]{:S(2)}) collective-permute-start(bf16[384,768]{1,0:T(8,128)(2,1)S(1)} %get-tuple-element.68.refs_8_), channel_id=1, source_target_pairs={{0,2},{1,5},{2,6},{3,1},{6,10},{7,3},{10,14},{11,7},{14,12},{15,11... | collective-permute-start | bytes 1769480 | tf_op jit(solution)/shard_map/ppermute | solution.py:612
  7.5 15.3 %collective-permute-start.5 = (bf16[384,896]{1,0:T(8,128)(2,1)S(1)}, bf16[384,896]{1,0:T(8,128)(2,1)S(1)}, u32[]{:S(2)}, u32[]{:S(2)}) collective-permute-start(bf16[384,896]{1,0:T(8,128)(2,1)S(1)} %get-tuple-element.70.refs_6_), channel_id=1, source_target_pairs={{0,2},{1,5},{2,6},{3,1},{6,10},{7,3},{10,14},{11,7},{14,12},{15,11... | collective-permute-start | bytes 2064392 | tf_op jit(solution)/shard_map/ppermute | solution.py:612
  10.4 1.1 %copy-start.4 = (f32[3072,64]{0,1:T(8,128)S(1)}, f32[3072,64]{0,1:T(8,128)}, u32[]{:S(2)}) copy-start(f32[3072,64]{0,1:T(8,128)} %param.14) | copy-start | bytes 2359300
  11.5 1.1 %copy-start.5 = (f32[64,3072]{1,0:T(8,128)S(1)}, f32[64,3072]{1,0:T(8,128)}, u32[]{:S(2)}) copy-start(f32[64,3072]{1,0:T(8,128)} %up.1) | copy-start | bytes 2359300
  12.7 1.1 %copy-start.6 = (f32[50,3072]{1,0:T(8,128)S(1)}, f32[50,3072]{1,0:T(8,128)}, u32[]{:S(2)}) copy-start(f32[50,3072]{1,0:T(8,128)} %t_gate.1) | copy-start | bytes 1843204
  16.3 24.6 %collective-permute-start.4 = (bf16[256,3200]{1,0:T(8,128)(2,1)S(1)}, bf16[256,3200]{1,0:T(8,128)(2,1)S(1)}, u32[]{:S(2)}, u32[]{:S(2)}) collective-permute-start(bf16[256,3200]{1,0:T(8,128)(2,1)S(1)} %get-tuple-element.93.refs_2_), channel_id=1, source_target_pairs={{0,1},{1,0},{2,3},{3,2},{4,5},{5,4},{6,7},{7,6},{8,9},{9,8},{10,11... | collective-permute-start | bytes 4915208 | tf_op jit(solution)/shard_map/ppermute | solution.py:623
  16.4 8.4 %collective-permute-start.6 = (bf16[8,384,128]{2,1,0:T(8,128)(2,1)S(1)}, bf16[8,384,128]{2,1,0:T(8,128)(2,1)S(1)}, u32[]{:S(2)}, u32[]{:S(2)}) collective-permute-start(bf16[8,384,128]{2,1,0:T(8,128)(2,1)S(1)} %get-tuple-element.78), channel_id=1, source_target_pairs={{0,1},{1,0},{2,3},{3,2},{4,5},{5,4},{6,7},{7,6},{8,9},{9,8},{10,11... | collective-permute-start | bytes 2359304 | tf_op jit(solution)/shard_map/ppermute | solution.py:619
  16.9 26.3 %collective-permute-start.3 = (bf16[256,3072]{1,0:T(8,128)(2,1)S(1)}, bf16[256,3072]{1,0:T(8,128)(2,1)S(1)}, u32[]{:S(2)}, u32[]{:S(2)}) collective-permute-start(bf16[256,3072]{1,0:T(8,128)(2,1)S(1)} %copy-done), channel_id=1, source_target_pairs={{0,1},{1,0},{2,3},{3,2},{4,5},{5,4},{6,7},{7,6},{8,9},{9,8},{10,11... | collective-permute-start | bytes 4718600 | tf_op jit(solution)/shard_map/ppermute | solution.py:614
  22.8 10.9 %collective-permute-start.10 = (bf16[384,896]{1,0:T(8,128)(2,1)S(1)}, bf16[384,896]{1,0:T(8,128)(2,1)S(1)}, u32[]{:S(2)}, u32[]{:S(2)}) collective-permute-start(bf16[384,896]{1,0:T(8,128)(2,1)S(1)} %collective-permute-done.5.refs_6_), channel_id=1, source_target_pairs={{0,2},{1,5},{2,6},{3,1},{6,10},{7,3},{10,14},{11,7},{14,12},{15,11... | collective-permute-start | bytes 2064392 | tf_op jit(solution)/shard_map/ppermute | solution.py:645
  25.3 13.6 %collective-permute-start.7 = (bf16[384,640]{1,0:T(8,128)(2,1)S(1)}, bf16[384,640]{1,0:T(8,128)(2,1)S(1)}, u32[]{:S(2)}, u32[]{:S(2)}) collective-permute-start(bf16[384,640]{1,0:T(8,128)(2,1)S(1)} %shard_map.142), channel_id=1, source_target_pairs={{0,2},{1,5},{2,6},{3,1},{6,10},{7,3},{10,14},{11,7},{14,12},{15,11... | collective-permute-start | bytes 1474568 | tf_op jit(solution)/shard_map/ppermute | solution.py:621
  27.0 25.7 %collective-permute-start.8 = (bf16[384,896]{1,0:T(8,128)(2,1)S(1)}, bf16[384,896]{1,0:T(8,128)(2,1)S(1)}, u32[]{:S(2)}, u32[]{:S(2)}) collective-permute-start(bf16[384,896]{1,0:T(8,128)(2,1)S(1)} %collective-permute-done.5.refs_6_), channel_id=1, source_target_pairs={{0,16},{16,0},{1,17},{17,1},{2,18},{18,2},{3,19},{19,3},{4,20},{20... | collective-permute-start | bytes 2064392 | tf_op jit(solution)/shard_map/ppermute | solution.py:646
  33.7 19.0 %collective-permute-start.11 = (bf16[384,896]{1,0:T(8,128)(2,1)S(1)}, bf16[384,896]{1,0:T(8,128)(2,1)S(1)}, u32[]{:S(2)}, u32[]{:S(2)}) collective-permute-start(bf16[384,896]{1,0:T(8,128)(2,1)S(1)} %collective-permute-done.10.refs_6_), channel_id=1, source_target_pairs={{0,2},{1,5},{2,6},{3,1},{6,10},{7,3},{10,14},{11,7},{14,12},{15,11... | collective-permute-start | bytes 2064392 | tf_op jit(solution)/shard_map/ppermute | solution.py:645
  39.0 13.7 %collective-permute-start.2 = (bf16[384,768]{1,0:T(8,128)(2,1)S(1)}, bf16[384,768]{1,0:T(8,128)(2,1)S(1)}, u32[]{:S(2)}, u32[]{:S(2)}) collective-permute-start(bf16[384,768]{1,0:T(8,128)(2,1)S(1)} %collective-permute-done.1.refs_8_), channel_id=1, source_target_pairs={{0,2},{1,5},{2,6},{3,1},{6,10},{7,3},{10,14},{11,7},{14,12},{15,11... | collective-permute-start | bytes 1769480 | tf_op jit(solution)/shard_map/ppermute | solution.py:660
  41.6 16.4 %collective-permute-start.13 = (bf16[384,640]{1,0:T(8,128)(2,1)S(1)}, bf16[384,640]{1,0:T(8,128)(2,1)S(1)}, u32[]{:S(2)}, u32[]{:S(2)}) collective-permute-start(bf16[384,640]{1,0:T(8,128)(2,1)S(1)} %shard_map.144), channel_id=1, source_target_pairs={{0,2},{1,5},{2,6},{3,1},{6,10},{7,3},{10,14},{11,7},{14,12},{15,11... | collective-permute-start | bytes 1474568 | tf_op jit(solution)/shard_map/ppermute | solution.py:652
  43.2 19.8 %collective-permute-start.12 = (bf16[384,896]{1,0:T(8,128)(2,1)S(1)}, bf16[384,896]{1,0:T(8,128)(2,1)S(1)}, u32[]{:S(2)}, u32[]{:S(2)}) collective-permute-start(bf16[384,896]{1,0:T(8,128)(2,1)S(1)} %collective-permute-done.10.refs_6_), channel_id=1, source_target_pairs={{0,16},{16,0},{1,17},{17,1},{2,18},{18,2},{3,19},{19,3},{4,20},{20... | collective-permute-start | bytes 2064392 | tf_op jit(solution)/shard_map/ppermute | solution.py:646
  52.7 22.3 %collective-permute-start.16 = (bf16[384,896]{1,0:T(8,128)(2,1)S(1)}, bf16[384,896]{1,0:T(8,128)(2,1)S(1)}, u32[]{:S(2)}, u32[]{:S(2)}) collective-permute-start(bf16[384,896]{1,0:T(8,128)(2,1)S(1)} %collective-permute-done.11.refs_6_.whole), channel_id=1, source_target_pairs={{0,16},{16,0},{1,17},{17,1},{2,18},{18,2},{3,19},{19,3},{4,20},{20... | collective-permute-start | bytes 2064392 | tf_op jit(solution)/shard_map/ppermute | solution.py:646
  54.6 13.3 %collective-permute-start.9 = (bf16[384,768]{1,0:T(8,128)(2,1)S(1)}, bf16[384,768]{1,0:T(8,128)(2,1)S(1)}, u32[]{:S(2)}, u32[]{:S(2)}) collective-permute-start(bf16[384,768]{1,0:T(8,128)(2,1)S(1)} %collective-permute-done.2.refs_8_), channel_id=1, source_target_pairs={{0,2},{1,5},{2,6},{3,1},{6,10},{7,3},{10,14},{11,7},{14,12},{15,11... | collective-permute-start | bytes 1769480 | tf_op jit(solution)/shard_map/ppermute | solution.py:660
  58.6 11.2 %collective-permute-start.14 = (bf16[384,640]{1,0:T(8,128)(2,1)S(1)}, bf16[384,640]{1,0:T(8,128)(2,1)S(1)}, u32[]{:S(2)}, u32[]{:S(2)}) collective-permute-start(bf16[384,640]{1,0:T(8,128)(2,1)S(1)} %shard_map.146), channel_id=1, source_target_pairs={{0,2},{1,5},{2,6},{3,1},{6,10},{7,3},{10,14},{11,7},{14,12},{15,11... | collective-permute-start | bytes 1474568 | tf_op jit(solution)/shard_map/ppermute | solution.py:652
  61.2 13.8 %collective-permute-start.15 = (bf16[192,896]{1,0:T(8,128)(2,1)S(1)}, bf16[192,896]{1,0:T(8,128)(2,1)S(1)}, u32[]{:S(2)}, u32[]{:S(2)}) collective-permute-start(bf16[192,896]{1,0:T(8,128)(2,1)S(1)} %shard_map.148), channel_id=1, source_target_pairs={{0,2},{1,5},{2,6},{3,1},{6,10},{7,3},{10,14},{11,7},{14,12},{15,11... | collective-permute-start | bytes 1032200 | tf_op jit(solution)/shard_map/ppermute | solution.py:645
  75.0 13.2 %copy-start.1 = (bf16[256,3072]{1,0:T(8,128)(2,1)S(1)}, bf16[256,3072]{1,0:T(8,128)(2,1)}, u32[]{:S(2)}) copy-start(bf16[256,3072]{1,0:T(8,128)(2,1)} %refs_5_.1) | copy-start | bytes 4718596
  75.0 10.6 %collective-permute-start.17 = (bf16[256,4224]{1,0:T(8,128)(2,1)S(1)}, bf16[256,4224]{1,0:T(8,128)(2,1)S(1)}, u32[]{:S(2)}, u32[]{:S(2)}) collective-permute-start(bf16[256,4224]{1,0:T(8,128)(2,1)S(1)} %get-tuple-element.104), channel_id=1, source_target_pairs={{0,1},{1,0},{2,3},{3,2},{4,5},{5,4},{6,7},{7,6},{8,9},{9,8},{10,11... | collective-permute-start | bytes 6488072 | tf_op jit(solution)/shard_map/ppermute | solution.py:674
  75.7 9.9 %collective-permute-start.20 = (bf16[192,1536]{1,0:T(8,128)(2,1)S(1)}, bf16[192,1536]{1,0:T(8,128)(2,1)S(1)}, u32[]{:S(2)}, u32[]{:S(2)}) collective-permute-start(bf16[192,1536]{1,0:T(8,128)(2,1)S(1)} %shard_map.149), channel_id=1, source_target_pairs={{0,2},{1,5},{2,6},{3,1},{6,10},{7,3},{10,14},{11,7},{14,12},{15,11... | collective-permute-start | bytes 1769480 | tf_op jit(solution)/shard_map/ppermute | solution.py:658
  77.4 10.7 %collective-permute-start.18 = (bf16[384,896]{1,0:T(8,128)(2,1)S(1)}, bf16[384,896]{1,0:T(8,128)(2,1)S(1)}, u32[]{:S(2)}, u32[]{:S(2)}) collective-permute-start(bf16[384,896]{1,0:T(8,128)(2,1)S(1)} %collective-permute-done.16.refs_9_), channel_id=1, source_target_pairs={{0,1},{1,0},{2,3},{3,2},{4,5},{5,4},{6,7},{7,6},{8,9},{9,8},{10,11... | collective-permute-start | bytes 2064392 | tf_op jit(solution)/shard_map/ppermute | solution.py:669
  77.7 10.2 %collective-permute-start.22 = (bf16[192,896]{1,0:T(8,128)(2,1)S(1)}, bf16[192,896]{1,0:T(8,128)(2,1)S(1)}, u32[]{:S(2)}, u32[]{:S(2)}) collective-permute-start(bf16[192,896]{1,0:T(8,128)(2,1)S(1)} %collective-permute-done.15.refs_12_), channel_id=1, source_target_pairs={{0,16},{16,0},{1,17},{17,1},{2,18},{18,2},{3,19},{19,3},{4,20},{20... | collective-permute-start | bytes 1032200 | tf_op jit(solution)/shard_map/ppermute | solution.py:665
  85.6 2.5 %collective-permute-start.21 = (bf16[192,1536]{1,0:T(8,128)(2,1)S(1)}, bf16[192,1536]{1,0:T(8,128)(2,1)S(1)}, u32[]{:S(2)}, u32[]{:S(2)}) collective-permute-start(bf16[192,1536]{1,0:T(8,128)(2,1)S(1)} %collective-permute-done.20.refs_14_.refs_16_.refs_9_), channel_id=1, source_target_pairs={{0,1},{1,0},{2,3},{3,2},{4,5},{5,4},{6,7},{7,6},{8,9},{9,8},{10,11... | collective-permute-start | bytes 1769480 | tf_op jit(solution)/shard_map/ppermute | solution.py:675
  85.6 2.5 %collective-permute-start.19 = (bf16[192,896]{1,0:T(8,128)(2,1)S(1)}, bf16[192,896]{1,0:T(8,128)(2,1)S(1)}, u32[]{:S(2)}, u32[]{:S(2)}) collective-permute-start(bf16[192,896]{1,0:T(8,128)(2,1)S(1)} %collective-permute-done.15.refs_12_), channel_id=1, source_target_pairs={{0,1},{1,0},{2,3},{3,2},{4,5},{5,4},{6,7},{7,6},{8,9},{9,8},{10,11... | collective-permute-start | bytes 1032200 | tf_op jit(solution)/shard_map/ppermute | solution.py:669
  87.9 5.7 %collective-permute-start.23 = (bf16[192,896]{1,0:T(8,128)(2,1)S(1)}, bf16[192,896]{1,0:T(8,128)(2,1)S(1)}, u32[]{:S(2)}, u32[]{:S(2)}) collective-permute-start(bf16[192,896]{1,0:T(8,128)(2,1)S(1)} %collective-permute-done.22.refs_11_), channel_id=1, source_target_pairs={{0,1},{1,0},{2,3},{3,2},{4,5},{5,4},{6,7},{7,6},{8,9},{9,8},{10,11... | collective-permute-start | bytes 1032200 | tf_op jit(solution)/shard_map/ppermute | solution.py:687
